TPU v7x, 128 devices: a whole 4x4x4 slice. The times are simulated.
128 devices in a mesh: ctx: 8 (over y, core), seq: 16 (over x, z).
Axes of the slice: x: 4, y: 4, z: 4, core: 2. Of those that a mesh axis runs over, the one named last changes fastest.
Arguments:
- tokens: bfloat16 [131072, 1024], P(('ctx', 'seq')), parts along dimension 0, may hold values from -16 to 16
- ln_gain: float32 [1024], replicated, may hold values from 0.5 to 1.5
- post_gain: float32 [1024], replicated, may hold values from 0.25 to 1.75
- w_query: bfloat16 [1024, 1024], replicated, may hold values from -32 to 32
- w_key: bfloat16 [1024, 1024], replicated, may hold values from -1 to 1
- w_value: bfloat16 [1024, 1024], replicated, may hold values from -0.1875 to 0.1875
- w_out: bfloat16 [1024, 1024], replicated, may hold values from -0.1875 to 0.1875
Outputs:
- latent_out: bfloat16 [8192, 1024], P(('ctx', 'seq')), parts along dimension 0
There are 8 independent parts, one for each index of `ctx`. A program takes and returns all parts, laid end to end along the dimension named above; an argument that names none is the same for every part. Nothing has to cross between parts.
All inputs are finite; a program needn't handle non-finite values.
Results may differ from a plain program's by a relative error of at most 0.018.
Values may be sent and summed in bfloat16 or wider, within the bound.
No kernel may reach another device: no remote copies, remote signals or barrier semaphores. Data moves between devices by JAX's collectives and lax.ppermute only.
A program may use at most 320 MiB of HBM per device.

v0:
```python
import jax
import jax.numpy as jnp
from jax import lax
from jax.sharding import PartitionSpec as P

D = 1024
HEADS = 16
HEAD_DIM = 64
LATENTS = 1024


def spread(block, axis, source):
    block = jnp.where(lax.axis_index(axis) == source, block, jnp.zeros_like(block))
    return lax.psum(block, axis)


def rms_rows(rows, gain):
    wide = rows.astype(jnp.float32)
    scale = lax.rsqrt(jnp.mean(wide * wide, axis=-1, keepdims=True) + 1e-06)
    return (wide * scale * gain).astype(jnp.bfloat16)


def local(tokens, ln_gain, post_gain, w_query, w_key, w_value, w_out):
    count = lax.axis_size("seq")
    me = lax.axis_index("seq")
    tok_rows = tokens.shape[0]
    owned = LATENTS // count
    normed = rms_rows(tokens, ln_gain)
    queries = jnp.dot(normed, w_query, preferred_element_type=jnp.float32).astype(jnp.bfloat16)
    queries, latent_rows = (spread(queries, "seq", count - 1), spread(tokens, "seq", count - 1))
    keys = jnp.dot(normed, w_key, preferred_element_type=jnp.float32).astype(jnp.bfloat16)
    values = jnp.dot(normed, w_value, preferred_element_type=jnp.float32).astype(jnp.bfloat16)
    key_pos = me * tok_rows + jnp.arange(tok_rows, dtype=jnp.int32)
    query_pos = tok_rows * count - LATENTS + jnp.arange(LATENTS, dtype=jnp.int32)
    allowed = key_pos[None, :] <= query_pos[:, None]
    factor = HEAD_DIM ** (-0.5)

    def one_head(head, carry):
        maxima, sums, mixes = carry
        start = head * HEAD_DIM
        query_h = lax.dynamic_slice_in_dim(queries, start, HEAD_DIM, 1)
        key_h = lax.dynamic_slice_in_dim(keys, start, HEAD_DIM, 1)
        value_h = lax.dynamic_slice_in_dim(values, start, HEAD_DIM, 1)
        scores = (
            lax.dot_general(
                query_h, key_h, (((1,), (1,)), ((), ())), preferred_element_type=jnp.float32
            )
            * factor
        )
        scores = jnp.where(allowed, scores, jnp.float32(-1e30))
        local_max = jnp.max(scores, axis=-1)
        probs = jnp.exp(scores - local_max[:, None])
        local_sum = jnp.sum(probs, axis=-1)
        local_mix = jnp.dot(probs.astype(jnp.bfloat16), value_h, preferred_element_type=jnp.float32)
        maxima = lax.dynamic_update_slice_in_dim(maxima, local_max[:, None], head, 1)
        sums = lax.dynamic_update_slice_in_dim(sums, local_sum[:, None], head, 1)
        mixes = lax.dynamic_update_slice_in_dim(mixes, local_mix, start, 1)
        return (maxima, sums, mixes)

    start_state = (
        jnp.zeros((LATENTS, HEADS), jnp.float32),
        jnp.zeros((LATENTS, HEADS), jnp.float32),
        jnp.zeros((LATENTS, D), jnp.float32),
    )
    maxima, sums, mixes = lax.fori_loop(0, HEADS, one_head, start_state)
    top = lax.pmax(maxima.astype(jnp.bfloat16), "seq").astype(maxima.dtype)
    rescale = jnp.exp(maxima - top)
    own_sums, own_mix = (
        lax.psum_scatter(
            (sums * rescale).astype(jnp.bfloat16), "seq", scatter_dimension=0, tiled=True
        ).astype(jnp.float32),
        lax.psum_scatter(
            (mixes * jnp.repeat(rescale, HEAD_DIM, axis=-1)).astype(jnp.bfloat16),
            "seq",
            scatter_dimension=0,
            tiled=True,
        ).astype(jnp.float32),
    )
    attended = (own_mix / jnp.repeat(own_sums, HEAD_DIM, axis=-1)).astype(jnp.bfloat16)
    post = rms_rows(attended, post_gain)
    residual_rows = lax.dynamic_slice_in_dim(latent_rows, me * owned, owned, 0)
    mixed = residual_rows.astype(jnp.float32) + jnp.dot(
        post, w_out, preferred_element_type=jnp.float32
    )
    return mixed.astype(jnp.bfloat16)


def solution(mesh):
    return jax.shard_map(
        local,
        mesh=mesh,
        in_specs=(P(("ctx", "seq"), None), P(), P(), P(), P(), P(), P()),
        out_specs=P(("ctx", "seq"), None),
        check_vma=False,
    )
```

profile of v0, /device:TPU:0, one launch (start us, length us, event | category | flops | bytes accessed | tf_op | source)
XLA Modules:
  0.0 450.7 jit_solution(17636475302125967398)
XLA Ops:
  6.5 2.2 fusion.18
  8.8 1.4 broadcast_select_fusion
  10.2 0.9 copy-done.1
  11.1 3.8 convert_select_fusion
  15.0 6.1 %convolution_convert_fusion = bf16[1024,1024]{1,0:T(8,128)(2,1)} fusion(bf16[1024,1024]{1,0:T(8,128)(2,1)} %param.14, bf16[1024,1024]{1,0:T(8,128)(2,1)} %param.9, f32[1024]{0:T(1024)S(1)} %copy-done.5, f32[1024]{0:T(1024)S(1)} %add_rsqrt_fusion), kind=kOutput, calls=%fused_computation.25 | convolution fusion | flops 2152726528 | bytes 6299648 | tf_op jit(solution)/shard_map/dot_general | solution.py:32
  21.1 3.8 convolution_convert_fusion.1
  24.9 97.0 %all-reduce.3.cloned.1.call-done = (bf16[1024,1024]{1,0:T(8,128)(2,1)}, bf16[1024,1024]{1,0:T(8,128)(2,1)}) async-done(((bf16[1024,1024]{1,0:T(8,128)(2,1)}, bf16[1024,1024]{1,0:T(8,128)(2,1)}), (bf16[1024,1024]{1,0:T(8,128)(2,1)}, bf16[1024,1024]{1,0:T(8,128)(2,1)})) %all-reduce.3.cloned.1.call-update) | async-done | bytes 4194320 | tf_op jit(solution)/shard_map/psum | solution.py:14
  121.9 2.5 broadcast_in_dim.38
  124.4 96.5 %while.18 = (s32[]{:T(128)}, f32[1024,16]{0,1:T(8,128)S(1)}, f32[1024,16]{0,1:T(8,128)S(1)}, f32[1024,1024]{0,1:T(8,128)}, bf16[1024,1024]{1,0:T(8,128)(2,1)}, /...) while((s32[]{:T(128)}, f32[1024,16]{0,1:T(8,128)S(1)}, ...), condition=%wide.region_6.7_spmd.clone, body=%wide.region_3.6_spmd.clone.sunk | while | flops 283113472 | bytes 13691059 | solution.py:65
  124.4 1.8 fusion.45
  126.2 2.9 fusion.47
  129.1 1.0 fusion.46
  130.4 1.8 fusion.45
  132.2 2.9 fusion.47
  135.1 1.0 fusion.46
  136.4 1.8 fusion.45
  138.2 2.9 fusion.47
  141.1 1.0 fusion.46
  142.4 1.8 fusion.45
  144.3 2.9 fusion.47
  147.1 1.0 fusion.46
  148.4 1.8 fusion.45
  150.3 2.9 fusion.47
  153.2 1.0 fusion.46
  154.5 1.8 fusion.45
  156.3 2.9 fusion.47
  159.2 1.0 fusion.46
  160.5 1.8 fusion.45
  162.4 2.9 fusion.47
  165.3 1.0 fusion.46
  166.5 1.8 fusion.45
  168.4 2.9 fusion.47
  171.3 1.0 fusion.46
  172.6 1.8 fusion.45
  174.4 2.9 fusion.47
  177.3 1.0 fusion.46
  178.6 1.8 fusion.45
  180.5 2.9 fusion.47
  183.4 1.0 fusion.46
  184.7 1.8 fusion.45
  186.5 2.9 fusion.47
  189.4 1.0 fusion.46
  190.7 1.8 fusion.45
  192.5 2.9 fusion.47
  195.4 1.0 fusion.46
  196.7 1.8 fusion.45
  198.6 2.9 fusion.47
  201.5 1.0 fusion.46
  202.8 1.8 fusion.45
  204.6 2.9 fusion.47
  207.5 1.0 fusion.46
  208.8 1.8 fusion.45
  210.6 2.9 fusion.47
  213.5 1.0 fusion.46
  214.8 1.8 fusion.45
  216.7 2.9 fusion.47
  219.5 1.0 fusion.46
  220.8 72.3 %pmax.7 = bf16[1024,16]{0,1:T(8,128)(2,1)S(1)} all-reduce(bf16[1024,16]{0,1:T(8,128)(2,1)S(1)} %convert_element_type.61), channel_id=1, replica_groups=mesh['ctx'=8,'seq'=16] {'seq'}, use_global_device_ids=true, to_apply=%region_7.8 | all-reduce | flops 16384 | bytes 65536 | tf_op jit(solution)/shard_map/pmax | solution.py:66
  294.1 4.1 fusion.21
  298.3 4.0 copy.8
  302.3 60.3 %reduce-scatter.9.cloned.1.call-done = bf16[64,16]{1,0:T(8,128)(2,1)} async-done(((bf16[1024,16]{1,0:T(8,128)(2,1)}), bf16[64,16]{1,0:T(8,128)(2,1)}) %reduce-scatter.9.cloned.1.call-update) | async-done | bytes 2064
  363.4 76.6 %reduce-scatter.7.cloned.1.call-done = bf16[64,1024]{1,0:T(8,128)(2,1)} async-done(((bf16[1024,1024]{1,0:T(8,128)(2,1)}), bf16[64,1024]{1,0:T(8,128)(2,1)}) %reduce-scatter.7.cloned.1.call-update) | async-done | bytes 131088
  440.0 1.1 copy.9
  441.2 3.0 fusion.22
  (60 shorter events, 5.5 us)
Async XLA Ops:
  6.5 3.7 copy-start
  6.5 3.7 copy-start.5
  6.5 115.4 %all-reduce.3.cloned.1.call-start = ((), (), s32[]{:S(2)}) async-start(), calls=%async_computation.4 | async-start | bytes 8388608 | tf_op jit(solution)/shard_map/psum | solution.py:14
  8.8 2.4 copy-start.1
  14.9 347.7 %reduce-scatter.9.cloned.1.call-start = ((), (), s32[]{:S(2)}) async-start(), calls=%async_computation.3 | async-start | bytes 278528
  15.0 6.1 %copy-start.2 = (bf16[1024,1024]{1,0:T(8,128)(2,1)S(1)}, bf16[1024,1024]{1,0:T(8,128)(2,1)}, u32[]{:S(2)}) copy-start(bf16[1024,1024]{1,0:T(8,128)(2,1)} %param.9) | copy-start | bytes 6291460
  15.0 6.1 %copy-start.4 = (bf16[1024,1024]{1,0:T(8,128)(2,1)S(1)}, bf16[1024,1024]{1,0:T(8,128)(2,1)}, u32[]{:S(2)}) copy-start(bf16[1024,1024]{1,0:T(8,128)(2,1)} %param.13) | copy-start | bytes 6291460
  294.1 145.9 %reduce-scatter.7.cloned.1.call-start = ((), (), s32[]{:S(2)}) async-start(), calls=%async_computation.2 | async-start | bytes 2228224
  298.3 143.0 %copy-start.3 = (f32[1024]{0:T(1024)S(1)}, f32[1024]{0:T(1024)}, u32[]{:S(2)}) copy-start(f32[1024]{0:T(1024)} %param.11) | copy-start | bytes 12292
Sparse Core Ops, SparseCore 0:
  15.0 106.8 all-reduce.2
  294.2 68.3 reduce-scatter.8
  366.2 73.7 reduce-scatter.6
where the time goes:
time: 452 us; the launch traced here: 451 us
  waiting for transfers between devices  234 us (52%)
  matrix products  92.1 us (20%)
  blocking collectives  72.3 us (16%)
  other arithmetic  24.5 us (5%)
  local copies, waits for them, and re-layouts  13.6 us (3%)
  between operations  13.2 us (3%)
    unnamed x5, waiting for transfers between devices  137 us
    psum x1, waiting for transfers between devices, spread(): return lax.psum(block, axis)  97 us
    pmax x1, blocking collectives, local(): top = lax.pmax(maxima.astype(jnp.bfloat16), 'seq').astype(maxima.dtype)  72.3 us
    dot_general x16, matrix products, one_head(): jnp.dot(probs.astype(jnp.bfloat16), value_h, preferred_element_type=jnp.f...  46.1 us
    dot_general x16, matrix products, one_head(): lax.dot_general(query_h, key_h, (((1,), (1,)), ((), ())), preferred_eleme...  29.5 us
    reduce_sum x16, other arithmetic, one_head(): local_sum = jnp.sum(probs, axis=-1)  16.5 us
  transfers between devices with their start and end apart: 3, of which 3 were waited for; matrix products, arithmetic and copies ran while one was open for 4% of the time, Pallas kernels for 0%

commit v1 on v0

v1 whole, which is shorter than its diff:
```python
import functools

import jax
import jax.numpy as jnp
from jax import lax
from jax.experimental import pallas as pl
from jax.experimental.pallas import tpu as pltpu
from jax.sharding import PartitionSpec as P

D = 1024
HEADS = 16
HEAD_DIM = 64
LATENTS = 1024
CHUNKS = 2
LOG2E = 1.4426950408889634
EXP2_SCALE = LOG2E * HEAD_DIM ** (-0.5)
MASKED = -1e30
WIDE = D + 128


def rms_rows(rows, gain):
    wide = rows.astype(jnp.float32)
    scale = lax.rsqrt(jnp.mean(wide * wide, axis=-1, keepdims=True) + 1e-06)
    return (wide * scale * gain).astype(jnp.bfloat16)


def kv_kernel(tokens, gain, w_key, w_value, keys, values, normed):
    @pl.when(pl.program_id(0) == 0)
    def _():
        normed[...] = rms_rows(tokens[...], gain[...])

    rows = normed[...]
    keys[...] = jnp.dot(rows, w_key[...], preferred_element_type=jnp.float32).astype(jnp.bfloat16)
    values[...] = jnp.dot(rows, w_value[...], preferred_element_type=jnp.float32).astype(jnp.bfloat16)


def project_kv(tokens, gain, w_key, w_value):
    rows = tokens.shape[0]
    cols = 256
    whole = lambda c: (0, 0)
    block = lambda c: (0, c)
    return pl.pallas_call(
        kv_kernel,
        grid=(D // cols,),
        out_shape=(jax.ShapeDtypeStruct((rows, D), jnp.bfloat16),) * 2,
        in_specs=[
            pl.BlockSpec((rows, D), whole),
            pl.BlockSpec((1, D), whole),
            pl.BlockSpec((D, cols), block),
            pl.BlockSpec((D, cols), block),
        ],
        out_specs=(pl.BlockSpec((rows, cols), block),) * 2,
        scratch_shapes=[pltpu.VMEM((rows, D), jnp.bfloat16)],
        compiler_params=pltpu.CompilerParams(vmem_limit_bytes=56 * 2**20),
        cost_estimate=pl.CostEstimate(flops=4 * rows * D * D, bytes_accessed=10 * rows * D, transcendentals=0),
        name="project_kv",
    )(tokens, gain, w_key, w_value)


def attend_kernel(chunk, owned, flag, queries, keys, values, out):
    rows = queries.shape[0]
    count = keys.shape[0]
    step = pl.program_id(0)
    pairs = HEADS // 2
    part = owned // CHUNKS
    low = lax.broadcasted_iota(jnp.int32, (1, 128), 1) < HEAD_DIM

    def attention(causal):
        lane = lax.broadcasted_iota(jnp.int32, (rows, 128), 1)
        lse = jnp.zeros((rows, 128), jnp.float32)
        ones = jnp.ones((count, 128), jnp.bfloat16)
        if causal:
            key_pos = lax.broadcasted_iota(jnp.int32, (rows, count), 1)
            row = step * rows + lax.broadcasted_iota(jnp.int32, (rows, count), 0)
            query_pos = (row // part) * owned + chunk * part + row % part
            allowed = key_pos <= query_pos
            allowed = jnp.concatenate([allowed, allowed], axis=0)

        def scores_of(pair):
            at = slice(pair * 128, (pair + 1) * 128)
            query = queries[:, at]
            none = jnp.zeros_like(query)
            both = jnp.concatenate([jnp.where(low, query, none), jnp.where(low, none, query)], axis=0)
            scores = lax.dot_general(
                both, keys[:, at], (((1,), (1,)), ((), ())), preferred_element_type=jnp.float32
            )
            return jnp.where(allowed, scores, MASKED) if causal else scores

        ahead = scores_of(0)
        for pair in range(pairs):
            at = slice(pair * 128, (pair + 1) * 128)
            scores = ahead
            if pair + 1 < pairs:
                ahead = scores_of(pair + 1)
            top = jnp.max(scores, axis=-1, keepdims=True)
            weights = jnp.exp2((scores - top) * EXP2_SCALE).astype(jnp.bfloat16)
            mixed = jnp.dot(
                weights,
                jnp.concatenate([values[:, at], ones], axis=1),
                preferred_element_type=jnp.float32,
            )
            mix, total = mixed[:, 0:128], mixed[:, 128:256]
            both = jnp.where(low, mix[:rows], mix[rows:]) / jnp.where(low, total[:rows], total[rows:])
            out[:, at] = both.astype(jnp.bfloat16)
            level = top * EXP2_SCALE + jnp.log2(total)
            lse = jnp.where(lane == 2 * pair, level[:rows], lse)
            lse = jnp.where(lane == 2 * pair + 1, level[rows:], lse)
        first = lse.astype(jnp.bfloat16).astype(jnp.float32)
        second = (lse - first).astype(jnp.bfloat16).astype(jnp.float32)
        third = lse - first - second
        pieces = first + pltpu.roll(second, HEADS, 1) + pltpu.roll(third, 2 * HEADS, 1)
        out[:, D:WIDE] = pieces.astype(jnp.bfloat16)

    @pl.when(flag[0] == 0)
    def _():
        attention(False)

    @pl.when(flag[0] != 0)
    def _():
        attention(True)


def attend(chunk, owned, is_last, queries, keys, values):
    count = queries.shape[0]
    rows = 256
    whole = lambda c: (0, 0)
    block = lambda c: (c, 0)
    return pl.pallas_call(
        functools.partial(attend_kernel, chunk, owned),
        grid=(count // rows,),
        out_shape=jax.ShapeDtypeStruct((count, WIDE), jnp.bfloat16),
        in_specs=[
            pl.BlockSpec(memory_space=pltpu.SMEM),
            pl.BlockSpec((rows, D), block),
            pl.BlockSpec(keys.shape, whole),
            pl.BlockSpec(values.shape, whole),
        ],
        out_specs=pl.BlockSpec((rows, WIDE), block),
        compiler_params=pltpu.CompilerParams(vmem_limit_bytes=56 * 2**20),
        cost_estimate=pl.CostEstimate(
            flops=16 * count * D * D, bytes_accessed=8 * D * D, transcendentals=HEADS * count * D
        ),
        name="attend_%d" % chunk,
    )(is_last, queries, keys, values)


def finish_kernel(*refs):
    parts = refs[:CHUNKS]
    residual, gain, w_out, out = refs[CHUNKS:]
    count, part, _ = parts[0].shape
    head = lax.broadcasted_iota(jnp.int32, (128, D), 0)
    column = lax.broadcasted_iota(jnp.int32, (128, D), 1)
    spread = (column // HEAD_DIM == head).astype(jnp.bfloat16)
    spread = jnp.concatenate([spread, spread], axis=0)
    lane = lax.broadcasted_iota(jnp.int32, (count * part, 128), 1)
    for chunk in range(CHUNKS):
        pieces = parts[chunk][:, :, D:WIDE].astype(jnp.float32).reshape(count * part, 128)
        level = pieces + pltpu.roll(pieces, 128 - HEADS, 1) + pltpu.roll(pieces, 128 - 2 * HEADS, 1)
        level = jnp.where(lane < HEADS, level, 0.0).reshape(count, part, 128)
        weight = jnp.exp2(level - jnp.max(level, axis=0, keepdims=True))
        weight = weight / jnp.sum(weight, axis=0, keepdims=True)
        weight = weight.reshape(count * part, 128)
        weight_high = weight.astype(jnp.bfloat16)
        weight_low = (weight - weight_high.astype(jnp.float32)).astype(jnp.bfloat16)
        wide = jnp.dot(
            jnp.concatenate([weight_high, weight_low], axis=1), spread, preferred_element_type=jnp.float32
        ).reshape(count, part, D)
        mix = jnp.sum(wide * parts[chunk][:, :, 0:D].astype(jnp.float32), axis=0)
        attended = mix.astype(jnp.bfloat16)
        post = rms_rows(attended, gain[...])
        at = slice(chunk * part, (chunk + 1) * part)
        mixed = residual[at, :].astype(jnp.float32) + jnp.dot(
            post, w_out[...], preferred_element_type=jnp.float32
        )
        out[at, :] = mixed.astype(jnp.bfloat16)


def finish(parts, residual, gain, w_out):
    return pl.pallas_call(
        finish_kernel,
        out_shape=jax.ShapeDtypeStruct(residual.shape, jnp.bfloat16),
        compiler_params=pltpu.CompilerParams(vmem_limit_bytes=48 * 2**20),
        name="finish",
    )(*parts, residual, gain, w_out)


def local(tokens, ln_gain, post_gain, w_query, w_key, w_value, w_out):
    count = lax.axis_size("seq")
    me = lax.axis_index("seq")
    owned = LATENTS // count
    part = owned // CHUNKS
    last = me == count - 1
    gain = ln_gain.reshape(1, D)
    sent = [
        lax.ppermute(tokens[to * owned : (to + 1) * owned], "seq", [(count - 1, to)])
        for to in range(count - 1)
    ]
    own_rows = jnp.where(last, tokens[(count - 1) * owned :], sum(sent))
    queries = jnp.dot(
        rms_rows(own_rows, ln_gain), w_query, preferred_element_type=jnp.float32
    ).astype(jnp.bfloat16)
    keys, values = project_kv(tokens, gain, w_key, w_value)
    flag = last.astype(jnp.int32).reshape(1)
    parts = []
    for chunk in range(CHUNKS):
        mine = queries[chunk * part : (chunk + 1) * part]
        tiled = jnp.broadcast_to(mine[None], (count, part, D))
        rows = lax.all_to_all(tiled, "seq", 0, 0).reshape(count * part, D)
        mixed = attend(chunk, owned, flag, rows, keys, values)
        parts.append(lax.all_to_all(mixed.reshape(count, part, WIDE), "seq", 0, 0))
    return finish(parts, own_rows, post_gain.reshape(1, D), w_out)


def solution(mesh):
    return jax.shard_map(
        local,
        mesh=mesh,
        in_specs=(P(("ctx", "seq"), None), P(), P(), P(), P(), P(), P()),
        out_specs=P(("ctx", "seq"), None),
        check_vma=False,
    )
```

time: 452 us -> 137 us (0.30)
  waiting for transfers between devices: 234 us -> 20.8 us
  matrix products: 92.1 us -> 0.52 us
  Pallas kernels: 0 us -> 40.9 us
  blocking collectives: 72.3 us -> 42.1 us
  starting transfers between devices: 0.09 us -> 26.2 us
  other arithmetic: 24.5 us -> 1.76 us
  between operations: 13.2 us -> 0.26 us
  local copies, waits for them, and re-layouts: 13.6 us -> 4.18 us
    unnamed x5 -> x0, waiting for transfers between devices: 137 us -> none
    psum x1 -> x0, waiting for transfers between devices: 97 us -> none  [spread(): return lax.psum(block, axis)]
    dot_general x36 -> x1, matrix products: 92.1 us -> 0.52 us  [local(): jnp.dot(rms_rows(own_rows, ln_gain), w_query, preferred_element_type=jnp....]
    pmax x1 -> x0, blocking collectives: 72.3 us -> none  [local(): top = lax.pmax(maxima.astype(jnp.bfloat16), 'seq').astype(maxima.dtype)]
    all_to_all x0 -> x2, blocking collectives: none -> 42.1 us  [the longest x1 22.3 us: local(): parts.append(lax.all_to_all(mixed.reshape(count, part, WIDE), 'seq', 0, 0))]
    pallas_call x0 -> x4, Pallas kernels: none -> 40.9 us  [the longest x2 29 us: attend(): pl.pallas_call(functools.partial(attend_kernel, chunk, owned), grid=(coun...]
    ppermute x0 -> x15, waiting for transfers between devices: none -> 20.8 us  [local(): lax.ppermute(tokens[to * owned:(to + 1) * owned], 'seq', [(count - 1, to)])]
    reduce_sum x16 -> x0, other arithmetic: 16.5 us -> none  [one_head(): local_sum = jnp.sum(probs, axis=-1)]
  transfers between devices with their start and end apart: 3 -> 17, of which waited for: 3 -> 1; matrix products, arithmetic and copies ran while one was open for 4% -> 0% of each run, Pallas kernels for 0% -> 28%
where the time goes in v1:
time: 137 us
  blocking collectives  42.1 us (31%)
  Pallas kernels  40.9 us (30%)
  starting transfers between devices  26.2 us (19%)
  waiting for transfers between devices  20.8 us (15%)
  local copies, waits for them, and re-layouts  4.18 us (3%)
  other arithmetic  1.76 us (1%)
    pallas_call x2, Pallas kernels, attend(): pl.pallas_call(functools.partial(attend_kernel, chunk, owned), grid=(coun...  29 us
    all_to_all x1, blocking collectives, local(): parts.append(lax.all_to_all(mixed.reshape(count, part, WIDE), 'seq', 0, 0))  22.3 us
    ppermute x15, waiting for transfers between devices, local(): lax.ppermute(tokens[to * owned:(to + 1) * owned], 'seq', [(count - 1, to)])  20.8 us
    all_to_all x1, blocking collectives, local(): rows = lax.all_to_all(tiled, 'seq', 0, 0).reshape(count * part, D)  19.8 us
    ppermute x15, starting transfers between devices, local(): lax.ppermute(tokens[to * owned:(to + 1) * owned], 'seq', [(count - 1, to)])  13.9 us
    pallas_call x1, Pallas kernels, project_kv(): pl.pallas_call(kv_kernel, grid=(D // cols,), out_shape=(jax.ShapeDtypeStr...  9.26 us
    all_to_all x1, starting transfers between devices, local(): parts.append(lax.all_to_all(mixed.reshape(count, part, WIDE), 'seq', 0, 0))  8.66 us
    all_to_all x1, starting transfers between devices, local(): rows = lax.all_to_all(tiled, 'seq', 0, 0).reshape(count * part, D)  3.65 us
  transfers between devices with their start and end apart: 17, of which 1 were waited for; matrix products, arithmetic and copies ran while one was open for 0% of the time, Pallas kernels for 28%

profile of v1, /device:TPU:0, one launch (start us, length us, event | category | flops | bytes accessed | tf_op | source)
XLA Modules:
  0.0 136.7 jit_solution(7238485664336863754)
XLA Ops:
  0.0 0.0 copy-start
  0.0 1.9 %fusion.6 = (bf16[64,1024]{1,0:T(8,128)(2,1)S(1)}, bf16[64,1024]{1,0:T(8,128)(2,1)S(1)}, bf16[64,1024]{1,0:T(8,128)(2,1)S(1)}, bf16[64,1024]{1,0:T(8,128)(2,1)S(...) fusion(bf16[1024,1024]{1,0:T(8,128)(2,1)} %tokens.1), kind=kLoop, calls=%fused_computation.10 | loop fusion | bytes 3932160 | tf_op jit(solution)/shard_map/slice | solution.py:195
  1.9 0.0 copy-start.7
  1.9 0.7 collective-permute-start.1
  2.6 0.7 collective-permute-start.13
  3.3 0.7 collective-permute-start.12
  4.0 0.7 collective-permute-start.11
  4.6 0.7 collective-permute-start.10
  5.3 0.0 collective-permute-done.1
  5.3 0.7 collective-permute-start.9
  6.0 0.0 collective-permute-done.13
  6.0 1.3 collective-permute-start.8
  7.3 0.0 collective-permute-done.12
  7.3 0.7 collective-permute-start.7
  8.0 0.0 collective-permute-done.11
  8.0 0.7 collective-permute-start.6
  8.7 0.0 collective-permute-done.10
  8.7 0.7 collective-permute-start.5
  9.4 0.0 collective-permute-done.9
  9.4 1.3 collective-permute-start.4
  10.7 0.0 collective-permute-done.8
  10.7 1.3 collective-permute-start.3
  12.0 0.0 collective-permute-done.7
  12.0 0.0 copy-start.4
  12.0 1.3 collective-permute-start.2
  13.3 0.0 collective-permute-done.6
  13.3 0.0 copy-start.5
  13.3 1.3 collective-permute-start
  14.6 0.0 collective-permute-done.5
  14.6 0.0 copy-start.6
  14.7 1.3 collective-permute-start.14
  16.0 0.0 copy-done.4
  16.0 0.0 copy-done.5
  16.0 0.0 copy-done.6
  16.0 0.0 collective-permute-done.4
  16.0 0.0 collective-permute-done.3
  16.0 0.0 collective-permute-done.2
  16.0 20.8 %collective-permute-done = bf16[64,1024]{1,0:T(8,128)(2,1)} collective-permute-done((bf16[64,1024]{1,0:T(8,128)(2,1)S(1)}, bf16[64,1024]{1,0:T(8,128)(2,1)}, u32[]{:S(2)}, u32[]{:S(2)}) %collective-permute-start) | collective-permute-done | bytes 131104 | tf_op jit(solution)/shard_map/ppermute | solution.py:195
  36.8 0.0 collective-permute-done.14
  36.8 1.8 %fusion = (f32[64]{0:T(128)S(1)}, bf16[64,1024]{1,0:T(8,128)(2,1)S(1)}) fusion(bf16[64,1024]{1,0:T(8,128)(2,1)} %collective-permute-done.14, bf16[64,1024]{1,0:T(8,128)(2,1)S(1)} %collective-permute-done.13, bf16[64,1024]{1,0:T(8,128)(2,1)S(1)} %collective-permute-done.12, bf16[64,1024]{1,0:T(8,128)(2,1)S(1)} %collective-permute-done.11, ...), kind=kLoop, calls=%fused_computation.3 | loop fusion | flops 1179584 | bytes 2228481 | tf_op jit(solution)/shard_map/reduce_sum | solution.py:23
  38.6 0.0 copy-done
  38.6 0.0 copy-done.7
  38.6 0.5 convolution_convert_fusion
  39.1 0.1 broadcast_in_dim.8
  39.3 19.8 %all_to_all.20 = bf16[16,32,1024]{2,1,0:T(8,128)(2,1)} all-to-all(bf16[16,32,1024]{2,1,0:T(8,128)(2,1)S(1)} %broadcast_in_dim.8), channel_id=1, replica_groups=mesh['ctx'=8,'seq'=16] {'seq'}, dimensions={0} | all-to-all | bytes 2097152 | tf_op jit(solution)/shard_map/all_to_all | solution.py:208
  59.0 1.1 broadcast_in_dim.6
  60.2 3.7 %all-to-all-start = ((bf16[16,32,1024]{2,1,0:T(8,128)(2,1)}), bf16[16,32,1024]{2,1,0:T(8,128)(2,1)S(1)}, u32[]{:S(2)}, u32[]{:S(2)}) async-start(bf16[16,32,1024]{2,1,0:T(8,128)(2,1)} %broadcast_in_dim.6), calls=%async_computation | async-start | bytes 2097152 | tf_op jit(solution)/shard_map/all_to_all | solution.py:208
  63.8 9.3 %project_kv.1 = (bf16[1024,1024]{1,0:T(8,128)(2,1)}, bf16[1024,1024]{1,0:T(8,128)(2,1)}) custom-call(bf16[1024,1024]{1,0:T(8,128)(2,1)} %tokens.1, f32[1,1024]{1,0:T(1,128)} %bitcast.13, bf16[1024,1024]{1,0:T(8,128)(2,1)} %w_key.1, bf16[1024,1024]{1,0:T(8,128)(2,1)} %w_value.1), custom_call_target="tpu_custom_call" | custom-call | flops 4294967296 | bytes 10485760 | tf_op jit(solution)/shard_map/project_kv/pallas_call | solution.py:42
  73.1 14.6 %attend_1.1 = bf16[512,1152]{1,0:T(8,128)(2,1)} custom-call(s32[1]{0:T(128)} %bitcast.flag, bf16[512,1024]{1,0:T(8,128)(2,1)} %bitcast.12, bf16[1024,1024]{1,0:T(8,128)(2,1)} %get-tuple-element.7.keys, bf16[1024,1024]{1,0:T(8,128)(2,1)} %get-tuple-element.8.values), custom_call_target="tpu_custom_call" | custom-call | flops 8589934592 | bytes 8388608 | tf_op jit(solution)/shard_map/attend_1/pallas_call | solution.py:128
  87.7 0.0 all-to-all-done
  87.7 0.0 copy-start.3
  87.7 1.0 copy-done.3
  88.7 8.7 %all-to-all-start.3 = ((bf16[16,32,1152]{2,1,0:T(8,128)(2,1)}), bf16[16,32,1152]{2,1,0:T(8,128)(2,1)S(1)}, u32[]{:S(2)}, u32[]{:S(2)}) async-start(bf16[16,32,1152]{2,1,0:T(8,128)(2,1)} %bitcast.9), calls=%async_computation.3 | async-start | bytes 2359296 | tf_op jit(solution)/shard_map/all_to_all | solution.py:210
  97.3 14.4 %attend_0.1 = bf16[512,1152]{1,0:T(8,128)(2,1)} custom-call(s32[1]{0:T(128)} %bitcast.flag, bf16[512,1024]{1,0:T(8,128)(2,1)} %bitcast.11, bf16[1024,1024]{1,0:T(8,128)(2,1)} %get-tuple-element.7.keys, bf16[1024,1024]{1,0:T(8,128)(2,1)} %get-tuple-element.8.values), custom_call_target="tpu_custom_call" | custom-call | flops 8589934592 | bytes 8388608 | tf_op jit(solution)/shard_map/attend_0/pallas_call | solution.py:128
  111.7 0.0 copy-start.2
  111.7 0.0 all-to-all-done.3.refs_1_
  111.7 0.0 copy-start.1
  111.7 22.3 %all_to_all.21.refs_0_ = bf16[16,32,1152]{2,1,0:T(8,128)(2,1)S(1)} all-to-all(bf16[16,32,1152]{2,1,0:T(8,128)(2,1)} %bitcast.10), channel_id=1, replica_groups=mesh['ctx'=8,'seq'=16] {'seq'}, dimensions={0} | all-to-all | bytes 2359296 | tf_op jit(solution)/shard_map/all_to_all | solution.py:210
  134.0 0.0 copy-done.2
  134.0 0.0 copy-done.1
  134.1 2.6 %finish.1 = bf16[64,1024]{1,0:T(8,128)(2,1)} custom-call(bf16[16,32,1152]{2,1,0:T(8,128)(2,1)S(1)} %all_to_all.21.refs_0_, bf16[16,32,1152]{2,1,0:T(8,128)(2,1)S(1)} %all-to-all-done.3.refs_1_, bf16[64,1024]{1,0:T(8,128)(2,1)S(1)} %get-tuple-element.10.refs_2_, f32[1,1024]{1,0:T(1,128)S(1)} %bitcast.8, bf16[1024,1024]{1,0:T(8,128)(2,1)S(1)} %copy-done.1), custom_call_target="tpu_custom_call" | custom-call | tf_op jit(solution)/shard_map/finish/pallas_call | solution.py:179
  (2 shorter events, 0.0 us)
Async XLA Ops:
  0.0 38.6 %copy-start = (bf16[1024,1024]{1,0:T(8,128)(2,1)S(1)}, bf16[1024,1024]{1,0:T(8,128)(2,1)}, u32[]{:S(2)}) copy-start(bf16[1024,1024]{1,0:T(8,128)(2,1)} %param.10) | copy-start | bytes 6291460
  1.9 36.7 %copy-start.7 = (f32[1024]{0:T(1024)S(1)}, f32[1024]{0:T(1024)}, u32[]{:S(2)}) copy-start(f32[1024]{0:T(1024)} %param.8) | copy-start | bytes 12292
  1.9 3.4 %collective-permute-start.1 = (bf16[64,1024]{1,0:T(8,128)(2,1)S(1)}, bf16[64,1024]{1,0:T(8,128)(2,1)S(1)}, u32[]{:S(2)}, u32[]{:S(2)}) collective-permute-start(bf16[64,1024]{1,0:T(8,128)(2,1)S(1)} %get-tuple-element.11), channel_id=1, source_target_pairs={{15,1},{31,17},{47,33},{63,49},{79,65},{95,81},{111,97},{127,113}} | collective-permute-start | bytes 393224 | tf_op jit(solution)/shard_map/ppermute | solution.py:195
  2.6 3.4 %collective-permute-start.13 = (bf16[64,1024]{1,0:T(8,128)(2,1)S(1)}, bf16[64,1024]{1,0:T(8,128)(2,1)S(1)}, u32[]{:S(2)}, u32[]{:S(2)}) collective-permute-start(bf16[64,1024]{1,0:T(8,128)(2,1)S(1)} %get-tuple-element.12), channel_id=1, source_target_pairs={{15,13},{31,29},{47,45},{63,61},{79,77},{95,93},{111,109},{127,125}} | collective-permute-start | bytes 393224 | tf_op jit(solution)/shard_map/ppermute | solution.py:195
  3.3 4.0 %collective-permute-start.12 = (bf16[64,1024]{1,0:T(8,128)(2,1)S(1)}, bf16[64,1024]{1,0:T(8,128)(2,1)S(1)}, u32[]{:S(2)}, u32[]{:S(2)}) collective-permute-start(bf16[64,1024]{1,0:T(8,128)(2,1)S(1)} %get-tuple-element.13), channel_id=1, source_target_pairs={{15,12},{31,28},{47,44},{63,60},{79,76},{95,92},{111,108},{127,124}} | collective-permute-start | bytes 393224 | tf_op jit(solution)/shard_map/ppermute | solution.py:195
  4.0 4.0 %collective-permute-start.11 = (bf16[64,1024]{1,0:T(8,128)(2,1)S(1)}, bf16[64,1024]{1,0:T(8,128)(2,1)S(1)}, u32[]{:S(2)}, u32[]{:S(2)}) collective-permute-start(bf16[64,1024]{1,0:T(8,128)(2,1)S(1)} %get-tuple-element.14), channel_id=1, source_target_pairs={{15,11},{31,27},{47,43},{63,59},{79,75},{95,91},{111,107},{127,123}} | collective-permute-start | bytes 393224 | tf_op jit(solution)/shard_map/ppermute | solution.py:195
  4.6 4.1 %collective-permute-start.10 = (bf16[64,1024]{1,0:T(8,128)(2,1)S(1)}, bf16[64,1024]{1,0:T(8,128)(2,1)S(1)}, u32[]{:S(2)}, u32[]{:S(2)}) collective-permute-start(bf16[64,1024]{1,0:T(8,128)(2,1)S(1)} %get-tuple-element.15), channel_id=1, source_target_pairs={{15,10},{31,26},{47,42},{63,58},{79,74},{95,90},{111,106},{127,122}} | collective-permute-start | bytes 393224 | tf_op jit(solution)/shard_map/ppermute | solution.py:195
  5.3 4.1 %collective-permute-start.9 = (bf16[64,1024]{1,0:T(8,128)(2,1)S(1)}, bf16[64,1024]{1,0:T(8,128)(2,1)S(1)}, u32[]{:S(2)}, u32[]{:S(2)}) collective-permute-start(bf16[64,1024]{1,0:T(8,128)(2,1)S(1)} %get-tuple-element.16), channel_id=1, source_target_pairs={{15,9},{31,25},{47,41},{63,57},{79,73},{95,89},{111,105},{127,121}} | collective-permute-start | bytes 393224 | tf_op jit(solution)/shard_map/ppermute | solution.py:195
  6.0 4.7 %collective-permute-start.8 = (bf16[64,1024]{1,0:T(8,128)(2,1)S(1)}, bf16[64,1024]{1,0:T(8,128)(2,1)}, u32[]{:S(2)}, u32[]{:S(2)}) collective-permute-start(bf16[64,1024]{1,0:T(8,128)(2,1)S(1)} %get-tuple-element.17), channel_id=1, source_target_pairs={{15,8},{31,24},{47,40},{63,56},{79,72},{95,88},{111,104},{127,120}} | collective-permute-start | bytes 393224 | tf_op jit(solution)/shard_map/ppermute | solution.py:195
  7.3 4.7 %collective-permute-start.7 = (bf16[64,1024]{1,0:T(8,128)(2,1)S(1)}, bf16[64,1024]{1,0:T(8,128)(2,1)S(1)}, u32[]{:S(2)}, u32[]{:S(2)}) collective-permute-start(bf16[64,1024]{1,0:T(8,128)(2,1)S(1)} %get-tuple-element.18), channel_id=1, source_target_pairs={{15,7},{31,23},{47,39},{63,55},{79,71},{95,87},{111,103},{127,119}} | collective-permute-start | bytes 393224 | tf_op jit(solution)/shard_map/ppermute | solution.py:195
  8.0 5.3 %collective-permute-start.6 = (bf16[64,1024]{1,0:T(8,128)(2,1)S(1)}, bf16[64,1024]{1,0:T(8,128)(2,1)S(1)}, u32[]{:S(2)}, u32[]{:S(2)}) collective-permute-start(bf16[64,1024]{1,0:T(8,128)(2,1)S(1)} %get-tuple-element.19), channel_id=1, source_target_pairs={{15,6},{31,22},{47,38},{63,54},{79,70},{95,86},{111,102},{127,118}} | collective-permute-start | bytes 393224 | tf_op jit(solution)/shard_map/ppermute | solution.py:195
  8.7 5.9 %collective-permute-start.5 = (bf16[64,1024]{1,0:T(8,128)(2,1)S(1)}, bf16[64,1024]{1,0:T(8,128)(2,1)S(1)}, u32[]{:S(2)}, u32[]{:S(2)}) collective-permute-start(bf16[64,1024]{1,0:T(8,128)(2,1)S(1)} %get-tuple-element.20), channel_id=1, source_target_pairs={{15,5},{31,21},{47,37},{63,53},{79,69},{95,85},{111,101},{127,117}} | collective-permute-start | bytes 393224 | tf_op jit(solution)/shard_map/ppermute | solution.py:195
  9.4 6.6 %collective-permute-start.4 = (bf16[64,1024]{1,0:T(8,128)(2,1)S(1)}, bf16[64,1024]{1,0:T(8,128)(2,1)}, u32[]{:S(2)}, u32[]{:S(2)}) collective-permute-start(bf16[64,1024]{1,0:T(8,128)(2,1)S(1)} %get-tuple-element.21), channel_id=1, source_target_pairs={{15,4},{31,20},{47,36},{63,52},{79,68},{95,84},{111,100},{127,116}} | collective-permute-start | bytes 393224 | tf_op jit(solution)/shard_map/ppermute | solution.py:195
  10.7 5.3 %collective-permute-start.3 = (bf16[64,1024]{1,0:T(8,128)(2,1)S(1)}, bf16[64,1024]{1,0:T(8,128)(2,1)}, u32[]{:S(2)}, u32[]{:S(2)}) collective-permute-start(bf16[64,1024]{1,0:T(8,128)(2,1)S(1)} %get-tuple-element.22), channel_id=1, source_target_pairs={{15,3},{31,19},{47,35},{63,51},{79,67},{95,83},{111,99},{127,115}} | collective-permute-start | bytes 393224 | tf_op jit(solution)/shard_map/ppermute | solution.py:195
  12.0 4.0 %copy-start.4 = (bf16[64,1024]{1,0:T(8,128)(2,1)}, bf16[64,1024]{1,0:T(8,128)(2,1)S(1)}, u32[]{:S(2)}) copy-start(bf16[64,1024]{1,0:T(8,128)(2,1)S(1)} %collective-permute-done.7) | copy-start | bytes 393220
  12.0 4.0 %collective-permute-start.2 = (bf16[64,1024]{1,0:T(8,128)(2,1)S(1)}, bf16[64,1024]{1,0:T(8,128)(2,1)}, u32[]{:S(2)}, u32[]{:S(2)}) collective-permute-start(bf16[64,1024]{1,0:T(8,128)(2,1)S(1)} %get-tuple-element.23), channel_id=1, source_target_pairs={{15,2},{31,18},{47,34},{63,50},{79,66},{95,82},{111,98},{127,114}} | collective-permute-start | bytes 393224 | tf_op jit(solution)/shard_map/ppermute | solution.py:195
  13.3 2.7 %copy-start.5 = (bf16[64,1024]{1,0:T(8,128)(2,1)}, bf16[64,1024]{1,0:T(8,128)(2,1)S(1)}, u32[]{:S(2)}) copy-start(bf16[64,1024]{1,0:T(8,128)(2,1)S(1)} %collective-permute-done.6) | copy-start | bytes 393220
  13.3 23.5 %collective-permute-start = (bf16[64,1024]{1,0:T(8,128)(2,1)S(1)}, bf16[64,1024]{1,0:T(8,128)(2,1)}, u32[]{:S(2)}, u32[]{:S(2)}) collective-permute-start(bf16[64,1024]{1,0:T(8,128)(2,1)S(1)} %get-tuple-element.24), channel_id=1, source_target_pairs={{15,0},{31,16},{47,32},{63,48},{79,64},{95,80},{111,96},{127,112}} | collective-permute-start | bytes 393224 | tf_op jit(solution)/shard_map/ppermute | solution.py:195
  14.6 1.4 copy-start.6
  14.7 22.1 %collective-permute-start.14 = (bf16[64,1024]{1,0:T(8,128)(2,1)S(1)}, bf16[64,1024]{1,0:T(8,128)(2,1)}, u32[]{:S(2)}, u32[]{:S(2)}) collective-permute-start(bf16[64,1024]{1,0:T(8,128)(2,1)S(1)} %get-tuple-element.25), channel_id=1, source_target_pairs={{15,14},{31,30},{47,46},{63,62},{79,78},{95,94},{111,110},{127,126}} | collective-permute-start | bytes 393224 | tf_op jit(solution)/shard_map/ppermute | solution.py:195
  60.2 27.5 %all-to-all-start = ((bf16[16,32,1024]{2,1,0:T(8,128)(2,1)}), bf16[16,32,1024]{2,1,0:T(8,128)(2,1)S(1)}, u32[]{:S(2)}, u32[]{:S(2)}) async-start(bf16[16,32,1024]{2,1,0:T(8,128)(2,1)} %broadcast_in_dim.6), calls=%async_computation | async-start | bytes 2097152 | tf_op jit(solution)/shard_map/all_to_all | solution.py:208
  87.7 1.0 copy-start.3
  88.7 23.1 %all-to-all-start.3 = ((bf16[16,32,1152]{2,1,0:T(8,128)(2,1)}), bf16[16,32,1152]{2,1,0:T(8,128)(2,1)S(1)}, u32[]{:S(2)}, u32[]{:S(2)}) async-start(bf16[16,32,1152]{2,1,0:T(8,128)(2,1)} %bitcast.9), calls=%async_computation.3 | async-start | bytes 2359296 | tf_op jit(solution)/shard_map/all_to_all | solution.py:210
  111.7 22.3 %copy-start.2 = (f32[1024]{0:T(1024)S(1)}, f32[1024]{0:T(1024)}, u32[]{:S(2)}) copy-start(f32[1024]{0:T(1024)} %param.9) | copy-start | bytes 12292
  111.7 22.3 %copy-start.1 = (bf16[1024,1024]{1,0:T(8,128)(2,1)S(1)}, bf16[1024,1024]{1,0:T(8,128)(2,1)}, u32[]{:S(2)}) copy-start(bf16[1024,1024]{1,0:T(8,128)(2,1)} %refs_4_.1) | copy-start | bytes 6291460

commit v2 on v1

v2 whole, which is shorter than its diff:
```python
import functools

import jax
import jax.numpy as jnp
from jax import lax
from jax.experimental import pallas as pl
from jax.experimental.pallas import tpu as pltpu
from jax.sharding import PartitionSpec as P

D = 1024
HEADS = 16
HEAD_DIM = 64
PAIRS = HEADS // 2
LATENTS = 1024
PART = 16
LOG2E = 1.4426950408889634
EXP2_SCALE = LOG2E * HEAD_DIM ** (-0.5)
MASKED = -1e30
WIDE = D + 128
MIB = 2**20

BUNDLES = ((3, 0, 2, 1), (11, 8, 10, 9), (12, 13, 4, 5), (14, 6, 7))


def rms_rows(rows, gain):
    wide = rows.astype(jnp.float32)
    scale = lax.rsqrt(jnp.mean(wide * wide, axis=-1, keepdims=True) + 1e-06)
    return (wide * scale * gain).astype(jnp.bfloat16)


def kv_kernel(tokens, gain, w_key, w_value, keys, values, normed):
    @pl.when(pl.program_id(0) == 0)
    def _():
        normed[...] = rms_rows(tokens[...], gain[...])

    rows = normed[...]
    keys[...] = jnp.dot(rows, w_key[...], preferred_element_type=jnp.float32).astype(jnp.bfloat16)
    values[...] = jnp.dot(rows, w_value[...], preferred_element_type=jnp.float32).astype(jnp.bfloat16)


def project_kv(tokens, gain, w_key, w_value):
    rows = tokens.shape[0]
    cols = 256
    whole = lambda c: (0, 0)
    block = lambda c: (0, c)
    return pl.pallas_call(
        kv_kernel,
        grid=(D // cols,),
        out_shape=(jax.ShapeDtypeStruct((rows, D), jnp.bfloat16),) * 2,
        in_specs=[
            pl.BlockSpec((rows, D), whole, pipeline_mode=pl.Buffered(1)),
            pl.BlockSpec((1, D), whole),
            pl.BlockSpec((D, cols), block),
            pl.BlockSpec((D, cols), block),
        ],
        out_specs=(pl.BlockSpec((rows, cols), block),) * 2,
        scratch_shapes=[pltpu.VMEM((rows, D), jnp.bfloat16)],
        compiler_params=pltpu.CompilerParams(vmem_limit_bytes=20 * MIB),
        cost_estimate=pl.CostEstimate(flops=4 * rows * D * D, bytes_accessed=10 * rows * D, transcendentals=0),
        name="project_kv",
    )(tokens, gain, w_key, w_value)


def query_kernel(count, gain, w_query, *refs):
    parts, (own, *tiled) = refs[:5], refs[5:]
    rows = parts[0][...].astype(jnp.float32)
    for part in parts[1:]:
        rows = rows + part[...].astype(jnp.float32)
    rows = rows.astype(jnp.bfloat16)
    own[...] = rows
    queries = jnp.dot(
        rms_rows(rows, gain[...]), w_query[...], preferred_element_type=jnp.float32
    ).astype(jnp.bfloat16)
    begin = 0
    for each in tiled:
        end = begin + each.shape[1]
        for to in range(count):
            each[to] = queries[begin:end]
        begin = end


def project_queries(count, gain, w_query, parts):
    rows = parts[0].shape[0]
    return pl.pallas_call(
        functools.partial(query_kernel, count),
        out_shape=(jax.ShapeDtypeStruct((rows, D), jnp.bfloat16),)
        + tuple(jax.ShapeDtypeStruct((count, each, D), jnp.bfloat16) for each in (PART, rows - PART)),
        compiler_params=pltpu.CompilerParams(vmem_limit_bytes=16 * MIB),
        cost_estimate=pl.CostEstimate(flops=2 * rows * D * D, bytes_accessed=4 * D * D, transcendentals=0),
        name="project_queries",
    )(gain, w_query, *parts)


def attend_kernel(first, owned, flag, queries, keys, values, out, s_a, s_b, p_a, p_b, top_a, top_b, lse):
    group, part, _ = queries.shape
    rows = group * part
    count = keys.shape[0]
    offset = (first + pl.program_id(0)) * part
    low = lax.broadcasted_iota(jnp.int32, (1, 128), 1) < HEAD_DIM
    sub = 32

    def score(pair, s):
        at = pl.ds(pl.multiple_of(pair * 128, 128), 128)
        query = queries[:, :, at].reshape(rows, 128)
        none = jnp.zeros_like(query)
        both = jnp.concatenate([jnp.where(low, query, none), jnp.where(low, none, query)], axis=0)
        s[...] = lax.dot_general(
            both, keys[:, at], (((1,), (1,)), ((), ())), preferred_element_type=jnp.float32
        )

    def soften(causal, s, p, top):
        for begin in range(0, 2 * rows, sub):
            at = slice(begin, begin + sub)
            begin = begin % rows
            span = count
            if causal:
                last = (begin + sub - 1) // part * owned + owned
                span = min(count, -(-last // 128) * 128)
            block = s[at, 0:span]
            if causal:
                row = begin + lax.broadcasted_iota(jnp.int32, (sub, span), 0)
                query_pos = row // part * owned + offset + row % part
                key_pos = lax.broadcasted_iota(jnp.int32, (sub, span), 1)
                block = jnp.where(key_pos <= query_pos, block, MASKED)
            most = jnp.max(block, axis=-1, keepdims=True)
            p[at, 0:span] = jnp.exp2((block - most) * EXP2_SCALE).astype(jnp.bfloat16)
            if span < count:
                p[at, span:count] = jnp.zeros((sub, count - span), jnp.bfloat16)
            top[at, :] = jnp.broadcast_to(most, (sub, 128))

    def blend(pair, p, top):
        at = pl.ds(pl.multiple_of(jnp.maximum(pair, 0) * 128, 128), 128)
        ones = jnp.ones((count, 128), jnp.bfloat16)
        mixed = jnp.dot(
            p[...], jnp.concatenate([values[:, at], ones], axis=1), preferred_element_type=jnp.float32
        )
        mix, total = mixed[:, 0:128], mixed[:, 128:256]
        both = jnp.where(low, mix[:rows], mix[rows:]) / jnp.where(low, total[:rows], total[rows:])
        out[:, :, at] = both.astype(jnp.bfloat16).reshape(group, part, 128)
        level = top[...] * EXP2_SCALE + jnp.log2(total)
        lane = lax.broadcasted_iota(jnp.int32, (rows, 128), 1)
        held = jnp.where(lane == 2 * pair, level[:rows], lse[...])
        lse[...] = jnp.where(lane == 2 * pair + 1, level[rows:], held)

    def attention(causal):
        score(0, s_a)
        score(1, s_b)
        soften(causal, s_a, p_a, top_a)

        def two_pairs(i, _):
            score(2 * i, s_a)
            blend(2 * i - 2, p_a, top_a)
            soften(causal, s_b, p_b, top_b)
            score(2 * i + 1, s_b)
            blend(2 * i - 1, p_b, top_b)
            soften(causal, s_a, p_a, top_a)
            return 0

        lse[...] = jnp.zeros_like(lse)
        lax.fori_loop(1, PAIRS // 2, two_pairs, 0)
        blend(PAIRS - 2, p_a, top_a)
        soften(causal, s_b, p_b, top_b)
        blend(PAIRS - 1, p_b, top_b)
        level = lse[...]
        one = level.astype(jnp.bfloat16).astype(jnp.float32)
        two = (level - one).astype(jnp.bfloat16).astype(jnp.float32)
        three = level - one - two
        pieces = one + pltpu.roll(two, HEADS, 1) + pltpu.roll(three, 2 * HEADS, 1)
        out[:, :, D:WIDE] = pieces.astype(jnp.bfloat16).reshape(group, part, 128)

    @pl.when(flag[0] == 0)
    def _():
        attention(False)

    @pl.when(flag[0] != 0)
    def _():
        attention(True)


def attend(first, begin, steps, owned, is_last, queries, keys, values):
    group = queries.shape[0]
    rows = group * PART
    count = keys.shape[0]
    whole = lambda c: (0, 0)
    return pl.pallas_call(
        functools.partial(attend_kernel, first, owned),
        grid=(steps,),
        out_shape=jax.ShapeDtypeStruct((group, steps * PART, WIDE), jnp.bfloat16),
        in_specs=[
            pl.BlockSpec(memory_space=pltpu.SMEM),
            pl.BlockSpec((group, PART, D), lambda c: (0, begin + c, 0)),
            pl.BlockSpec((count, D), whole, pipeline_mode=pl.Buffered(1)),
            pl.BlockSpec((count, D), whole, pipeline_mode=pl.Buffered(1)),
        ],
        out_specs=pl.BlockSpec((group, PART, WIDE), lambda c: (0, c, 0)),
        scratch_shapes=[
            pltpu.VMEM((2 * rows, count), jnp.float32),
            pltpu.VMEM((2 * rows, count), jnp.float32),
            pltpu.VMEM((2 * rows, count), jnp.bfloat16),
            pltpu.VMEM((2 * rows, count), jnp.bfloat16),
            pltpu.VMEM((2 * rows, 128), jnp.float32),
            pltpu.VMEM((2 * rows, 128), jnp.float32),
            pltpu.VMEM((rows, 128), jnp.float32),
        ],
        compiler_params=pltpu.CompilerParams(vmem_limit_bytes=28 * MIB),
        cost_estimate=pl.CostEstimate(
            flops=16 * steps * rows * D * D,
            bytes_accessed=8 * D * D,
            transcendentals=HEADS * steps * rows * D,
        ),
        name="attend_%d" % first,
    )(is_last, queries, keys, values)


def finish_kernel(number, *refs):
    parts, (own, gain, w_out, out) = refs[:number], refs[number:]
    head = lax.broadcasted_iota(jnp.int32, (128, D), 0)
    column = lax.broadcasted_iota(jnp.int32, (128, D), 1)
    spread = (column // HEAD_DIM == head).astype(jnp.bfloat16)
    spread = jnp.concatenate([spread, spread], axis=0)
    posts = []
    for each in parts:
        count, part, _ = each.shape
        lane = lax.broadcasted_iota(jnp.int32, (count * part, 128), 1)
        pieces = each[:, :, D:WIDE].astype(jnp.float32).reshape(count * part, 128)
        level = pieces + pltpu.roll(pieces, 128 - HEADS, 1) + pltpu.roll(pieces, 128 - 2 * HEADS, 1)
        level = jnp.where(lane < HEADS, level, 0.0).reshape(count, part, 128)
        weight = jnp.exp2(level - jnp.max(level, axis=0, keepdims=True))
        weight = weight / jnp.sum(weight, axis=0, keepdims=True)
        weight = weight.reshape(count * part, 128)
        high = weight.astype(jnp.bfloat16)
        rest = (weight - high.astype(jnp.float32)).astype(jnp.bfloat16)
        wide = jnp.dot(
            jnp.concatenate([high, rest], axis=1), spread, preferred_element_type=jnp.float32
        ).reshape(count, part, D)
        mix = jnp.sum(wide * each[:, :, 0:D].astype(jnp.float32), axis=0)
        posts.append(rms_rows(mix.astype(jnp.bfloat16), gain[...]))
    mixed = own[...].astype(jnp.float32) + jnp.dot(
        jnp.concatenate(posts, axis=0), w_out[...], preferred_element_type=jnp.float32
    )
    out[...] = mixed.astype(jnp.bfloat16)


def finish(parts, own, gain, w_out):
    rows = own.shape[0]
    return pl.pallas_call(
        functools.partial(finish_kernel, len(parts)),
        out_shape=jax.ShapeDtypeStruct((rows, D), jnp.bfloat16),
        compiler_params=pltpu.CompilerParams(vmem_limit_bytes=28 * MIB),
        cost_estimate=pl.CostEstimate(flops=4 * rows * D * D, bytes_accessed=8 * D * D, transcendentals=0),
        name="finish",
    )(*parts, own, gain, w_out)


def pack_kernel(owned, source, flag, tokens, own, *bundles):
    def block(to):
        return tokens[to * owned : (to + 1) * owned, :]

    mine = block(source)
    own[...] = jnp.where(flag[0] != 0, mine, jnp.zeros_like(mine))
    for members, bundle in zip(BUNDLES, bundles):
        for place in range(4):
            at = slice(place * owned, (place + 1) * owned)
            bundle[at, :] = block(members[min(place, len(members) - 1)])


def relay_kernel(*refs):
    bundles, outs = refs[:4], refs[4:]
    rows = outs[0].shape[0]
    for place, out in enumerate(outs):
        at = slice(place * rows, (place + 1) * rows)
        total = bundles[0][at, :].astype(jnp.float32)
        for bundle in bundles[1:]:
            total = total + bundle[at, :].astype(jnp.float32)
        out[...] = total.astype(jnp.bfloat16)


def scatter(tokens, owned, source, flag, beside):
    limit = pltpu.CompilerParams(vmem_limit_bytes=16 * MIB)
    block = jax.ShapeDtypeStruct((owned, D), jnp.bfloat16)
    smem = pl.BlockSpec(memory_space=pltpu.SMEM)
    vmem = pl.BlockSpec(memory_space=pltpu.VMEM)
    own, *bundles = pl.pallas_call(
        functools.partial(pack_kernel, owned, source),
        out_shape=(block,) + (jax.ShapeDtypeStruct((4 * owned, D), jnp.bfloat16),) * 4,
        in_specs=[smem, vmem],
        compiler_params=limit,
        cost_estimate=pl.CostEstimate(flops=0, bytes_accessed=8 * D * D, transcendentals=0),
        name="pack",
    )(flag, tokens)
    bundles = [
        lax.ppermute(bundle, "seq", [(source, members[0])]) for members, bundle in zip(BUNDLES, bundles)
    ]
    bundles, _ = lax.optimization_barrier((bundles, beside))
    kept, *passed = pl.pallas_call(
        relay_kernel,
        out_shape=(block,) * 4,
        compiler_params=limit,
        cost_estimate=pl.CostEstimate(flops=0, bytes_accessed=4 * D * D, transcendentals=0),
        name="relay",
    )(*bundles)
    parts = [own, kept]
    for place in range(1, 4):
        pairs = [(members[0], members[place]) for members in BUNDLES if place < len(members)]
        parts.append(lax.ppermute(passed[place - 1], "seq", pairs))
    return parts


def local(tokens, ln_gain, post_gain, w_query, w_key, w_value, w_out):
    count = lax.axis_size("seq")
    last = lax.axis_index("seq") == count - 1
    flag = last.astype(jnp.int32).reshape(1)
    owned = LATENTS // count
    gain = ln_gain.reshape(1, D)
    keys, values = project_kv(tokens, gain, w_key, w_value)
    parts = scatter(tokens, owned, count - 1, flag, keys)
    own, tiled_a, tiled_b = project_queries(count, gain, w_query, parts)
    rows_a = lax.all_to_all(tiled_a, "seq", 0, 0)
    rows_a, tiled_b = lax.optimization_barrier((rows_a, tiled_b))
    rows_b = lax.all_to_all(tiled_b, "seq", 0, 0)
    mixed_a = attend(0, 0, 1, owned, flag, rows_a, keys, values)
    rows_b, _ = lax.optimization_barrier((rows_b, mixed_a))
    mixed_b = attend(1, 0, 2, owned, flag, rows_b, keys, values)
    rows_c, _ = lax.optimization_barrier((rows_b, mixed_b))
    mixed_c = attend(3, 2, 1, owned, flag, rows_c, keys, values)
    mixed = [lax.all_to_all(each, "seq", 0, 0) for each in (mixed_a, mixed_b, mixed_c)]
    return finish(mixed, own, post_gain.reshape(1, D), w_out)


def solution(mesh):
    return jax.shard_map(
        local,
        mesh=mesh,
        in_specs=(P(("ctx", "seq"), None), P(), P(), P(), P(), P(), P()),
        out_specs=P(("ctx", "seq"), None),
        check_vma=False,
    )
```

time: 137 us -> 142 us (1.036)
  blocking collectives: 42.1 us -> 56.2 us
  starting transfers between devices: 26.2 us -> 13.4 us
  local copies, waits for them, and re-layouts: 4.18 us -> 13.3 us
  waiting for transfers between devices: 20.8 us -> 18.3 us
  other arithmetic: 1.76 us -> 0 us
    all_to_all x2 -> x3, blocking collectives: 42.1 us -> 56.2 us  [the longest x2 36.7 us: local(): lax.all_to_all(each, 'seq', 0, 0)]
    unnamed x16 -> x32, local copies, waits for them, and re-layouts: 1.01 us -> 13.3 us
    ppermute x15 -> x7, waiting for transfers between devices: 20.8 us -> 9.1 us  [the longest x3 9.09 us: scatter(): parts.append(lax.ppermute(passed[place - 1], 'seq', pairs))]
    all_to_all x2, waiting for transfers between devices: 0.01 us -> 9.23 us  [the longest x1 9.23 us: local(): rows_b = lax.all_to_all(tiled_b, 'seq', 0, 0)]
    ppermute x15 -> x7, starting transfers between devices: 13.9 us -> 5.93 us  [the longest x3 3.02 us: scatter(): parts.append(lax.ppermute(passed[place - 1], 'seq', pairs))]
    all_to_all x2, starting transfers between devices: 12.3 us -> 7.5 us  [the longest x1 3.79 us: local(): lax.all_to_all(each, 'seq', 0, 0)]
    pallas_call x1, Pallas kernels: 9.26 us -> 6.9 us  [project_kv(): pl.pallas_call(kv_kernel, grid=(D // cols,), out_shape=(jax.ShapeDtypeStr...]
    slice x2 -> x0, local copies, waits for them, and re-layouts: 1.92 us -> none  [the longest x1 1.91 us: local(): tokens[to * owned:(to + 1) * owned]]
  transfers between devices with their start and end apart: 17 -> 9, of which waited for: 1 -> 2; matrix products, arithmetic and copies ran while one was open for 0% -> 0% of each run, Pallas kernels for 28% -> 26%
where the time goes in v2:
time: 142 us; the launch traced here: 141 us
  blocking collectives  56.2 us (40%)
  Pallas kernels  39.8 us (28%)
  waiting for transfers between devices  18.3 us (13%)
  starting transfers between devices  13.4 us (9%)
  local copies, waits for them, and re-layouts  13.3 us (9%)
    all_to_all x2, blocking collectives, local(): lax.all_to_all(each, 'seq', 0, 0)  36.7 us
    pallas_call x3, Pallas kernels, attend(): pl.pallas_call(functools.partial(attend_kernel, first, owned), grid=(step...  29.7 us
    all_to_all x1, blocking collectives, local(): rows_a = lax.all_to_all(tiled_a, 'seq', 0, 0)  19.5 us
    unnamed x32, local copies, waits for them, and re-layouts  13.3 us
    all_to_all x1, waiting for transfers between devices, local(): rows_b = lax.all_to_all(tiled_b, 'seq', 0, 0)  9.23 us
    ppermute x3, waiting for transfers between devices, scatter(): parts.append(lax.ppermute(passed[place - 1], 'seq', pairs))  9.09 us
    pallas_call x1, Pallas kernels, project_kv(): pl.pallas_call(kv_kernel, grid=(D // cols,), out_shape=(jax.ShapeDtypeStr...  6.9 us
    all_to_all x1, starting transfers between devices, local(): lax.all_to_all(each, 'seq', 0, 0)  3.79 us
  transfers between devices with their start and end apart: 9, of which 2 were waited for; matrix products, arithmetic and copies ran while one was open for 0% of the time, Pallas kernels for 26%

profile of v2, /device:TPU:0, one launch (start us, length us, event | category | flops | bytes accessed | tf_op | source)
XLA Modules:
  0.0 141.4 jit_solution(4894285688005538317)
XLA Ops:
  0.0 0.0 copy-start.6
  0.0 0.0 copy-start
  0.0 1.6 %copy-done = bf16[1024,1024]{1,0:T(8,128)(2,1)S(1)} copy-done((bf16[1024,1024]{1,0:T(8,128)(2,1)S(1)}, bf16[1024,1024]{1,0:T(8,128)(2,1)}, u32[]{:S(2)}) %copy-start) | copy-done | bytes 2097176
  1.6 0.0 copy-start.1
  1.6 0.1 pack.1
  1.8 0.8 collective-permute-start
  2.6 0.7 collective-permute-start.1
  3.3 0.7 collective-permute-start.2
  4.0 0.7 collective-permute-start.3
  4.7 0.0 copy-done.6
  4.7 0.0 copy-done.1
  4.7 0.0 copy-start.8
  4.7 1.6 %copy-done.8 = bf16[1024,1024]{1,0:T(8,128)(2,1)S(1)} copy-done((bf16[1024,1024]{1,0:T(8,128)(2,1)S(1)}, bf16[1024,1024]{1,0:T(8,128)(2,1)}, u32[]{:S(2)}) %copy-start.8) | copy-done | bytes 2097176
  6.3 0.0 copy-start.9
  6.3 1.6 %copy-done.9 = bf16[1024,1024]{1,0:T(8,128)(2,1)S(1)} copy-done((bf16[1024,1024]{1,0:T(8,128)(2,1)S(1)}, bf16[1024,1024]{1,0:T(8,128)(2,1)}, u32[]{:S(2)}) %copy-start.9) | copy-done | bytes 2097176
  7.9 6.9 %project_kv.1 = (bf16[1024,1024]{1,0:T(8,128)(2,1)S(1)}, bf16[1024,1024]{1,0:T(8,128)(2,1)S(1)}) custom-call(bf16[1024,1024]{1,0:T(8,128)(2,1)S(1)} %copy-done.1, f32[1,1024]{1,0:T(1,128)S(1)} %bitcast.3, bf16[1024,1024]{1,0:T(8,128)(2,1)S(1)} %copy-done.8, bf16[1024,1024]{1,0:T(8,128)(2,1)S(1)} %copy-done.9), custom_call_target="tpu_custom_call" | custom-call | flops 4294967296 | bytes 10485760 | tf_op jit(solution)/shard_map/project_kv/pallas_call | solution.py:46
  14.8 0.0 copy-start.10
  14.8 0.0 copy-start.13
  14.8 0.0 copy-start.2
  14.8 0.0 collective-permute-done.refs_0_
  14.9 0.0 collective-permute-done.1.refs_1_
  14.9 0.0 collective-permute-done.2.refs_2_
  14.9 0.0 collective-permute-done.3.refs_3_
  14.9 0.3 relay.1
  15.2 1.6 %collective-permute-start.4 = (bf16[64,1024]{1,0:T(8,128)(2,1)S(1)}, bf16[64,1024]{1,0:T(8,128)(2,1)S(1)}, u32[]{:S(2)}, u32[]{:S(2)}) collective-permute-start(bf16[64,1024]{1,0:T(8,128)(2,1)S(1)} %get-tuple-element.38), channel_id=1, source_target_pairs={{3,0},{11,8},{12,13},{14,6},{19,16},{27,24},{28,29},{30,22},{35,32... | collective-permute-start | bytes 393224 | tf_op jit(solution)/shard_map/ppermute | solution.py:305
  16.7 0.8 collective-permute-start.5
  17.5 0.7 collective-permute-start.6
  18.2 9.1 %collective-permute-done.4.refs_2_ = bf16[64,1024]{1,0:T(8,128)(2,1)S(1)} collective-permute-done((bf16[64,1024]{1,0:T(8,128)(2,1)S(1)}, bf16[64,1024]{1,0:T(8,128)(2,1)S(1)}, u32[]{:S(2)}, u32[]{:S(2)}) %collective-permute-start.4) | collective-permute-done | bytes 131104 | tf_op jit(solution)/shard_map/ppermute | solution.py:305
  27.3 0.0 collective-permute-done.5.refs_3_
  27.3 0.0 collective-permute-done.6.refs_4_
  27.3 0.0 copy-done.2
  27.3 0.7 project_queries.1
  28.0 0.0 copy-done.10
  28.0 0.0 copy-done.13
  28.1 0.0 copy-start.4
  28.1 1.2 copy-done.4
  29.2 19.5 %all_to_all.25.queries = bf16[16,16,1024]{2,1,0:T(8,128)(2,1)S(1)} all-to-all(bf16[16,16,1024]{2,1,0:T(8,128)(2,1)S(1)} %get-tuple-element.41), channel_id=1, replica_groups=mesh['ctx'=8,'seq'=16] {'seq'}, dimensions={0} | all-to-all | bytes 1048576 | tf_op jit(solution)/shard_map/all_to_all | solution.py:318
  48.7 3.7 %all-to-all-start.2 = ((bf16[16,48,1024]{2,1,0:T(8,128)(2,1)}), bf16[16,48,1024]{2,1,0:T(8,128)(2,1)S(1)}, u32[]{:S(2)}, u32[]{:S(2)}) async-start(bf16[16,48,1024]{2,1,0:T(8,128)(2,1)} %copy-done.4), calls=%async_computation.2 | async-start | bytes 3145728 | tf_op jit(solution)/shard_map/all_to_all | solution.py:320
  52.4 0.0 copy-start.11
  52.4 1.6 %copy-done.11 = bf16[1024,1024]{1,0:T(8,128)(2,1)S(1)} copy-done((bf16[1024,1024]{1,0:T(8,128)(2,1)S(1)}, bf16[1024,1024]{1,0:T(8,128)(2,1)}, u32[]{:S(2)}) %copy-start.11) | copy-done | bytes 2097176
  54.0 0.0 copy-start.14
  54.0 1.6 %copy-done.14 = bf16[1024,1024]{1,0:T(8,128)(2,1)S(1)} copy-done((bf16[1024,1024]{1,0:T(8,128)(2,1)S(1)}, bf16[1024,1024]{1,0:T(8,128)(2,1)}, u32[]{:S(2)}) %copy-start.14) | copy-done | bytes 2097176
  55.6 7.9 %attend_0.1 = bf16[16,16,1152]{2,1,0:T(8,128)(2,1)} custom-call(s32[1]{0:T(128)} %bitcast.flag, bf16[16,16,1024]{2,1,0:T(8,128)(2,1)S(1)} %all_to_all.25.queries, bf16[1024,1024]{1,0:T(8,128)(2,1)S(1)} %copy-done.11, bf16[1024,1024]{1,0:T(8,128)(2,1)S(1)} %copy-done.14), custom_call_target="tpu_custom_call" | custom-call | flops 4294967296 | bytes 8388608 | tf_op jit(solution)/shard_map/attend_0/pallas_call | solution.py:185
  63.5 9.2 %all-to-all-done.2.queries = bf16[16,48,1024]{2,1,0:T(8,128)(2,1)S(1)} async-done(((bf16[16,48,1024]{2,1,0:T(8,128)(2,1)}), bf16[16,48,1024]{2,1,0:T(8,128)(2,1)S(1)}, u32[]{:S(2)}, u32[]{:S(2)}) %all-to-all-start.2) | async-done | bytes 1572896 | tf_op jit(solution)/shard_map/all_to_all | solution.py:320
  72.7 3.8 %all-to-all-start.1 = ((bf16[16,16,1152]{2,1,0:T(8,128)(2,1)}), bf16[16,16,1152]{2,1,0:T(8,128)(2,1)S(1)}, u32[]{:S(2)}, u32[]{:S(2)}) async-start(bf16[16,16,1152]{2,1,0:T(8,128)(2,1)} %attend_0.1), calls=%async_computation.1 | async-start | bytes 1179648 | tf_op jit(solution)/shard_map/all_to_all | solution.py:326
  76.5 0.0 copy-start.12
  76.6 1.6 %copy-done.12 = bf16[1024,1024]{1,0:T(8,128)(2,1)S(1)} copy-done((bf16[1024,1024]{1,0:T(8,128)(2,1)S(1)}, bf16[1024,1024]{1,0:T(8,128)(2,1)}, u32[]{:S(2)}) %copy-start.12) | copy-done | bytes 2097176
  78.1 0.0 copy-start.15
  78.1 1.6 %copy-done.15 = bf16[1024,1024]{1,0:T(8,128)(2,1)S(1)} copy-done((bf16[1024,1024]{1,0:T(8,128)(2,1)S(1)}, bf16[1024,1024]{1,0:T(8,128)(2,1)}, u32[]{:S(2)}) %copy-start.15) | copy-done | bytes 2097176
  79.7 14.4 %attend_1.1 = bf16[16,32,1152]{2,1,0:T(8,128)(2,1)S(1)} custom-call(s32[1]{0:T(128)} %bitcast.flag, bf16[16,48,1024]{2,1,0:T(8,128)(2,1)S(1)} %all-to-all-done.2.queries, bf16[1024,1024]{1,0:T(8,128)(2,1)S(1)} %copy-done.12, bf16[1024,1024]{1,0:T(8,128)(2,1)S(1)} %copy-done.15), custom_call_target="tpu_custom_call" | custom-call | flops 8589934592 | bytes 8388608 | tf_op jit(solution)/shard_map/attend_1/pallas_call | solution.py:185
  94.2 0.0 copy-start.5
  94.2 1.0 copy-done.5
  95.2 7.3 %attend_3.1 = bf16[16,16,1152]{2,1,0:T(8,128)(2,1)S(1)} custom-call(s32[1]{0:T(128)} %bitcast.flag, bf16[16,48,1024]{2,1,0:T(8,128)(2,1)S(1)} %all-to-all-done.2.queries, bf16[1024,1024]{1,0:T(8,128)(2,1)S(1)} %copy-done.12, bf16[1024,1024]{1,0:T(8,128)(2,1)S(1)} %copy-done.15), custom_call_target="tpu_custom_call" | custom-call | flops 4294967296 | bytes 8388608 | tf_op jit(solution)/shard_map/attend_3/pallas_call | solution.py:185
  102.6 0.0 copy-start.3
  102.6 0.0 copy-start.7
  102.6 0.0 all-to-all-done.1.refs_0_
  102.6 17.5 %all_to_all.26.refs_2_ = bf16[16,16,1152]{2,1,0:T(8,128)(2,1)S(1)} all-to-all(bf16[16,16,1152]{2,1,0:T(8,128)(2,1)S(1)} %attend_3.1), channel_id=1, replica_groups=mesh['ctx'=8,'seq'=16] {'seq'}, dimensions={0} | all-to-all | bytes 1179648 | tf_op jit(solution)/shard_map/all_to_all | solution.py:326
  120.1 19.2 %all_to_all.27.refs_1_ = bf16[16,32,1152]{2,1,0:T(8,128)(2,1)S(1)} all-to-all(bf16[16,32,1152]{2,1,0:T(8,128)(2,1)} %copy-done.5), channel_id=1, replica_groups=mesh['ctx'=8,'seq'=16] {'seq'}, dimensions={0} | all-to-all | bytes 2359296 | tf_op jit(solution)/shard_map/all_to_all | solution.py:326
  139.3 0.0 copy-done.3
  139.3 0.0 copy-done.7
  139.3 2.1 %finish.1 = bf16[64,1024]{1,0:T(8,128)(2,1)} custom-call(bf16[16,16,1152]{2,1,0:T(8,128)(2,1)S(1)} %all-to-all-done.1.refs_0_, bf16[16,32,1152]{2,1,0:T(8,128)(2,1)S(1)} %all_to_all.27.refs_1_, bf16[16,16,1152]{2,1,0:T(8,128)(2,1)S(1)} %all_to_all.26.refs_2_, bf16[64,1024]{1,0:T(8,128)(2,1)S(1)} %get-tuple-element.48.refs_3_, f32[1,1024]{1,0:T(1,128)S(1)} %bitcast.5, ...), custom_call_target="tpu_custom_call" | custom-call | flops 268435456 | bytes 8388608 | tf_op jit(solution)/shard_map/finish/pallas_call | solution.py:246
Async XLA Ops:
  0.0 4.7 %copy-start.6 = (f32[1024]{0:T(1024)S(1)}, f32[1024]{0:T(1024)}, u32[]{:S(2)}) copy-start(f32[1024]{0:T(1024)} %param.8) | copy-start | bytes 12292
  0.0 1.6 %copy-start = (bf16[1024,1024]{1,0:T(8,128)(2,1)S(1)}, bf16[1024,1024]{1,0:T(8,128)(2,1)}, u32[]{:S(2)}) copy-start(bf16[1024,1024]{1,0:T(8,128)(2,1)} %tokens.3) | copy-start | bytes 6291460
  1.6 3.1 %copy-start.1 = (bf16[1024,1024]{1,0:T(8,128)(2,1)S(1)}, bf16[1024,1024]{1,0:T(8,128)(2,1)}, u32[]{:S(2)}) copy-start(bf16[1024,1024]{1,0:T(8,128)(2,1)} %tokens.3) | copy-start | bytes 6291460
  1.8 13.1 %collective-permute-start = (bf16[256,1024]{1,0:T(8,128)(2,1)S(1)}, bf16[256,1024]{1,0:T(8,128)(2,1)S(1)}, u32[]{:S(2)}, u32[]{:S(2)}) collective-permute-start(bf16[256,1024]{1,0:T(8,128)(2,1)S(1)} %get-tuple-element.28), channel_id=1, source_target_pairs={{15,3},{31,19},{47,35},{63,51},{79,67},{95,83},{111,99},{127,115}} | collective-permute-start | bytes 1572872 | tf_op jit(solution)/shard_map/ppermute | solution.py:292
  2.6 12.3 %collective-permute-start.1 = (bf16[256,1024]{1,0:T(8,128)(2,1)S(1)}, bf16[256,1024]{1,0:T(8,128)(2,1)S(1)}, u32[]{:S(2)}, u32[]{:S(2)}) collective-permute-start(bf16[256,1024]{1,0:T(8,128)(2,1)S(1)} %get-tuple-element.29), channel_id=1, source_target_pairs={{15,11},{31,27},{47,43},{63,59},{79,75},{95,91},{111,107},{127,123}} | collective-permute-start | bytes 1572872 | tf_op jit(solution)/shard_map/ppermute | solution.py:292
  3.3 11.6 %collective-permute-start.2 = (bf16[256,1024]{1,0:T(8,128)(2,1)S(1)}, bf16[256,1024]{1,0:T(8,128)(2,1)S(1)}, u32[]{:S(2)}, u32[]{:S(2)}) collective-permute-start(bf16[256,1024]{1,0:T(8,128)(2,1)S(1)} %get-tuple-element.30), channel_id=1, source_target_pairs={{15,12},{31,28},{47,44},{63,60},{79,76},{95,92},{111,108},{127,124}} | collective-permute-start | bytes 1572872 | tf_op jit(solution)/shard_map/ppermute | solution.py:292
  4.0 10.9 %collective-permute-start.3 = (bf16[256,1024]{1,0:T(8,128)(2,1)S(1)}, bf16[256,1024]{1,0:T(8,128)(2,1)S(1)}, u32[]{:S(2)}, u32[]{:S(2)}) collective-permute-start(bf16[256,1024]{1,0:T(8,128)(2,1)S(1)} %get-tuple-element.31), channel_id=1, source_target_pairs={{15,14},{31,30},{47,46},{63,62},{79,78},{95,94},{111,110},{127,126}} | collective-permute-start | bytes 1572872 | tf_op jit(solution)/shard_map/ppermute | solution.py:292
  4.7 1.6 %copy-start.8 = (bf16[1024,1024]{1,0:T(8,128)(2,1)S(1)}, bf16[1024,1024]{1,0:T(8,128)(2,1)}, u32[]{:S(2)}) copy-start(bf16[1024,1024]{1,0:T(8,128)(2,1)} %w_key.1) | copy-start | bytes 6291460
  6.3 1.6 %copy-start.9 = (bf16[1024,1024]{1,0:T(8,128)(2,1)S(1)}, bf16[1024,1024]{1,0:T(8,128)(2,1)}, u32[]{:S(2)}) copy-start(bf16[1024,1024]{1,0:T(8,128)(2,1)} %w_value.1) | copy-start | bytes 6291460
  14.8 13.2 %copy-start.10 = (bf16[1024,1024]{1,0:T(8,128)(2,1)}, bf16[1024,1024]{1,0:T(8,128)(2,1)S(1)}, u32[]{:S(2)}) copy-start(bf16[1024,1024]{1,0:T(8,128)(2,1)S(1)} %get-tuple-element.32.keys) | copy-start | bytes 6291460
  14.8 13.2 %copy-start.13 = (bf16[1024,1024]{1,0:T(8,128)(2,1)}, bf16[1024,1024]{1,0:T(8,128)(2,1)S(1)}, u32[]{:S(2)}) copy-start(bf16[1024,1024]{1,0:T(8,128)(2,1)S(1)} %get-tuple-element.44.values) | copy-start | bytes 6291460
  14.8 12.5 %copy-start.2 = (bf16[1024,1024]{1,0:T(8,128)(2,1)S(1)}, bf16[1024,1024]{1,0:T(8,128)(2,1)}, u32[]{:S(2)}) copy-start(bf16[1024,1024]{1,0:T(8,128)(2,1)} %w_query.1) | copy-start | bytes 6291460
  15.2 12.1 %collective-permute-start.4 = (bf16[64,1024]{1,0:T(8,128)(2,1)S(1)}, bf16[64,1024]{1,0:T(8,128)(2,1)S(1)}, u32[]{:S(2)}, u32[]{:S(2)}) collective-permute-start(bf16[64,1024]{1,0:T(8,128)(2,1)S(1)} %get-tuple-element.38), channel_id=1, source_target_pairs={{3,0},{11,8},{12,13},{14,6},{19,16},{27,24},{28,29},{30,22},{35,32... | collective-permute-start | bytes 393224 | tf_op jit(solution)/shard_map/ppermute | solution.py:305
  16.7 10.6 %collective-permute-start.5 = (bf16[64,1024]{1,0:T(8,128)(2,1)S(1)}, bf16[64,1024]{1,0:T(8,128)(2,1)S(1)}, u32[]{:S(2)}, u32[]{:S(2)}) collective-permute-start(bf16[64,1024]{1,0:T(8,128)(2,1)S(1)} %get-tuple-element.39), channel_id=1, source_target_pairs={{3,2},{11,10},{12,4},{14,7},{19,18},{27,26},{28,20},{30,23},{35,34... | collective-permute-start | bytes 393224 | tf_op jit(solution)/shard_map/ppermute | solution.py:305
  17.5 9.8 %collective-permute-start.6 = (bf16[64,1024]{1,0:T(8,128)(2,1)S(1)}, bf16[64,1024]{1,0:T(8,128)(2,1)S(1)}, u32[]{:S(2)}, u32[]{:S(2)}) collective-permute-start(bf16[64,1024]{1,0:T(8,128)(2,1)S(1)} %get-tuple-element.40), channel_id=1, source_target_pairs={{3,1},{11,9},{12,5},{19,17},{27,25},{28,21},{35,33},{43,41},{44,37... | collective-permute-start | bytes 393224 | tf_op jit(solution)/shard_map/ppermute | solution.py:305
  28.1 1.2 copy-start.4
  48.7 24.1 %all-to-all-start.2 = ((bf16[16,48,1024]{2,1,0:T(8,128)(2,1)}), bf16[16,48,1024]{2,1,0:T(8,128)(2,1)S(1)}, u32[]{:S(2)}, u32[]{:S(2)}) async-start(bf16[16,48,1024]{2,1,0:T(8,128)(2,1)} %copy-done.4), calls=%async_computation.2 | async-start | bytes 3145728 | tf_op jit(solution)/shard_map/all_to_all | solution.py:320
  52.4 1.6 %copy-start.11 = (bf16[1024,1024]{1,0:T(8,128)(2,1)S(1)}, bf16[1024,1024]{1,0:T(8,128)(2,1)}, u32[]{:S(2)}) copy-start(bf16[1024,1024]{1,0:T(8,128)(2,1)} %copy-done.10) | copy-start | bytes 6291460
  54.0 1.6 %copy-start.14 = (bf16[1024,1024]{1,0:T(8,128)(2,1)S(1)}, bf16[1024,1024]{1,0:T(8,128)(2,1)}, u32[]{:S(2)}) copy-start(bf16[1024,1024]{1,0:T(8,128)(2,1)} %copy-done.13) | copy-start | bytes 6291460
  72.7 29.8 %all-to-all-start.1 = ((bf16[16,16,1152]{2,1,0:T(8,128)(2,1)}), bf16[16,16,1152]{2,1,0:T(8,128)(2,1)S(1)}, u32[]{:S(2)}, u32[]{:S(2)}) async-start(bf16[16,16,1152]{2,1,0:T(8,128)(2,1)} %attend_0.1), calls=%async_computation.1 | async-start | bytes 1179648 | tf_op jit(solution)/shard_map/all_to_all | solution.py:326
  76.5 1.6 %copy-start.12 = (bf16[1024,1024]{1,0:T(8,128)(2,1)S(1)}, bf16[1024,1024]{1,0:T(8,128)(2,1)}, u32[]{:S(2)}) copy-start(bf16[1024,1024]{1,0:T(8,128)(2,1)} %copy-done.10) | copy-start | bytes 6291460
  78.1 1.6 %copy-start.15 = (bf16[1024,1024]{1,0:T(8,128)(2,1)S(1)}, bf16[1024,1024]{1,0:T(8,128)(2,1)}, u32[]{:S(2)}) copy-start(bf16[1024,1024]{1,0:T(8,128)(2,1)} %copy-done.13) | copy-start | bytes 6291460
  94.2 1.0 copy-start.5
  102.6 36.7 %copy-start.3 = (bf16[1024,1024]{1,0:T(8,128)(2,1)S(1)}, bf16[1024,1024]{1,0:T(8,128)(2,1)}, u32[]{:S(2)}) copy-start(bf16[1024,1024]{1,0:T(8,128)(2,1)} %refs_5_.1) | copy-start | bytes 6291460
  102.6 36.7 %copy-start.7 = (f32[1024]{0:T(1024)S(1)}, f32[1024]{0:T(1024)}, u32[]{:S(2)}) copy-start(f32[1024]{0:T(1024)} %param.9) | copy-start | bytes 12292

commit v3 on v0

v3 whole, which is shorter than its diff:
```python
import functools

import jax
import jax.numpy as jnp
from jax import lax
from jax.experimental import pallas as pl
from jax.experimental.pallas import tpu as pltpu
from jax.sharding import PartitionSpec as P

D = 1024
HEADS = 16
HEAD_DIM = 64
LATENTS = 1024
LOG2E = 1.4426950408889634
EXP2_SCALE = LOG2E * HEAD_DIM ** (-0.5)
MASKED = -1e30
MIB = 2**20
SMEM = pl.BlockSpec(memory_space=pltpu.SMEM)
VMEM = pl.BlockSpec(memory_space=pltpu.VMEM)

BUNDLES = ((3, 0, 2, 1), (11, 8, 10, 9), (12, 13, 4, 5), (14, 6, 7))


def limit(mib):
    return pltpu.CompilerParams(vmem_limit_bytes=mib * MIB)


def low_lanes():
    return lax.broadcasted_iota(jnp.int32, (1, 128), 1) < HEAD_DIM


def rms_rows(rows, gain):
    wide = rows.astype(jnp.float32)
    scale = lax.rsqrt(jnp.mean(wide * wide, axis=-1, keepdims=True) + 1e-06)
    return (wide * scale * gain).astype(jnp.bfloat16)


def kv_kernel(tokens, gain, w_key, w_value, out, normed):
    @pl.when(pl.program_id(0) == 0)
    def _():
        normed[...] = rms_rows(tokens[...], gain[...])

    rows = normed[...]
    keys = jnp.dot(rows, w_key[...], preferred_element_type=jnp.float32)
    values = jnp.dot(rows, w_value[...], preferred_element_type=jnp.float32)
    low = low_lanes()
    for pair in range(out.shape[0] // 2):
        at = slice(pair * 128, (pair + 1) * 128)
        key, value = keys[:, at], values[:, at]
        out[2 * pair] = jnp.where(low, key, pltpu.roll(value, HEAD_DIM, 1)).astype(jnp.bfloat16)
        out[2 * pair + 1] = jnp.where(low, pltpu.roll(key, HEAD_DIM, 1), value).astype(jnp.bfloat16)


def project_kv(tokens, part, parts, gain, w_key, w_value):
    rows = tokens.shape[0] // parts
    cols = 256
    heads = cols // HEAD_DIM
    return pl.pallas_call(
        kv_kernel,
        grid=(D // cols,),
        out_shape=jax.ShapeDtypeStruct((HEADS, rows, 128), jnp.bfloat16),
        in_specs=[
            pl.BlockSpec((rows, D), lambda c: (part, 0)),
            pl.BlockSpec((1, D), lambda c: (0, 0)),
            pl.BlockSpec((D, cols), lambda c: (0, c)),
            pl.BlockSpec((D, cols), lambda c: (0, c)),
        ],
        out_specs=pl.BlockSpec((heads, rows, 128), lambda c: (c, 0, 0)),
        scratch_shapes=[pltpu.VMEM((rows, D), jnp.bfloat16)],
        compiler_params=limit(56),
        cost_estimate=pl.CostEstimate(flops=4 * rows * D * D, bytes_accessed=4 * D * D, transcendentals=0),
        name="project_kv_%d" % part,
    )(tokens, gain, w_key, w_value)


def query_kernel(source, flag, tokens, gain, w_query, own, *bundles):
    queries = jnp.dot(
        rms_rows(tokens[...], gain[...]), w_query[...], preferred_element_type=jnp.float32
    )
    rows = queries.shape[0] // 2
    low = low_lanes()

    def head(number):
        at = slice(number // 2 * 128, (number // 2 + 1) * 128)
        first, second = queries[:rows, at], queries[rows:, at]
        if number % 2:
            first = pltpu.roll(first, HEAD_DIM, 1)
        else:
            second = pltpu.roll(second, HEAD_DIM, 1)
        return jnp.where(low, first, second).astype(jnp.bfloat16)

    mine = head(source)
    own[...] = jnp.where(flag[0] != 0, mine, jnp.zeros_like(mine))
    for members, bundle in zip(BUNDLES, bundles):
        for place in range(4):
            bundle[place] = head(members[min(place, len(members) - 1)])


def project_queries(flag, tokens, gain, w_query, source):
    rows = tokens.shape[0] // 2
    return pl.pallas_call(
        functools.partial(query_kernel, source),
        out_shape=(jax.ShapeDtypeStruct((rows, 128), jnp.bfloat16),)
        + (jax.ShapeDtypeStruct((4, rows, 128), jnp.bfloat16),) * 4,
        in_specs=[SMEM, VMEM, VMEM, VMEM],
        compiler_params=limit(56),
        cost_estimate=pl.CostEstimate(flops=4 * rows * D * D, bytes_accessed=8 * rows * D, transcendentals=0),
        name="project_queries",
    )(flag, tokens, gain, w_query)


def pack_kernel(source, flag, tokens, own, *bundles):
    rows = own.shape[0]

    def block(to):
        return tokens[to * rows : (to + 1) * rows, :]

    mine = block(source)
    own[...] = jnp.where(flag[0] != 0, mine, jnp.zeros_like(mine))
    for members, bundle in zip(BUNDLES, bundles):
        for place in range(4):
            bundle[place] = block(members[min(place, len(members) - 1)])


def pack_rows(flag, tokens, owned, source):
    return pl.pallas_call(
        functools.partial(pack_kernel, source),
        out_shape=(jax.ShapeDtypeStruct((owned, D), jnp.bfloat16),)
        + (jax.ShapeDtypeStruct((4, owned, D), jnp.bfloat16),) * 4,
        in_specs=[SMEM, VMEM],
        compiler_params=limit(56),
        cost_estimate=pl.CostEstimate(flops=0, bytes_accessed=8 * D * D, transcendentals=0),
        name="pack_rows",
    )(flag, tokens)


def relay_kernel(*refs):
    bundles, outs = refs[:4], refs[4:]
    for place, out in enumerate(outs):
        total = bundles[0][place].astype(jnp.float32)
        for bundle in bundles[1:]:
            total = total + bundle[place].astype(jnp.float32)
        out[...] = total.astype(jnp.bfloat16)


def send_bundles(bundles, source):
    return [lax.ppermute(bundle, "seq", [(source, members[0])]) for members, bundle in zip(BUNDLES, bundles)]


def pass_on(own, bundles):
    kept, *passed = pl.pallas_call(
        relay_kernel,
        out_shape=(jax.ShapeDtypeStruct(own.shape, jnp.bfloat16),) * 4,
        compiler_params=limit(24),
        cost_estimate=pl.CostEstimate(flops=0, bytes_accessed=4 * D * D, transcendentals=0),
        name="relay",
    )(*bundles)
    parts = [own, kept]
    for place in range(1, 4):
        pairs = [(members[0], members[place]) for members in BUNDLES if place < len(members)]
        parts.append(lax.ppermute(passed[place - 1], "seq", pairs))
    return parts


def add_parts(parts):
    total = parts[0][...].astype(jnp.float32)
    for part in parts[1:]:
        total = total + part[...].astype(jnp.float32)
    return total


def attend_kernel(base, final, *refs):
    parts, refs = refs[:5], refs[5:]
    kv, refs = refs[0], refs[1:]
    if final:
        acc_in, run_in, out, *refs = refs
        s, p, top, alpha, queries, acc, run = refs[:3], *refs[3:]
    else:
        acc, run, *refs = refs
        s, p, top, alpha, queries = refs[:3], *refs[3:]
    devices, span, _ = kv.shape
    rows = parts[0].shape[0]
    count = 2 * span
    units = devices
    sub = 32
    quarters = 4
    low = low_lanes()

    def keys_of(unit):
        return kv[unit // 2 * 2 : unit // 2 * 2 + 2].reshape(count, 128)

    def score(unit, quarter):
        width = count // quarters
        at = slice(quarter * width, (quarter + 1) * width)
        s[unit % 3][:, at] = lax.dot_general(
            queries[unit % 2],
            keys_of(unit)[at],
            (((1,), (1,)), ((), ())),
            preferred_element_type=jnp.float32,
        )

    def blocks(unit, quarter):
        height = rows // quarters
        for begin in range(quarter * height, (quarter + 1) * height, sub):
            free = some = count
            if unit // 2 * 2 + 2 == devices:
                row = unit % 2 * rows + begin - base
                free = span + min(span, max(0, (row + 1) // 128 * 128))
                some = span + min(span, max(0, -(-(row + sub) // 128) * 128))
            yield slice(begin, begin + sub), free, some

    def edge(unit, begin, free, some, block):
        row = unit % 2 * rows + begin - base + lax.broadcasted_iota(jnp.int32, (sub, some - free), 0)
        key = free - span + lax.broadcasted_iota(jnp.int32, (sub, some - free), 1)
        return jnp.where(key <= row, block, MASKED)

    def peak(unit, quarter):
        for at, free, some in blocks(unit, quarter):
            most = jnp.max(s[unit % 3][at, 0:free], axis=-1, keepdims=True)
            if some > free:
                block = edge(unit, at.start, free, some, s[unit % 3][at, free:some])
                most = jnp.maximum(most, jnp.max(block, axis=-1, keepdims=True))
            before = run[unit % 2, at, :]
            most = jnp.maximum(before, most)
            alpha[unit % 3, at, :] = jnp.exp2((before - most) * EXP2_SCALE)
            run[unit % 2, at, :] = most
            top[unit % 2, at, :] = most

    def soften(unit, quarter):
        for at, free, some in blocks(unit, quarter):
            most = top[unit % 2, at, 0:1]
            block = s[unit % 3][at, 0:free]
            p[unit % 2, at, 0:free] = jnp.exp2((block - most) * EXP2_SCALE).astype(jnp.bfloat16)
            if some > free:
                block = edge(unit, at.start, free, some, s[unit % 3][at, free:some])
                p[unit % 2, at, free:some] = jnp.exp2((block - most) * EXP2_SCALE).astype(jnp.bfloat16)
            if count > some:
                p[unit % 2, at, some:count] = jnp.zeros((sub, count - some), jnp.bfloat16)

    def blend(unit, half):
        height = rows // 2
        at = slice(half * height, (half + 1) * height)
        ones = jnp.ones((count, 128), jnp.bfloat16)
        mixed = jnp.dot(
            p[unit % 2, at, :],
            jnp.concatenate([keys_of(unit), ones], axis=1),
            preferred_element_type=jnp.float32,
        )
        scale = alpha[unit % 3, at, :]
        acc[unit % 2, at, 0:128] = acc[unit % 2, at, 0:128] * scale + mixed[:, 0:128]
        acc[unit % 2, at, 128:256] = acc[unit % 2, at, 128:256] * scale + mixed[:, 128:256]

    both = add_parts(parts)
    none = jnp.zeros_like(both)
    queries[0] = jnp.where(low, both, none).astype(jnp.bfloat16)
    queries[1] = jnp.where(low, pltpu.roll(both, HEAD_DIM, 1), none).astype(jnp.bfloat16)
    if final:
        acc[...] = acc_in[...]
        run[...] = run_in[...]
    else:
        acc[...] = jnp.zeros_like(acc)
        run[...] = jnp.full(run.shape, MASKED, jnp.float32)
    for turn in range(units + 3):
        for quarter in range(quarters):
            if turn < units:
                score(turn, quarter)
            if 0 <= turn - 3 and quarter % 2 == 0:
                blend(turn - 3, quarter // 2)
            if 0 <= turn - 2 < units:
                soften(turn - 2, quarter)
            if 0 <= turn - 1 < units:
                peak(turn - 1, quarter)
    if final:
        for half in range(2):
            at = slice(half * rows, (half + 1) * rows)
            out[at, :] = (acc[half, :, 0:128] / acc[half, :, 128:256]).astype(jnp.bfloat16)


def attend(base, parts, kv, state=None):
    devices, span, _ = kv.shape
    rows = parts[0].shape[0]
    final = state is not None
    acc = (2, rows, 256)
    run = (2, rows, 128)
    shapes = (jax.ShapeDtypeStruct(acc, jnp.float32), jax.ShapeDtypeStruct(run, jnp.float32))
    return pl.pallas_call(
        functools.partial(attend_kernel, base, final),
        out_shape=jax.ShapeDtypeStruct((2 * rows, 128), jnp.bfloat16) if final else shapes,
        scratch_shapes=[pltpu.VMEM((rows, 2 * span), jnp.float32)] * 3
        + [
            pltpu.VMEM((2, rows, 2 * span), jnp.bfloat16),
            pltpu.VMEM(run, jnp.float32),
            pltpu.VMEM((3, rows, 128), jnp.float32),
            pltpu.VMEM((2, rows, 128), jnp.bfloat16),
        ]
        + ([pltpu.VMEM(acc, jnp.float32), pltpu.VMEM(run, jnp.float32)] if final else []),
        compiler_params=limit(56),
        cost_estimate=pl.CostEstimate(
            flops=4 * 256 * 2 * rows * devices * span,
            bytes_accessed=4 * D * D,
            transcendentals=2 * rows * devices * span,
        ),
        name="attend_%d" % base,
    )(*parts, kv, *(state or ()))


def finish_kernel(heads, *refs):
    parts, (gain, w_out, out) = refs[:5], refs[5:]
    low = low_lanes()
    pairs = []
    for pair in range(HEADS // 2):
        even, odd = heads[2 * pair].astype(jnp.float32), heads[2 * pair + 1].astype(jnp.float32)
        pairs.append(jnp.where(low, pltpu.roll(even, HEAD_DIM, 1), odd))
    attended = jnp.concatenate(pairs, axis=1).astype(jnp.bfloat16)
    post = rms_rows(attended, gain[...])
    mixed = add_parts(parts) + jnp.dot(post, w_out[...], preferred_element_type=jnp.float32)
    out[...] = mixed.astype(jnp.bfloat16)


def finish(heads, parts, gain, w_out):
    rows = heads.shape[1]
    return pl.pallas_call(
        finish_kernel,
        out_shape=jax.ShapeDtypeStruct((rows, D), jnp.bfloat16),
        compiler_params=limit(28),
        cost_estimate=pl.CostEstimate(flops=2 * rows * D * D, bytes_accessed=4 * D * D, transcendentals=0),
        name="finish",
    )(heads, *parts, gain, w_out)


def after(value, *others):
    return lax.optimization_barrier((value, others))[0]


def local(tokens, ln_gain, post_gain, w_query, w_key, w_value, w_out):
    count = lax.axis_size("seq")
    source = count - 1
    last = lax.axis_index("seq") == source
    flag = last.astype(jnp.int32).reshape(1)
    owned = LATENTS // count
    gain = ln_gain.reshape(1, D)
    exchange = lambda blocks: lax.all_to_all(blocks, "seq", 0, 0)

    kv_0 = project_kv(tokens, 0, 2, gain, w_key, w_value)
    sent_0 = exchange(kv_0)
    own, *bundles = project_queries(flag, after(tokens, kv_0), gain, w_query, source)
    came = send_bundles(bundles, source)
    kv_1 = project_kv(after(tokens, bundles), 1, 2, gain, w_key, w_value)
    queries = pass_on(own, after(came, kv_1))
    own, *bundles = pack_rows(flag, after(tokens, queries[1]), owned, source)
    came = send_bundles(bundles, source)
    sent_0, kv_1 = lax.optimization_barrier((sent_0, kv_1))
    sent_1 = exchange(kv_1)
    state = attend(0, queries, sent_0)
    rows = pass_on(own, after(came, state))
    mixed = attend(tokens.shape[0] // 2, queries, after(sent_1, state, rows[1]), state)
    heads = exchange(mixed.reshape(count, owned, 128))
    return finish(heads, rows, post_gain.reshape(1, D), w_out)


def solution(mesh):
    return jax.shard_map(
        local,
        mesh=mesh,
        in_specs=(P(("ctx", "seq"), None), P(), P(), P(), P(), P(), P()),
        out_specs=P(("ctx", "seq"), None),
        check_vma=False,
    )
```

time: 452 us -> 148 us (0.33)
  waiting for transfers between devices: 234 us -> 55.5 us
  matrix products: 92.1 us -> 0 us
  blocking collectives: 72.3 us -> 0 us
  Pallas kernels: 0 us -> 52.4 us
  starting transfers between devices: 0.09 us -> 34.7 us
  other arithmetic: 24.5 us -> 0 us
  between operations: 13.2 us -> 0.35 us
  local copies, waits for them, and re-layouts: 13.6 us -> 2.71 us
    unnamed x5 -> x0, waiting for transfers between devices: 137 us -> none
    psum x1 -> x0, waiting for transfers between devices: 97 us -> none  [spread(): return lax.psum(block, axis)]
    dot_general x36 -> x0, matrix products: 92.1 us -> none  [the longest x16 46.1 us: one_head(): jnp.dot(probs.astype(jnp.bfloat16), value_h, preferred_element_type=jnp.f...]
    pmax x1 -> x0, blocking collectives: 72.3 us -> none  [local(): top = lax.pmax(maxima.astype(jnp.bfloat16), 'seq').astype(maxima.dtype)]
    pallas_call x0 -> x9, Pallas kernels: none -> 52.4 us  [the longest x2 28 us: attend(): pl.pallas_call(functools.partial(attend_kernel, base, final), out_shape=j...]
    ppermute x0 -> x14, waiting for transfers between devices: none -> 38 us  [the longest x6 38 us: pass_on(): parts.append(lax.ppermute(passed[place - 1], 'seq', pairs))]
    all_to_all x0 -> x3, starting transfers between devices: none -> 23.8 us  [local(): exchange = lambda blocks: lax.all_to_all(blocks, 'seq', 0, 0)]
    reduce_sum x18 -> x0, other arithmetic: 18.9 us -> none  [the longest x16 16.5 us: one_head(): local_sum = jnp.sum(probs, axis=-1)]
  transfers between devices with their start and end apart: 3 -> 17, of which waited for: 3 -> 3; matrix products, arithmetic and copies ran while one was open for 4% -> 0% of each run, Pallas kernels for 0% -> 21%
where the time goes in v3:
time: 148 us; the launch traced here: 146 us
  waiting for transfers between devices  55.5 us (38%)
  Pallas kernels  52.4 us (35%)
  starting transfers between devices  34.7 us (23%)
  local copies, waits for them, and re-layouts  2.71 us (2%)
    ppermute x6, waiting for transfers between devices, pass_on(): parts.append(lax.ppermute(passed[place - 1], 'seq', pairs))  38 us
    pallas_call x2, Pallas kernels, attend(): pl.pallas_call(functools.partial(attend_kernel, base, final), out_shape=j...  28 us
    all_to_all x3, starting transfers between devices, local(): exchange = lambda blocks: lax.all_to_all(blocks, 'seq', 0, 0)  23.8 us
    all_to_all x3, waiting for transfers between devices, local(): exchange = lambda blocks: lax.all_to_all(blocks, 'seq', 0, 0)  17.5 us
    pallas_call x2, Pallas kernels, project_kv(): pl.pallas_call(kv_kernel, grid=(D // cols,), out_shape=jax.ShapeDtypeStru...  13.3 us
    pallas_call x1, Pallas kernels, project_queries(): pl.pallas_call(functools.partial(query_kernel, source), out_shape=(jax.Sh...  6.24 us
    ppermute x8, starting transfers between devices, send_bundles(): lax.ppermute(bundle, 'seq', [(source, members[0])])  5.71 us
    ppermute x6, starting transfers between devices, pass_on(): parts.append(lax.ppermute(passed[place - 1], 'seq', pairs))  5.25 us
  transfers between devices with their start and end apart: 17, of which 3 were waited for; matrix products, arithmetic and copies ran while one was open for 0% of the time, Pallas kernels for 21%

profile of v3, /device:TPU:0, one launch (start us, length us, event | category | flops | bytes accessed | tf_op | source)
XLA Modules:
  0.0 145.7 jit_solution(9495702902579656952)
XLA Ops:
  0.0 6.6 %project_kv_0.1 = bf16[16,512,128]{2,1,0:T(8,128)(2,1)} custom-call(bf16[1024,1024]{1,0:T(8,128)(2,1)} %tokens.4, f32[1,1024]{1,0:T(1,128)} %bitcast.6, bf16[1024,1024]{1,0:T(8,128)(2,1)} %w_key.3, bf16[1024,1024]{1,0:T(8,128)(2,1)} %w_value.3), custom_call_target="tpu_custom_call" | custom-call | flops 2147483648 | bytes 4194304 | tf_op jit(solution)/shard_map/project_kv_0/pallas_call | solution.py:58
  6.6 8.0 %all-to-all-start = ((bf16[16,512,128]{2,1,0:T(8,128)(2,1)}), bf16[16,512,128]{2,1,0:T(8,128)(2,1)S(1)}, u32[]{:S(2)}, u32[]{:S(2)}) async-start(bf16[16,512,128]{2,1,0:T(8,128)(2,1)} %project_kv_0.1), calls=%async_computation | async-start | bytes 4194304 | tf_op jit(solution)/shard_map/all_to_all | solution.py:342
  14.6 6.2 %project_queries.1 = (bf16[512,128]{1,0:T(8,128)(2,1)}, bf16[4,512,128]{2,1,0:T(8,128)(2,1)}, bf16[4,512,128]{2,1,0:T(8,128)(2,1)}, bf16[4,512,128]{2,1,0:T(8,128)(2,1)}, bf16[4,512,128]{2,1,0:T(8,128)(2,1)}) custom-call(s32[1]{0:T(128)} %bitcast.flag, bf16[1024,1024]{1,0:T(8,128)(2,1)} %tokens.4, f32[1,1024]{1,0:T(1,128)} %bitcast.7, bf16[1024,1024]{1,0:T(8,128)(2,1)} %w_query.1), custom_call_target="tpu_custom_call" | custom-call | flops 2147483648 | bytes 4194304 | tf_op jit(solution)/shard_map/project_queries/pallas_call | solution.py:101
  20.9 6.6 %project_kv_1.1 = bf16[16,512,128]{2,1,0:T(8,128)(2,1)} custom-call(bf16[1024,1024]{1,0:T(8,128)(2,1)} %tokens.4, f32[1,1024]{1,0:T(1,128)} %bitcast.8, bf16[1024,1024]{1,0:T(8,128)(2,1)} %w_key.3, bf16[1024,1024]{1,0:T(8,128)(2,1)} %w_value.3), custom_call_target="tpu_custom_call" | custom-call | flops 2147483648 | bytes 4194304 | tf_op jit(solution)/shard_map/project_kv_1/pallas_call | solution.py:58
  27.5 0.0 copy-start.6
  27.5 0.0 copy-start.5
  27.5 17.5 %all-to-all-done.refs_5_ = bf16[16,512,128]{2,1,0:T(8,128)(2,1)S(1)} async-done(((bf16[16,512,128]{2,1,0:T(8,128)(2,1)}), bf16[16,512,128]{2,1,0:T(8,128)(2,1)S(1)}, u32[]{:S(2)}, u32[]{:S(2)}) %all-to-all-start) | async-done | bytes 2097184 | tf_op jit(solution)/shard_map/all_to_all | solution.py:342
  45.0 0.0 copy-start.4
  45.0 1.4 copy-done.4
  46.4 4.4 %all-to-all-start.1 = ((bf16[16,512,128]{2,1,0:T(8,128)(2,1)}), bf16[16,512,128]{2,1,0:T(8,128)(2,1)}, u32[]{:S(2)}, u32[]{:S(2)}) async-start(bf16[16,512,128]{2,1,0:T(8,128)(2,1)} %project_kv_1.1), calls=%async_computation.1 | async-start | bytes 4194304 | tf_op jit(solution)/shard_map/all_to_all | solution.py:342
  50.8 0.7 collective-permute-start
  51.5 0.7 collective-permute-start.1
  52.2 0.0 copy-done.6
  52.2 0.7 collective-permute-start.2
  52.9 0.0 copy-done.5
  52.9 0.7 collective-permute-start.3
  53.6 0.0 collective-permute-done.refs_0_
  53.7 0.0 collective-permute-done.1.refs_1_
  53.7 0.0 collective-permute-done.2.refs_2_
  53.7 0.0 collective-permute-done.3.refs_3_
  53.7 0.3 relay.2
  54.0 0.0 copy-start.3
  54.0 0.7 copy-done.3
  54.6 1.3 collective-permute-start.4
  55.9 0.7 collective-permute-start.5
  56.6 0.7 collective-permute-start.6
  57.3 3.0 %pack_rows.1 = (bf16[64,1024]{1,0:T(8,128)(2,1)}, bf16[4,64,1024]{2,1,0:T(8,128)(2,1)}, bf16[4,64,1024]{2,1,0:T(8,128)(2,1)}, bf16[4,64,1024]{2,1,0:T(8,128)(2,1)}, bf16[4,64,1024]{2,1,0:T(8,128)(2,1)}) custom-call(s32[1]{0:T(128)} %bitcast.flag, bf16[1024,1024]{1,0:T(8,128)(2,1)} %tokens.4), custom_call_target="tpu_custom_call" | custom-call | bytes 8388608 | tf_op jit(solution)/shard_map/pack_rows/pallas_call | solution.py:126
  60.3 0.7 collective-permute-start.7
  61.0 0.7 collective-permute-start.8
  61.7 31.7 %collective-permute-done.4.refs_2_ = bf16[512,128]{1,0:T(8,128)(2,1)S(1)} collective-permute-done((bf16[512,128]{1,0:T(8,128)(2,1)S(1)}, bf16[512,128]{1,0:T(8,128)(2,1)S(1)}, u32[]{:S(2)}, u32[]{:S(2)}) %collective-permute-start.4) | collective-permute-done | bytes 131104 | tf_op jit(solution)/shard_map/ppermute | solution.py:161
  93.4 0.0 copy-start.7
  93.4 0.7 collective-permute-start.9
  94.1 0.0 collective-permute-done.5.refs_3_
  94.1 0.0 copy-start.8
  94.1 0.9 collective-permute-start.10
  95.0 0.0 collective-permute-done.6.refs_4_
  95.0 0.0 copy-start.9
  95.0 0.0 copy-done.7
  95.0 0.0 copy-done.8
  95.0 0.6 copy-done.9
  95.7 13.8 %attend_0.1 = (f32[2,512,256]{2,1,0:T(8,128)}, f32[2,512,128]{2,1,0:T(8,128)}) custom-call(bf16[512,128]{1,0:T(8,128)(2,1)} %get-tuple-element.40.refs_0_, bf16[512,128]{1,0:T(8,128)(2,1)} %copy-done.3, bf16[512,128]{1,0:T(8,128)(2,1)} %copy-done.7, bf16[512,128]{1,0:T(8,128)(2,1)} %copy-done.8, bf16[512,128]{1,0:T(8,128)(2,1)} %copy-done.9, ...), custom_call_target="tpu_custom_call" | custom-call | flops 8589934592 | bytes 4194304 | tf_op jit(solution)/shard_map/attend_0/pallas_call | solution.py:286
  109.4 0.0 collective-permute-done.7.refs_0_
  109.4 0.0 collective-permute-done.8.refs_1_
  109.4 0.0 collective-permute-done.9.refs_2_
  109.5 0.0 collective-permute-done.10.refs_3_
  109.5 0.3 relay.3
  109.7 0.0 all-to-all-done.1.refs_5_
  109.7 0.0 copy-start
  109.8 0.0 copy-start.1
  109.8 0.0 copy-start.2
  109.8 14.3 %attend_512.1 = bf16[1024,128]{1,0:T(8,128)(2,1)} custom-call(bf16[512,128]{1,0:T(8,128)(2,1)} %get-tuple-element.40.refs_0_, bf16[512,128]{1,0:T(8,128)(2,1)} %copy-done.3, bf16[512,128]{1,0:T(8,128)(2,1)} %copy-done.7, bf16[512,128]{1,0:T(8,128)(2,1)} %copy-done.8, bf16[512,128]{1,0:T(8,128)(2,1)} %copy-done.9, ...), custom_call_target="tpu_custom_call" | custom-call | flops 8589934592 | bytes 4194304 | tf_op jit(solution)/shard_map/attend_512/pallas_call | solution.py:286
  124.0 11.3 %all-to-all-start.2 = ((bf16[16,64,128]{2,1,0:T(8,128)(2,1)}), bf16[16,64,128]{2,1,0:T(8,128)(2,1)S(1)}, u32[]{:S(2)}, u32[]{:S(2)}) async-start(bf16[16,64,128]{2,1,0:T(8,128)(2,1)} %bitcast.5), calls=%async_computation.2 | async-start | bytes 524288 | tf_op jit(solution)/shard_map/all_to_all | solution.py:342
  135.4 1.3 collective-permute-start.11
  136.7 0.7 collective-permute-start.12
  137.4 0.7 collective-permute-start.13
  138.0 6.3 %collective-permute-done.11.refs_2_ = bf16[64,1024]{1,0:T(8,128)(2,1)S(1)} collective-permute-done((bf16[64,1024]{1,0:T(8,128)(2,1)S(1)}, bf16[64,1024]{1,0:T(8,128)(2,1)S(1)}, u32[]{:S(2)}, u32[]{:S(2)}) %collective-permute-start.11) | collective-permute-done | bytes 131104 | tf_op jit(solution)/shard_map/ppermute | solution.py:161
  144.3 0.0 collective-permute-done.12.refs_3_
  144.3 0.0 collective-permute-done.13.refs_4_
  144.3 0.0 all-to-all-done.2.heads
  144.3 0.0 copy-done
  144.3 0.0 copy-done.1
  144.4 0.0 copy-done.2
  144.4 1.3 finish.1
Async XLA Ops:
  6.6 38.4 %all-to-all-start = ((bf16[16,512,128]{2,1,0:T(8,128)(2,1)}), bf16[16,512,128]{2,1,0:T(8,128)(2,1)S(1)}, u32[]{:S(2)}, u32[]{:S(2)}) async-start(bf16[16,512,128]{2,1,0:T(8,128)(2,1)} %project_kv_0.1), calls=%async_computation | async-start | bytes 4194304 | tf_op jit(solution)/shard_map/all_to_all | solution.py:342
  27.5 24.7 %copy-start.6 = (bf16[4,512,128]{2,1,0:T(8,128)(2,1)S(1)}, bf16[4,512,128]{2,1,0:T(8,128)(2,1)}, u32[]{:S(2)}) copy-start(bf16[4,512,128]{2,1,0:T(8,128)(2,1)} %get-tuple-element.43) | copy-start | bytes 1572868
  27.5 25.4 %copy-start.5 = (bf16[4,512,128]{2,1,0:T(8,128)(2,1)S(1)}, bf16[4,512,128]{2,1,0:T(8,128)(2,1)}, u32[]{:S(2)}) copy-start(bf16[4,512,128]{2,1,0:T(8,128)(2,1)} %get-tuple-element.44) | copy-start | bytes 1572868
  45.0 1.4 copy-start.4
  46.4 63.4 %all-to-all-start.1 = ((bf16[16,512,128]{2,1,0:T(8,128)(2,1)}), bf16[16,512,128]{2,1,0:T(8,128)(2,1)}, u32[]{:S(2)}, u32[]{:S(2)}) async-start(bf16[16,512,128]{2,1,0:T(8,128)(2,1)} %project_kv_1.1), calls=%async_computation.1 | async-start | bytes 4194304 | tf_op jit(solution)/shard_map/all_to_all | solution.py:342
  50.8 2.8 %collective-permute-start = (bf16[4,512,128]{2,1,0:T(8,128)(2,1)}, bf16[4,512,128]{2,1,0:T(8,128)(2,1)S(1)}, u32[]{:S(2)}, u32[]{:S(2)}) collective-permute-start(bf16[4,512,128]{2,1,0:T(8,128)(2,1)} %get-tuple-element.41), channel_id=1, source_target_pairs={{15,3},{31,19},{47,35},{63,51},{79,67},{95,83},{111,99},{127,115}} | collective-permute-start | bytes 1572872 | tf_op jit(solution)/shard_map/ppermute | solution.py:147
  51.5 2.1 %collective-permute-start.1 = (bf16[4,512,128]{2,1,0:T(8,128)(2,1)}, bf16[4,512,128]{2,1,0:T(8,128)(2,1)S(1)}, u32[]{:S(2)}, u32[]{:S(2)}) collective-permute-start(bf16[4,512,128]{2,1,0:T(8,128)(2,1)} %get-tuple-element.42), channel_id=1, source_target_pairs={{15,11},{31,27},{47,43},{63,59},{79,75},{95,91},{111,107},{127,123}} | collective-permute-start | bytes 1572872 | tf_op jit(solution)/shard_map/ppermute | solution.py:147
  52.2 1.4 collective-permute-start.2
  52.9 0.7 collective-permute-start.3
  54.0 0.7 copy-start.3
  54.6 38.8 %collective-permute-start.4 = (bf16[512,128]{1,0:T(8,128)(2,1)S(1)}, bf16[512,128]{1,0:T(8,128)(2,1)S(1)}, u32[]{:S(2)}, u32[]{:S(2)}) collective-permute-start(bf16[512,128]{1,0:T(8,128)(2,1)S(1)} %get-tuple-element.51), channel_id=1, source_target_pairs={{3,0},{11,8},{12,13},{14,6},{19,16},{27,24},{28,29},{30,22},{35,32... | collective-permute-start | bytes 393224 | tf_op jit(solution)/shard_map/ppermute | solution.py:161
  55.9 38.2 %collective-permute-start.5 = (bf16[512,128]{1,0:T(8,128)(2,1)S(1)}, bf16[512,128]{1,0:T(8,128)(2,1)S(1)}, u32[]{:S(2)}, u32[]{:S(2)}) collective-permute-start(bf16[512,128]{1,0:T(8,128)(2,1)S(1)} %get-tuple-element.52), channel_id=1, source_target_pairs={{3,2},{11,10},{12,4},{14,7},{19,18},{27,26},{28,20},{30,23},{35,34... | collective-permute-start | bytes 393224 | tf_op jit(solution)/shard_map/ppermute | solution.py:161
  56.6 38.4 %collective-permute-start.6 = (bf16[512,128]{1,0:T(8,128)(2,1)S(1)}, bf16[512,128]{1,0:T(8,128)(2,1)S(1)}, u32[]{:S(2)}, u32[]{:S(2)}) collective-permute-start(bf16[512,128]{1,0:T(8,128)(2,1)S(1)} %get-tuple-element.53), channel_id=1, source_target_pairs={{3,1},{11,9},{12,5},{19,17},{27,25},{28,21},{35,33},{43,41},{44,37... | collective-permute-start | bytes 393224 | tf_op jit(solution)/shard_map/ppermute | solution.py:161
  60.3 49.1 %collective-permute-start.7 = (bf16[4,64,1024]{2,1,0:T(8,128)(2,1)}, bf16[4,64,1024]{2,1,0:T(8,128)(2,1)S(1)}, u32[]{:S(2)}, u32[]{:S(2)}) collective-permute-start(bf16[4,64,1024]{2,1,0:T(8,128)(2,1)} %get-tuple-element.59), channel_id=1, source_target_pairs={{15,3},{31,19},{47,35},{63,51},{79,67},{95,83},{111,99},{127,115}} | collective-permute-start | bytes 1572872 | tf_op jit(solution)/shard_map/ppermute | solution.py:147
  61.0 48.4 %collective-permute-start.8 = (bf16[4,64,1024]{2,1,0:T(8,128)(2,1)}, bf16[4,64,1024]{2,1,0:T(8,128)(2,1)S(1)}, u32[]{:S(2)}, u32[]{:S(2)}) collective-permute-start(bf16[4,64,1024]{2,1,0:T(8,128)(2,1)} %get-tuple-element.60), channel_id=1, source_target_pairs={{15,11},{31,27},{47,43},{63,59},{79,75},{95,91},{111,107},{127,123}} | collective-permute-start | bytes 1572872 | tf_op jit(solution)/shard_map/ppermute | solution.py:147
  93.4 1.6 %copy-start.7 = (bf16[512,128]{1,0:T(8,128)(2,1)}, bf16[512,128]{1,0:T(8,128)(2,1)S(1)}, u32[]{:S(2)}) copy-start(bf16[512,128]{1,0:T(8,128)(2,1)S(1)} %collective-permute-done.4.refs_2_) | copy-start | bytes 393220
  93.4 16.0 %collective-permute-start.9 = (bf16[4,64,1024]{2,1,0:T(8,128)(2,1)}, bf16[4,64,1024]{2,1,0:T(8,128)(2,1)S(1)}, u32[]{:S(2)}, u32[]{:S(2)}) collective-permute-start(bf16[4,64,1024]{2,1,0:T(8,128)(2,1)} %get-tuple-element.61), channel_id=1, source_target_pairs={{15,12},{31,28},{47,44},{63,60},{79,76},{95,92},{111,108},{127,124}} | collective-permute-start | bytes 1572872 | tf_op jit(solution)/shard_map/ppermute | solution.py:147
  94.1 0.9 copy-start.8
  94.1 15.3 %collective-permute-start.10 = (bf16[4,64,1024]{2,1,0:T(8,128)(2,1)}, bf16[4,64,1024]{2,1,0:T(8,128)(2,1)S(1)}, u32[]{:S(2)}, u32[]{:S(2)}) collective-permute-start(bf16[4,64,1024]{2,1,0:T(8,128)(2,1)} %get-tuple-element.62), channel_id=1, source_target_pairs={{15,14},{31,30},{47,46},{63,62},{79,78},{95,94},{111,110},{127,126}} | collective-permute-start | bytes 1572872 | tf_op jit(solution)/shard_map/ppermute | solution.py:147
  95.0 0.7 copy-start.9
  109.7 34.6 %copy-start = (bf16[1024,1024]{1,0:T(8,128)(2,1)S(1)}, bf16[1024,1024]{1,0:T(8,128)(2,1)}, u32[]{:S(2)}) copy-start(bf16[1024,1024]{1,0:T(8,128)(2,1)} %refs_6_.1) | copy-start | bytes 6291460
  109.8 34.6 %copy-start.1 = (bf16[64,1024]{1,0:T(8,128)(2,1)S(1)}, bf16[64,1024]{1,0:T(8,128)(2,1)}, u32[]{:S(2)}) copy-start(bf16[64,1024]{1,0:T(8,128)(2,1)} %get-tuple-element.69.refs_0_) | copy-start | bytes 393220
  109.8 34.6 %copy-start.2 = (f32[1024]{0:T(1024)S(1)}, f32[1024]{0:T(1024)}, u32[]{:S(2)}) copy-start(f32[1024]{0:T(1024)} %param.9) | copy-start | bytes 12292
  124.0 20.3 %all-to-all-start.2 = ((bf16[16,64,128]{2,1,0:T(8,128)(2,1)}), bf16[16,64,128]{2,1,0:T(8,128)(2,1)S(1)}, u32[]{:S(2)}, u32[]{:S(2)}) async-start(bf16[16,64,128]{2,1,0:T(8,128)(2,1)} %bitcast.5), calls=%async_computation.2 | async-start | bytes 524288 | tf_op jit(solution)/shard_map/all_to_all | solution.py:342
  135.4 8.9 %collective-permute-start.11 = (bf16[64,1024]{1,0:T(8,128)(2,1)S(1)}, bf16[64,1024]{1,0:T(8,128)(2,1)S(1)}, u32[]{:S(2)}, u32[]{:S(2)}) collective-permute-start(bf16[64,1024]{1,0:T(8,128)(2,1)S(1)} %get-tuple-element.70), channel_id=1, source_target_pairs={{3,0},{11,8},{12,13},{14,6},{19,16},{27,24},{28,29},{30,22},{35,32... | collective-permute-start | bytes 393224 | tf_op jit(solution)/shard_map/ppermute | solution.py:161
  136.7 7.7 %collective-permute-start.12 = (bf16[64,1024]{1,0:T(8,128)(2,1)S(1)}, bf16[64,1024]{1,0:T(8,128)(2,1)S(1)}, u32[]{:S(2)}, u32[]{:S(2)}) collective-permute-start(bf16[64,1024]{1,0:T(8,128)(2,1)S(1)} %get-tuple-element.71), channel_id=1, source_target_pairs={{3,2},{11,10},{12,4},{14,7},{19,18},{27,26},{28,20},{30,23},{35,34... | collective-permute-start | bytes 393224 | tf_op jit(solution)/shard_map/ppermute | solution.py:161
  137.4 7.0 %collective-permute-start.13 = (bf16[64,1024]{1,0:T(8,128)(2,1)S(1)}, bf16[64,1024]{1,0:T(8,128)(2,1)S(1)}, u32[]{:S(2)}, u32[]{:S(2)}) collective-permute-start(bf16[64,1024]{1,0:T(8,128)(2,1)S(1)} %get-tuple-element.72), channel_id=1, source_target_pairs={{3,1},{11,9},{12,5},{19,17},{27,25},{28,21},{35,33},{43,41},{44,37... | collective-permute-start | bytes 393224 | tf_op jit(solution)/shard_map/ppermute | solution.py:161

commit v4 on v2

--- a/solution.py
+++ b/solution.py
@@ -12,7 +12,7 @@
 HEAD_DIM = 64
 PAIRS = HEADS // 2
 LATENTS = 1024
-PART = 16
+PART = 32
 LOG2E = 1.4426950408889634
 EXP2_SCALE = LOG2E * HEAD_DIM ** (-0.5)
 MASKED = -1e30
@@ -55,7 +55,7 @@
         ],
         out_specs=(pl.BlockSpec((rows, cols), block),) * 2,
         scratch_shapes=[pltpu.VMEM((rows, D), jnp.bfloat16)],
-        compiler_params=pltpu.CompilerParams(vmem_limit_bytes=20 * MIB),
+        compiler_params=pltpu.CompilerParams(vmem_limit_bytes=56 * MIB),
         cost_estimate=pl.CostEstimate(flops=4 * rows * D * D, bytes_accessed=10 * rows * D, transcendentals=0),
         name="project_kv",
     )(tokens, gain, w_key, w_value)
@@ -91,124 +91,94 @@
     )(gain, w_query, *parts)
 
 
-def attend_kernel(first, owned, flag, queries, keys, values, out, s_a, s_b, p_a, p_b, top_a, top_b, lse):
-    group, part, _ = queries.shape
-    rows = group * part
+def attend_kernel(chunk, owned, flag, queries, keys, values, out):
+    rows = queries.shape[0]
     count = keys.shape[0]
-    offset = (first + pl.program_id(0)) * part
+    step = pl.program_id(0)
+    pairs = HEADS // 2
+    part = PART
     low = lax.broadcasted_iota(jnp.int32, (1, 128), 1) < HEAD_DIM
-    sub = 32
-
-    def score(pair, s):
-        at = pl.ds(pl.multiple_of(pair * 128, 128), 128)
-        query = queries[:, :, at].reshape(rows, 128)
-        none = jnp.zeros_like(query)
-        both = jnp.concatenate([jnp.where(low, query, none), jnp.where(low, none, query)], axis=0)
-        s[...] = lax.dot_general(
-            both, keys[:, at], (((1,), (1,)), ((), ())), preferred_element_type=jnp.float32
-        )
-
-    def soften(causal, s, p, top):
-        for begin in range(0, 2 * rows, sub):
-            at = slice(begin, begin + sub)
-            begin = begin % rows
-            span = count
-            if causal:
-                last = (begin + sub - 1) // part * owned + owned
-                span = min(count, -(-last // 128) * 128)
-            block = s[at, 0:span]
-            if causal:
-                row = begin + lax.broadcasted_iota(jnp.int32, (sub, span), 0)
-                query_pos = row // part * owned + offset + row % part
-                key_pos = lax.broadcasted_iota(jnp.int32, (sub, span), 1)
-                block = jnp.where(key_pos <= query_pos, block, MASKED)
-            most = jnp.max(block, axis=-1, keepdims=True)
-            p[at, 0:span] = jnp.exp2((block - most) * EXP2_SCALE).astype(jnp.bfloat16)
-            if span < count:
-                p[at, span:count] = jnp.zeros((sub, count - span), jnp.bfloat16)
-            top[at, :] = jnp.broadcast_to(most, (sub, 128))
-
-    def blend(pair, p, top):
-        at = pl.ds(pl.multiple_of(jnp.maximum(pair, 0) * 128, 128), 128)
+
+    def attention(causal, count):
+        lane = lax.broadcasted_iota(jnp.int32, (rows, 128), 1)
+        lse = jnp.zeros((rows, 128), jnp.float32)
         ones = jnp.ones((count, 128), jnp.bfloat16)
-        mixed = jnp.dot(
-            p[...], jnp.concatenate([values[:, at], ones], axis=1), preferred_element_type=jnp.float32
-        )
-        mix, total = mixed[:, 0:128], mixed[:, 128:256]
-        both = jnp.where(low, mix[:rows], mix[rows:]) / jnp.where(low, total[:rows], total[rows:])
-        out[:, :, at] = both.astype(jnp.bfloat16).reshape(group, part, 128)
-        level = top[...] * EXP2_SCALE + jnp.log2(total)
-        lane = lax.broadcasted_iota(jnp.int32, (rows, 128), 1)
-        held = jnp.where(lane == 2 * pair, level[:rows], lse[...])
-        lse[...] = jnp.where(lane == 2 * pair + 1, level[rows:], held)
-
-    def attention(causal):
-        score(0, s_a)
-        score(1, s_b)
-        soften(causal, s_a, p_a, top_a)
-
-        def two_pairs(i, _):
-            score(2 * i, s_a)
-            blend(2 * i - 2, p_a, top_a)
-            soften(causal, s_b, p_b, top_b)
-            score(2 * i + 1, s_b)
-            blend(2 * i - 1, p_b, top_b)
-            soften(causal, s_a, p_a, top_a)
-            return 0
-
-        lse[...] = jnp.zeros_like(lse)
-        lax.fori_loop(1, PAIRS // 2, two_pairs, 0)
-        blend(PAIRS - 2, p_a, top_a)
-        soften(causal, s_b, p_b, top_b)
-        blend(PAIRS - 1, p_b, top_b)
-        level = lse[...]
-        one = level.astype(jnp.bfloat16).astype(jnp.float32)
-        two = (level - one).astype(jnp.bfloat16).astype(jnp.float32)
-        three = level - one - two
-        pieces = one + pltpu.roll(two, HEADS, 1) + pltpu.roll(three, 2 * HEADS, 1)
-        out[:, :, D:WIDE] = pieces.astype(jnp.bfloat16).reshape(group, part, 128)
+        if causal:
+            key_pos = lax.broadcasted_iota(jnp.int32, (rows, count), 1)
+            row = step * rows + lax.broadcasted_iota(jnp.int32, (rows, count), 0)
+            query_pos = (row // part) * owned + chunk * part + row % part
+            allowed = key_pos <= query_pos
+            allowed = jnp.concatenate([allowed, allowed], axis=0)
+
+        def scores_of(pair):
+            at = slice(pair * 128, (pair + 1) * 128)
+            query = queries[:, at]
+            none = jnp.zeros_like(query)
+            both = jnp.concatenate([jnp.where(low, query, none), jnp.where(low, none, query)], axis=0)
+            scores = lax.dot_general(
+                both, keys[0:count, at], (((1,), (1,)), ((), ())), preferred_element_type=jnp.float32
+            )
+            return jnp.where(allowed, scores, MASKED) if causal else scores
+
+        ahead = scores_of(0)
+        for pair in range(pairs):
+            at = slice(pair * 128, (pair + 1) * 128)
+            scores = ahead
+            if pair + 1 < pairs:
+                ahead = scores_of(pair + 1)
+            top = jnp.max(scores, axis=-1, keepdims=True)
+            weights = jnp.exp2((scores - top) * EXP2_SCALE).astype(jnp.bfloat16)
+            mixed = jnp.dot(
+                weights,
+                jnp.concatenate([values[0:count, at], ones], axis=1),
+                preferred_element_type=jnp.float32,
+            )
+            mix, total = mixed[:, 0:128], mixed[:, 128:256]
+            both = jnp.where(low, mix[:rows], mix[rows:]) / jnp.where(low, total[:rows], total[rows:])
+            out[:, at] = both.astype(jnp.bfloat16)
+            level = top * EXP2_SCALE + jnp.log2(total)
+            lse = jnp.where(lane == 2 * pair, level[:rows], lse)
+            lse = jnp.where(lane == 2 * pair + 1, level[rows:], lse)
+        first = lse.astype(jnp.bfloat16).astype(jnp.float32)
+        second = (lse - first).astype(jnp.bfloat16).astype(jnp.float32)
+        third = lse - first - second
+        pieces = first + pltpu.roll(second, HEADS, 1) + pltpu.roll(third, 2 * HEADS, 1)
+        out[:, D:WIDE] = pieces.astype(jnp.bfloat16)
 
     @pl.when(flag[0] == 0)
     def _():
-        attention(False)
-
-    @pl.when(flag[0] != 0)
+        attention(False, count)
+
+    @pl.when(jnp.logical_and(flag[0] != 0, step == 0))
     def _():
-        attention(True)
-
-
-def attend(first, begin, steps, owned, is_last, queries, keys, values):
-    group = queries.shape[0]
-    rows = group * PART
-    count = keys.shape[0]
+        attention(True, rows // part * owned)
+
+    @pl.when(jnp.logical_and(flag[0] != 0, step != 0))
+    def _():
+        attention(True, count)
+
+
+def attend(chunk, owned, is_last, queries, keys, values):
+    count = queries.shape[0]
+    rows = 256
     whole = lambda c: (0, 0)
+    block = lambda c: (c, 0)
     return pl.pallas_call(
-        functools.partial(attend_kernel, first, owned),
-        grid=(steps,),
-        out_shape=jax.ShapeDtypeStruct((group, steps * PART, WIDE), jnp.bfloat16),
+        functools.partial(attend_kernel, chunk, owned),
+        grid=(count // rows,),
+        out_shape=jax.ShapeDtypeStruct((count, WIDE), jnp.bfloat16),
         in_specs=[
             pl.BlockSpec(memory_space=pltpu.SMEM),
-            pl.BlockSpec((group, PART, D), lambda c: (0, begin + c, 0)),
-            pl.BlockSpec((count, D), whole, pipeline_mode=pl.Buffered(1)),
-            pl.BlockSpec((count, D), whole, pipeline_mode=pl.Buffered(1)),
+            pl.BlockSpec((rows, D), block),
+            pl.BlockSpec(keys.shape, whole),
+            pl.BlockSpec(values.shape, whole),
         ],
-        out_specs=pl.BlockSpec((group, PART, WIDE), lambda c: (0, c, 0)),
-        scratch_shapes=[
-            pltpu.VMEM((2 * rows, count), jnp.float32),
-            pltpu.VMEM((2 * rows, count), jnp.float32),
-            pltpu.VMEM((2 * rows, count), jnp.bfloat16),
-            pltpu.VMEM((2 * rows, count), jnp.bfloat16),
-            pltpu.VMEM((2 * rows, 128), jnp.float32),
-            pltpu.VMEM((2 * rows, 128), jnp.float32),
-            pltpu.VMEM((rows, 128), jnp.float32),
-        ],
-        compiler_params=pltpu.CompilerParams(vmem_limit_bytes=28 * MIB),
+        out_specs=pl.BlockSpec((rows, WIDE), block),
+        compiler_params=pltpu.CompilerParams(vmem_limit_bytes=56 * MIB),
         cost_estimate=pl.CostEstimate(
-            flops=16 * steps * rows * D * D,
-            bytes_accessed=8 * D * D,
-            transcendentals=HEADS * steps * rows * D,
+            flops=16 * count * D * D, bytes_accessed=8 * D * D, transcendentals=HEADS * count * D
         ),
-        name="attend_%d" % first,
+        name="attend_%d" % chunk,
     )(is_last, queries, keys, values)
 
 
@@ -318,12 +288,10 @@
     rows_a = lax.all_to_all(tiled_a, "seq", 0, 0)
     rows_a, tiled_b = lax.optimization_barrier((rows_a, tiled_b))
     rows_b = lax.all_to_all(tiled_b, "seq", 0, 0)
-    mixed_a = attend(0, 0, 1, owned, flag, rows_a, keys, values)
+    mixed_a = attend(0, owned, flag, rows_a.reshape(-1, D), keys, values)
     rows_b, _ = lax.optimization_barrier((rows_b, mixed_a))
-    mixed_b = attend(1, 0, 2, owned, flag, rows_b, keys, values)
-    rows_c, _ = lax.optimization_barrier((rows_b, mixed_b))
-    mixed_c = attend(3, 2, 1, owned, flag, rows_c, keys, values)
-    mixed = [lax.all_to_all(each, "seq", 0, 0) for each in (mixed_a, mixed_b, mixed_c)]
+    mixed_b = attend(1, owned, flag, rows_b.reshape(-1, D), keys, values)
+    mixed = [lax.all_to_all(each.reshape(count, PART, WIDE), "seq", 0, 0) for each in (mixed_a, mixed_b)]
     return finish(mixed, own, post_gain.reshape(1, D), w_out)
 
 

time: 142 us -> 127 us (0.89); the launches traced: 141 us -> 129 us
  Pallas kernels: 39.8 us -> 54.6 us
  local copies, waits for them, and re-layouts: 13.3 us -> 1.61 us
  blocking collectives: 56.2 us -> 46.2 us
  waiting for transfers between devices: 18.3 us -> 10.2 us
  starting transfers between devices: 13.4 us -> 16.3 us
    all_to_all x2 -> x1, blocking collectives: 36.7 us -> 21.4 us  [local(): lax.all_to_all(each.reshape(count, PART, WIDE), 'seq', 0, 0)]
    unnamed x32 -> x12, local copies, waits for them, and re-layouts: 13.3 us -> 1.61 us
    pallas_call x3 -> x2, Pallas kernels: 29.7 us -> 41.2 us  [attend(): pl.pallas_call(functools.partial(attend_kernel, chunk, owned), grid=(coun...]
    all_to_all x1, waiting for transfers between devices: 9.23 us -> 0.01 us  [local(): rows_b = lax.all_to_all(tiled_b, 'seq', 0, 0)]
    all_to_all x1, blocking collectives: 19.5 us -> 24.8 us  [local(): rows_a = lax.all_to_all(tiled_a, 'seq', 0, 0)]
    all_to_all x1, starting transfers between devices: 3.79 us -> 7.14 us  [local(): lax.all_to_all(each.reshape(count, PART, WIDE), 'seq', 0, 0)]
    pallas_call x1, Pallas kernels: 6.9 us -> 9.27 us  [project_kv(): pl.pallas_call(kv_kernel, grid=(D // cols,), out_shape=(jax.ShapeDtypeStr...]
  transfers between devices with their start and end apart: 9 -> 9, of which waited for: 2 -> 1; matrix products, arithmetic and copies ran while one was open for 0% -> 0% of each run, Pallas kernels for 26% -> 39%
where the time goes in v4:
time: 127 us; the launch traced here: 129 us
  Pallas kernels  54.6 us (43%)
  blocking collectives  46.2 us (36%)
  starting transfers between devices  16.3 us (13%)
  waiting for transfers between devices  10.2 us (8%)
  local copies, waits for them, and re-layouts  1.61 us (1%)
    pallas_call x2, Pallas kernels, attend(): pl.pallas_call(functools.partial(attend_kernel, chunk, owned), grid=(coun...  41.2 us
    all_to_all x1, blocking collectives, local(): rows_a = lax.all_to_all(tiled_a, 'seq', 0, 0)  24.8 us
    all_to_all x1, blocking collectives, local(): lax.all_to_all(each.reshape(count, PART, WIDE), 'seq', 0, 0)  21.4 us
    ppermute x3, waiting for transfers between devices, scatter(): parts.append(lax.ppermute(passed[place - 1], 'seq', pairs))  10.2 us
    pallas_call x1, Pallas kernels, project_kv(): pl.pallas_call(kv_kernel, grid=(D // cols,), out_shape=(jax.ShapeDtypeStr...  9.27 us
    all_to_all x1, starting transfers between devices, local(): lax.all_to_all(each.reshape(count, PART, WIDE), 'seq', 0, 0)  7.14 us
    all_to_all x1, starting transfers between devices, local(): rows_b = lax.all_to_all(tiled_b, 'seq', 0, 0)  3.65 us
    ppermute x4, starting transfers between devices, scatter(): lax.ppermute(bundle, 'seq', [(source, members[0])])  2.78 us
  transfers between devices with their start and end apart: 9, of which 1 were waited for; matrix products, arithmetic and copies ran while one was open for 0% of the time, Pallas kernels for 39%

profile of v4, /device:TPU:0, one launch (start us, length us, event | category | flops | bytes accessed | tf_op | source)
XLA Modules:
  0.0 129.3 jit_solution(13659802164417726755)
XLA Ops:
  0.0 0.0 copy-start
  0.0 1.6 %copy-done = bf16[1024,1024]{1,0:T(8,128)(2,1)S(1)} copy-done((bf16[1024,1024]{1,0:T(8,128)(2,1)S(1)}, bf16[1024,1024]{1,0:T(8,128)(2,1)}, u32[]{:S(2)}) %copy-start) | copy-done | bytes 2097176
  1.6 0.1 pack.1
  1.7 0.7 collective-permute-start
  2.4 0.7 collective-permute-start.1
  3.1 0.7 collective-permute-start.2
  3.9 0.7 collective-permute-start.3
  4.6 9.3 %project_kv.1 = (bf16[1024,1024]{1,0:T(8,128)(2,1)}, bf16[1024,1024]{1,0:T(8,128)(2,1)}) custom-call(bf16[1024,1024]{1,0:T(8,128)(2,1)} %tokens.3, f32[1,1024]{1,0:T(1,128)} %bitcast.7, bf16[1024,1024]{1,0:T(8,128)(2,1)} %w_key.1, bf16[1024,1024]{1,0:T(8,128)(2,1)} %w_value.1), custom_call_target="tpu_custom_call" | custom-call | flops 4294967296 | bytes 10485760 | tf_op jit(solution)/shard_map/project_kv/pallas_call | solution.py:46
  13.8 0.0 copy-start.1
  13.8 0.0 copy-start.3
  13.8 0.0 collective-permute-done.refs_0_
  13.8 0.0 collective-permute-done.1.refs_1_
  13.8 0.0 collective-permute-done.2.refs_2_
  13.9 0.0 collective-permute-done.3.refs_3_
  13.9 0.3 relay.1
  14.1 1.4 %collective-permute-start.4 = (bf16[64,1024]{1,0:T(8,128)(2,1)S(1)}, bf16[64,1024]{1,0:T(8,128)(2,1)S(1)}, u32[]{:S(2)}, u32[]{:S(2)}) collective-permute-start(bf16[64,1024]{1,0:T(8,128)(2,1)S(1)} %get-tuple-element.37), channel_id=1, source_target_pairs={{3,0},{11,8},{12,13},{14,6},{19,16},{27,24},{28,29},{30,22},{35,32... | collective-permute-start | bytes 393224 | tf_op jit(solution)/shard_map/ppermute | solution.py:275
  15.6 0.7 collective-permute-start.5
  16.2 0.7 collective-permute-start.6
  16.9 10.2 %collective-permute-done.4.refs_2_ = bf16[64,1024]{1,0:T(8,128)(2,1)S(1)} collective-permute-done((bf16[64,1024]{1,0:T(8,128)(2,1)S(1)}, bf16[64,1024]{1,0:T(8,128)(2,1)S(1)}, u32[]{:S(2)}, u32[]{:S(2)}) %collective-permute-start.4) | collective-permute-done | bytes 131104 | tf_op jit(solution)/shard_map/ppermute | solution.py:275
  27.1 0.0 collective-permute-done.5.refs_3_
  27.1 0.0 collective-permute-done.6.refs_4_
  27.1 0.0 copy-done.1
  27.1 0.0 copy-done.3
  27.2 1.7 %project_queries.1 = (bf16[64,1024]{1,0:T(8,128)(2,1)S(1)}, bf16[16,32,1024]{2,1,0:T(8,128)(2,1)S(1)}, bf16[16,32,1024]{2,1,0:T(8,128)(2,1)}) custom-call(f32[1,1024]{1,0:T(1,128)S(1)} %bitcast.8, bf16[1024,1024]{1,0:T(8,128)(2,1)S(1)} %copy-done.1, bf16[64,1024]{1,0:T(8,128)(2,1)S(1)} %get-tuple-element.26.refs_0_, ...), custom_call_target="tpu_custom_call" | custom-call | flops 134217728 | bytes 4194304 | tf_op jit(solution)/shard_map/project_queries/pallas_call | solution.py:84
  28.9 24.8 %all_to_all.20 = bf16[16,32,1024]{2,1,0:T(8,128)(2,1)} all-to-all(bf16[16,32,1024]{2,1,0:T(8,128)(2,1)S(1)} %get-tuple-element.40), channel_id=1, replica_groups=mesh['ctx'=8,'seq'=16] {'seq'}, dimensions={0} | all-to-all | bytes 2097152 | tf_op jit(solution)/shard_map/all_to_all | solution.py:288
  53.7 3.7 %all-to-all-start.2 = ((bf16[16,32,1024]{2,1,0:T(8,128)(2,1)}), bf16[16,32,1024]{2,1,0:T(8,128)(2,1)S(1)}, u32[]{:S(2)}, u32[]{:S(2)}) async-start(bf16[16,32,1024]{2,1,0:T(8,128)(2,1)} %get-tuple-element.44), calls=%async_computation.2 | async-start | bytes 2097152 | tf_op jit(solution)/shard_map/all_to_all | solution.py:290
  57.3 14.7 %attend_0.1 = bf16[512,1152]{1,0:T(8,128)(2,1)} custom-call(s32[1]{0:T(128)} %bitcast.flag, bf16[512,1024]{1,0:T(8,128)(2,1)} %bitcast.13, bf16[1024,1024]{1,0:T(8,128)(2,1)} %get-tuple-element.31.keys, bf16[1024,1024]{1,0:T(8,128)(2,1)} %get-tuple-element.43.values), custom_call_target="tpu_custom_call" | custom-call | flops 8589934592 | bytes 8388608 | tf_op jit(solution)/shard_map/attend_0/pallas_call | solution.py:166
  72.0 0.0 all-to-all-done.2
  72.0 0.0 copy-start.5
  72.0 7.1 %all-to-all-start.1 = ((bf16[16,32,1152]{2,1,0:T(8,128)(2,1)}), bf16[16,32,1152]{2,1,0:T(8,128)(2,1)S(1)}, u32[]{:S(2)}, u32[]{:S(2)}) async-start(bf16[16,32,1152]{2,1,0:T(8,128)(2,1)} %bitcast.10), calls=%async_computation.1 | async-start | bytes 2359296 | tf_op jit(solution)/shard_map/all_to_all | solution.py:294
  79.1 0.0 copy-done.5
  79.2 26.5 %attend_1.1 = bf16[512,1152]{1,0:T(8,128)(2,1)} custom-call(s32[1]{0:T(128)} %bitcast.flag, bf16[512,1024]{1,0:T(8,128)(2,1)} %bitcast.12, bf16[1024,1024]{1,0:T(8,128)(2,1)} %get-tuple-element.31.keys, bf16[1024,1024]{1,0:T(8,128)(2,1)} %get-tuple-element.43.values), custom_call_target="tpu_custom_call" | custom-call | flops 8589934592 | bytes 8388608 | tf_op jit(solution)/shard_map/attend_1/pallas_call | solution.py:166
  105.6 0.0 copy-start.2
  105.6 0.0 copy-start.4
  105.6 0.0 all-to-all-done.1.refs_0_
  105.6 21.4 %all_to_all.21.refs_1_ = bf16[16,32,1152]{2,1,0:T(8,128)(2,1)S(1)} all-to-all(bf16[16,32,1152]{2,1,0:T(8,128)(2,1)} %bitcast.11), channel_id=1, replica_groups=mesh['ctx'=8,'seq'=16] {'seq'}, dimensions={0} | all-to-all | bytes 2359296 | tf_op jit(solution)/shard_map/all_to_all | solution.py:294
  127.1 0.0 copy-done.2
  127.1 0.0 copy-done.4
  127.1 2.1 %finish.1 = bf16[64,1024]{1,0:T(8,128)(2,1)} custom-call(bf16[16,32,1152]{2,1,0:T(8,128)(2,1)S(1)} %all-to-all-done.1.refs_0_, bf16[16,32,1152]{2,1,0:T(8,128)(2,1)S(1)} %all_to_all.21.refs_1_, bf16[64,1024]{1,0:T(8,128)(2,1)S(1)} %get-tuple-element.46.refs_2_, f32[1,1024]{1,0:T(1,128)S(1)} %bitcast.9, bf16[1024,1024]{1,0:T(8,128)(2,1)S(1)} %copy-done.2), custom_call_target="tpu_custom_call" | custom-call | flops 268435456 | bytes 8388608 | tf_op jit(solution)/shard_map/finish/pallas_call | solution.py:216
Async XLA Ops:
  0.0 1.6 %copy-start = (bf16[1024,1024]{1,0:T(8,128)(2,1)S(1)}, bf16[1024,1024]{1,0:T(8,128)(2,1)}, u32[]{:S(2)}) copy-start(bf16[1024,1024]{1,0:T(8,128)(2,1)} %tokens.3) | copy-start | bytes 6291460
  1.7 12.1 %collective-permute-start = (bf16[256,1024]{1,0:T(8,128)(2,1)S(1)}, bf16[256,1024]{1,0:T(8,128)(2,1)S(1)}, u32[]{:S(2)}, u32[]{:S(2)}) collective-permute-start(bf16[256,1024]{1,0:T(8,128)(2,1)S(1)} %get-tuple-element.27), channel_id=1, source_target_pairs={{15,3},{31,19},{47,35},{63,51},{79,67},{95,83},{111,99},{127,115}} | collective-permute-start | bytes 1572872 | tf_op jit(solution)/shard_map/ppermute | solution.py:262
  2.4 11.4 %collective-permute-start.1 = (bf16[256,1024]{1,0:T(8,128)(2,1)S(1)}, bf16[256,1024]{1,0:T(8,128)(2,1)S(1)}, u32[]{:S(2)}, u32[]{:S(2)}) collective-permute-start(bf16[256,1024]{1,0:T(8,128)(2,1)S(1)} %get-tuple-element.28), channel_id=1, source_target_pairs={{15,11},{31,27},{47,43},{63,59},{79,75},{95,91},{111,107},{127,123}} | collective-permute-start | bytes 1572872 | tf_op jit(solution)/shard_map/ppermute | solution.py:262
  3.1 10.7 %collective-permute-start.2 = (bf16[256,1024]{1,0:T(8,128)(2,1)S(1)}, bf16[256,1024]{1,0:T(8,128)(2,1)S(1)}, u32[]{:S(2)}, u32[]{:S(2)}) collective-permute-start(bf16[256,1024]{1,0:T(8,128)(2,1)S(1)} %get-tuple-element.29), channel_id=1, source_target_pairs={{15,12},{31,28},{47,44},{63,60},{79,76},{95,92},{111,108},{127,124}} | collective-permute-start | bytes 1572872 | tf_op jit(solution)/shard_map/ppermute | solution.py:262
  3.9 10.0 %collective-permute-start.3 = (bf16[256,1024]{1,0:T(8,128)(2,1)S(1)}, bf16[256,1024]{1,0:T(8,128)(2,1)S(1)}, u32[]{:S(2)}, u32[]{:S(2)}) collective-permute-start(bf16[256,1024]{1,0:T(8,128)(2,1)S(1)} %get-tuple-element.30), channel_id=1, source_target_pairs={{15,14},{31,30},{47,46},{63,62},{79,78},{95,94},{111,110},{127,126}} | collective-permute-start | bytes 1572872 | tf_op jit(solution)/shard_map/ppermute | solution.py:262
  13.8 13.3 %copy-start.1 = (bf16[1024,1024]{1,0:T(8,128)(2,1)S(1)}, bf16[1024,1024]{1,0:T(8,128)(2,1)}, u32[]{:S(2)}) copy-start(bf16[1024,1024]{1,0:T(8,128)(2,1)} %w_query.1) | copy-start | bytes 6291460
  13.8 13.3 %copy-start.3 = (f32[1024]{0:T(1024)S(1)}, f32[1024]{0:T(1024)}, u32[]{:S(2)}) copy-start(f32[1024]{0:T(1024)} %param.8) | copy-start | bytes 12292
  14.1 13.0 %collective-permute-start.4 = (bf16[64,1024]{1,0:T(8,128)(2,1)S(1)}, bf16[64,1024]{1,0:T(8,128)(2,1)S(1)}, u32[]{:S(2)}, u32[]{:S(2)}) collective-permute-start(bf16[64,1024]{1,0:T(8,128)(2,1)S(1)} %get-tuple-element.37), channel_id=1, source_target_pairs={{3,0},{11,8},{12,13},{14,6},{19,16},{27,24},{28,29},{30,22},{35,32... | collective-permute-start | bytes 393224 | tf_op jit(solution)/shard_map/ppermute | solution.py:275
  15.6 11.6 %collective-permute-start.5 = (bf16[64,1024]{1,0:T(8,128)(2,1)S(1)}, bf16[64,1024]{1,0:T(8,128)(2,1)S(1)}, u32[]{:S(2)}, u32[]{:S(2)}) collective-permute-start(bf16[64,1024]{1,0:T(8,128)(2,1)S(1)} %get-tuple-element.38), channel_id=1, source_target_pairs={{3,2},{11,10},{12,4},{14,7},{19,18},{27,26},{28,20},{30,23},{35,34... | collective-permute-start | bytes 393224 | tf_op jit(solution)/shard_map/ppermute | solution.py:275
  16.2 10.9 %collective-permute-start.6 = (bf16[64,1024]{1,0:T(8,128)(2,1)S(1)}, bf16[64,1024]{1,0:T(8,128)(2,1)S(1)}, u32[]{:S(2)}, u32[]{:S(2)}) collective-permute-start(bf16[64,1024]{1,0:T(8,128)(2,1)S(1)} %get-tuple-element.39), channel_id=1, source_target_pairs={{3,1},{11,9},{12,5},{19,17},{27,25},{28,21},{35,33},{43,41},{44,37... | collective-permute-start | bytes 393224 | tf_op jit(solution)/shard_map/ppermute | solution.py:275
  53.7 18.3 %all-to-all-start.2 = ((bf16[16,32,1024]{2,1,0:T(8,128)(2,1)}), bf16[16,32,1024]{2,1,0:T(8,128)(2,1)S(1)}, u32[]{:S(2)}, u32[]{:S(2)}) async-start(bf16[16,32,1024]{2,1,0:T(8,128)(2,1)} %get-tuple-element.44), calls=%async_computation.2 | async-start | bytes 2097152 | tf_op jit(solution)/shard_map/all_to_all | solution.py:290
  72.0 7.2 %copy-start.5 = (bf16[16,32,1024]{2,1,0:T(8,128)(2,1)}, bf16[16,32,1024]{2,1,0:T(8,128)(2,1)S(1)}, u32[]{:S(2)}) copy-start(bf16[16,32,1024]{2,1,0:T(8,128)(2,1)S(1)} %all-to-all-done.2) | copy-start | bytes 3145732
  72.0 33.7 %all-to-all-start.1 = ((bf16[16,32,1152]{2,1,0:T(8,128)(2,1)}), bf16[16,32,1152]{2,1,0:T(8,128)(2,1)S(1)}, u32[]{:S(2)}, u32[]{:S(2)}) async-start(bf16[16,32,1152]{2,1,0:T(8,128)(2,1)} %bitcast.10), calls=%async_computation.1 | async-start | bytes 2359296 | tf_op jit(solution)/shard_map/all_to_all | solution.py:294
  105.6 21.4 %copy-start.2 = (bf16[1024,1024]{1,0:T(8,128)(2,1)S(1)}, bf16[1024,1024]{1,0:T(8,128)(2,1)}, u32[]{:S(2)}) copy-start(bf16[1024,1024]{1,0:T(8,128)(2,1)} %refs_4_.1) | copy-start | bytes 6291460
  105.6 21.4 %copy-start.4 = (f32[1024]{0:T(1024)S(1)}, f32[1024]{0:T(1024)}, u32[]{:S(2)}) copy-start(f32[1024]{0:T(1024)} %param.9) | copy-start | bytes 12292

commit v5 on v4

--- a/solution.py
+++ b/solution.py
@@ -61,8 +61,8 @@
     )(tokens, gain, w_key, w_value)
 
 
-def query_kernel(count, gain, w_query, *refs):
-    parts, (own, *tiled) = refs[:5], refs[5:]
+def query_kernel(gain, w_query, *refs):
+    parts, (own, tiled) = refs[:5], refs[5:]
     rows = parts[0][...].astype(jnp.float32)
     for part in parts[1:]:
         rows = rows + part[...].astype(jnp.float32)
@@ -71,20 +71,18 @@
     queries = jnp.dot(
         rms_rows(rows, gain[...]), w_query[...], preferred_element_type=jnp.float32
     ).astype(jnp.bfloat16)
-    begin = 0
-    for each in tiled:
-        end = begin + each.shape[1]
-        for to in range(count):
-            each[to] = queries[begin:end]
-        begin = end
+    for to in range(tiled.shape[0]):
+        tiled[to] = queries
 
 
 def project_queries(count, gain, w_query, parts):
     rows = parts[0].shape[0]
     return pl.pallas_call(
-        functools.partial(query_kernel, count),
-        out_shape=(jax.ShapeDtypeStruct((rows, D), jnp.bfloat16),)
-        + tuple(jax.ShapeDtypeStruct((count, each, D), jnp.bfloat16) for each in (PART, rows - PART)),
+        query_kernel,
+        out_shape=(
+            jax.ShapeDtypeStruct((rows, D), jnp.bfloat16),
+            jax.ShapeDtypeStruct((count, rows, D), jnp.bfloat16),
+        ),
         compiler_params=pltpu.CompilerParams(vmem_limit_bytes=16 * MIB),
         cost_estimate=pl.CostEstimate(flops=2 * rows * D * D, bytes_accessed=4 * D * D, transcendentals=0),
         name="project_queries",
@@ -102,7 +100,6 @@
     def attention(causal, count):
         lane = lax.broadcasted_iota(jnp.int32, (rows, 128), 1)
         lse = jnp.zeros((rows, 128), jnp.float32)
-        ones = jnp.ones((count, 128), jnp.bfloat16)
         if causal:
             key_pos = lax.broadcasted_iota(jnp.int32, (rows, count), 1)
             row = step * rows + lax.broadcasted_iota(jnp.int32, (rows, count), 0)
@@ -127,13 +124,11 @@
             if pair + 1 < pairs:
                 ahead = scores_of(pair + 1)
             top = jnp.max(scores, axis=-1, keepdims=True)
-            weights = jnp.exp2((scores - top) * EXP2_SCALE).astype(jnp.bfloat16)
-            mixed = jnp.dot(
-                weights,
-                jnp.concatenate([values[0:count, at], ones], axis=1),
-                preferred_element_type=jnp.float32,
+            weights = jnp.exp2((scores - top) * EXP2_SCALE)
+            total = jnp.sum(weights, axis=-1, keepdims=True)
+            mix = jnp.dot(
+                weights.astype(jnp.bfloat16), values[0:count, at], preferred_element_type=jnp.float32
             )
-            mix, total = mixed[:, 0:128], mixed[:, 128:256]
             both = jnp.where(low, mix[:rows], mix[rows:]) / jnp.where(low, total[:rows], total[rows:])
             out[:, at] = both.astype(jnp.bfloat16)
             level = top * EXP2_SCALE + jnp.log2(total)
@@ -183,7 +178,8 @@
 
 
 def finish_kernel(number, *refs):
-    parts, (own, gain, w_out, out) = refs[:number], refs[number:]
+    parts, owns = refs[:number], refs[number : number + 2]
+    gain, w_out, out = refs[number + 2 :]
     head = lax.broadcasted_iota(jnp.int32, (128, D), 0)
     column = lax.broadcasted_iota(jnp.int32, (128, D), 1)
     spread = (column // HEAD_DIM == head).astype(jnp.bfloat16)
@@ -205,33 +201,55 @@
         ).reshape(count, part, D)
         mix = jnp.sum(wide * each[:, :, 0:D].astype(jnp.float32), axis=0)
         posts.append(rms_rows(mix.astype(jnp.bfloat16), gain[...]))
-    mixed = own[...].astype(jnp.float32) + jnp.dot(
+    own = jnp.concatenate([rows[...] for rows in owns], axis=0)
+    mixed = own.astype(jnp.float32) + jnp.dot(
         jnp.concatenate(posts, axis=0), w_out[...], preferred_element_type=jnp.float32
     )
     out[...] = mixed.astype(jnp.bfloat16)
 
 
-def finish(parts, own, gain, w_out):
-    rows = own.shape[0]
+def finish(parts, owns, gain, w_out):
+    rows = sum(own.shape[0] for own in owns)
     return pl.pallas_call(
         functools.partial(finish_kernel, len(parts)),
         out_shape=jax.ShapeDtypeStruct((rows, D), jnp.bfloat16),
         compiler_params=pltpu.CompilerParams(vmem_limit_bytes=28 * MIB),
         cost_estimate=pl.CostEstimate(flops=4 * rows * D * D, bytes_accessed=8 * D * D, transcendentals=0),
         name="finish",
-    )(*parts, own, gain, w_out)
-
-
-def pack_kernel(owned, source, flag, tokens, own, *bundles):
-    def block(to):
-        return tokens[to * owned : (to + 1) * owned, :]
-
-    mine = block(source)
-    own[...] = jnp.where(flag[0] != 0, mine, jnp.zeros_like(mine))
-    for members, bundle in zip(BUNDLES, bundles):
-        for place in range(4):
-            at = slice(place * owned, (place + 1) * owned)
-            bundle[at, :] = block(members[min(place, len(members) - 1)])
+    )(*parts, *owns, gain, w_out)
+
+
+def pack_kernel(owned, source, flag, tokens, *outs):
+    for half, begin in enumerate(range(0, owned, PART)):
+        own, *bundles = outs[5 * half : 5 * half + 5]
+
+        def block(to):
+            return tokens[to * owned + begin : to * owned + begin + PART, :]
+
+        mine = block(source)
+        own[...] = jnp.where(flag[0] != 0, mine, jnp.zeros_like(mine))
+        for members, bundle in zip(BUNDLES, bundles):
+            for place in range(4):
+                at = slice(place * PART, (place + 1) * PART)
+                bundle[at, :] = block(members[min(place, len(members) - 1)])
+
+
+def pack(tokens, owned, source, flag):
+    shapes = (jax.ShapeDtypeStruct((PART, D), jnp.bfloat16),)
+    shapes += (jax.ShapeDtypeStruct((4 * PART, D), jnp.bfloat16),) * 4
+    outs = pl.pallas_call(
+        functools.partial(pack_kernel, owned, source),
+        out_shape=shapes * (owned // PART),
+        in_specs=[pl.BlockSpec(memory_space=pltpu.SMEM), pl.BlockSpec(memory_space=pltpu.VMEM)],
+        compiler_params=pltpu.CompilerParams(vmem_limit_bytes=16 * MIB),
+        cost_estimate=pl.CostEstimate(flops=0, bytes_accessed=8 * D * D, transcendentals=0),
+        name="pack",
+    )(flag, tokens)
+    return outs[:5], outs[5:]
+
+
+def send_bundles(bundles, source):
+    return [lax.ppermute(bundle, "seq", [(source, members[0])]) for members, bundle in zip(BUNDLES, bundles)]
 
 
 def relay_kernel(*refs):
@@ -245,27 +263,11 @@
         out[...] = total.astype(jnp.bfloat16)
 
 
-def scatter(tokens, owned, source, flag, beside):
-    limit = pltpu.CompilerParams(vmem_limit_bytes=16 * MIB)
-    block = jax.ShapeDtypeStruct((owned, D), jnp.bfloat16)
-    smem = pl.BlockSpec(memory_space=pltpu.SMEM)
-    vmem = pl.BlockSpec(memory_space=pltpu.VMEM)
-    own, *bundles = pl.pallas_call(
-        functools.partial(pack_kernel, owned, source),
-        out_shape=(block,) + (jax.ShapeDtypeStruct((4 * owned, D), jnp.bfloat16),) * 4,
-        in_specs=[smem, vmem],
-        compiler_params=limit,
-        cost_estimate=pl.CostEstimate(flops=0, bytes_accessed=8 * D * D, transcendentals=0),
-        name="pack",
-    )(flag, tokens)
-    bundles = [
-        lax.ppermute(bundle, "seq", [(source, members[0])]) for members, bundle in zip(BUNDLES, bundles)
-    ]
-    bundles, _ = lax.optimization_barrier((bundles, beside))
+def pass_on(own, bundles):
     kept, *passed = pl.pallas_call(
         relay_kernel,
-        out_shape=(block,) * 4,
-        compiler_params=limit,
+        out_shape=(jax.ShapeDtypeStruct(own.shape, jnp.bfloat16),) * 4,
+        compiler_params=pltpu.CompilerParams(vmem_limit_bytes=16 * MIB),
         cost_estimate=pl.CostEstimate(flops=0, bytes_accessed=4 * D * D, transcendentals=0),
         name="relay",
     )(*bundles)
@@ -276,23 +278,32 @@
     return parts
 
 
+def after(value, *others):
+    return lax.optimization_barrier((value, others))[0]
+
+
 def local(tokens, ln_gain, post_gain, w_query, w_key, w_value, w_out):
     count = lax.axis_size("seq")
-    last = lax.axis_index("seq") == count - 1
+    source = count - 1
+    last = lax.axis_index("seq") == source
     flag = last.astype(jnp.int32).reshape(1)
     owned = LATENTS // count
     gain = ln_gain.reshape(1, D)
-    keys, values = project_kv(tokens, gain, w_key, w_value)
-    parts = scatter(tokens, owned, count - 1, flag, keys)
-    own, tiled_a, tiled_b = project_queries(count, gain, w_query, parts)
-    rows_a = lax.all_to_all(tiled_a, "seq", 0, 0)
+    exchange = lambda blocks: lax.all_to_all(blocks, "seq", 0, 0)
+
+    (own_a, *bundles_a), (own_b, *bundles_b) = pack(tokens, owned, source, flag)
+    came_a, came_b = send_bundles(bundles_a, source), send_bundles(bundles_b, source)
+    own_a, tiled_a = project_queries(count, gain, w_query, pass_on(own_a, came_a))
+    rows_a = exchange(tiled_a)
+    parts_b = pass_on(own_b, after(came_b, tiled_a))
+    keys, values = project_kv(after(tokens, parts_b[1]), gain, w_key, w_value)
+    own_b, tiled_b = project_queries(count, gain, w_query, after(parts_b, keys))
     rows_a, tiled_b = lax.optimization_barrier((rows_a, tiled_b))
-    rows_b = lax.all_to_all(tiled_b, "seq", 0, 0)
+    rows_b = exchange(tiled_b)
     mixed_a = attend(0, owned, flag, rows_a.reshape(-1, D), keys, values)
-    rows_b, _ = lax.optimization_barrier((rows_b, mixed_a))
-    mixed_b = attend(1, owned, flag, rows_b.reshape(-1, D), keys, values)
-    mixed = [lax.all_to_all(each.reshape(count, PART, WIDE), "seq", 0, 0) for each in (mixed_a, mixed_b)]
-    return finish(mixed, own, post_gain.reshape(1, D), w_out)
+    mixed_b = attend(1, owned, flag, after(rows_b, mixed_a).reshape(-1, D), keys, values)
+    mixed = [exchange(each.reshape(count, PART, WIDE)) for each in (mixed_a, mixed_b)]
+    return finish(mixed, (own_a, own_b), post_gain.reshape(1, D), w_out)
 
 
 def solution(mesh):

time: 127 us -> 144 us (1.13)
  blocking collectives: 46.2 us -> 21.3 us
  starting transfers between devices: 16.3 us -> 38.3 us
  waiting for transfers between devices: 10.2 us -> 26.2 us
  Pallas kernels: 54.6 us -> 57.3 us
    all_to_all x2 -> x1, blocking collectives: 46.2 us -> 21.3 us  [local(): exchange = lambda blocks: lax.all_to_all(blocks, 'seq', 0, 0)]
    all_to_all x2 -> x3, starting transfers between devices: 10.8 us -> 27.7 us  [local(): exchange = lambda blocks: lax.all_to_all(blocks, 'seq', 0, 0)]
    ppermute x7 -> x14, waiting for transfers between devices: 10.2 us -> 23.8 us  [the longest x6 23.8 us: pass_on(): parts.append(lax.ppermute(passed[place - 1], 'seq', pairs))]
    ppermute x7 -> x14, starting transfers between devices: 5.54 us -> 10.7 us  [the longest x8 5.42 us: send_bundles(): lax.ppermute(bundle, 'seq', [(source, members[0])])]
    all_to_all x2 -> x3, waiting for transfers between devices: 0.01 us -> 2.38 us  [local(): exchange = lambda blocks: lax.all_to_all(blocks, 'seq', 0, 0)]
    pallas_call x3 -> x5, Pallas kernels: 2.12 us -> 3.69 us  [the longest x2 3.28 us: project_queries(): pl.pallas_call(query_kernel, out_shape=(jax.ShapeDtypeStruct((rows, D), j...]
  transfers between devices with their start and end apart: 9 -> 17, of which waited for: 1 -> 3; matrix products, arithmetic and copies ran while one was open for 0% -> 0% of each run, Pallas kernels for 39% -> 37%
where the time goes in v5:
time: 144 us; the launch traced here: 145 us
  Pallas kernels  57.3 us (40%)
  starting transfers between devices  38.3 us (27%)
  waiting for transfers between devices  26.2 us (18%)
  blocking collectives  21.3 us (15%)
  local copies, waits for them, and re-layouts  1.77 us (1%)
    pallas_call x2, Pallas kernels, attend(): pl.pallas_call(functools.partial(attend_kernel, chunk, owned), grid=(coun...  42.3 us
    all_to_all x3, starting transfers between devices, local(): exchange = lambda blocks: lax.all_to_all(blocks, 'seq', 0, 0)  27.7 us
    ppermute x6, waiting for transfers between devices, pass_on(): parts.append(lax.ppermute(passed[place - 1], 'seq', pairs))  23.8 us
    all_to_all x1, blocking collectives, local(): exchange = lambda blocks: lax.all_to_all(blocks, 'seq', 0, 0)  21.3 us
    pallas_call x1, Pallas kernels, project_kv(): pl.pallas_call(kv_kernel, grid=(D // cols,), out_shape=(jax.ShapeDtypeStr...  9.26 us
    ppermute x8, starting transfers between devices, send_bundles(): lax.ppermute(bundle, 'seq', [(source, members[0])])  5.42 us
    ppermute x6, starting transfers between devices, pass_on(): parts.append(lax.ppermute(passed[place - 1], 'seq', pairs))  5.24 us
    pallas_call x2, Pallas kernels, project_queries(): pl.pallas_call(query_kernel, out_shape=(jax.ShapeDtypeStruct((rows, D), j...  3.28 us
  transfers between devices with their start and end apart: 17, of which 3 were waited for; matrix products, arithmetic and copies ran while one was open for 0% of the time, Pallas kernels for 37%

profile of v5, /device:TPU:0, one launch (start us, length us, event | category | flops | bytes accessed | tf_op | source)
XLA Modules:
  0.0 145.3 jit_solution(4002449041108814791)
XLA Ops:
  0.0 0.0 copy-start
  0.0 0.0 copy-start.1
  0.0 1.7 %copy-done.1 = bf16[1024,1024]{1,0:T(8,128)(2,1)S(1)} copy-done((bf16[1024,1024]{1,0:T(8,128)(2,1)S(1)}, bf16[1024,1024]{1,0:T(8,128)(2,1)}, u32[]{:S(2)}) %copy-start.1) | copy-done | bytes 2097176
  1.7 0.0 copy-start.3
  1.7 0.1 pack.1
  1.9 0.7 collective-permute-start
  2.6 0.7 collective-permute-start.1
  3.3 0.7 collective-permute-start.2
  4.0 0.7 collective-permute-start.3
  4.6 0.0 collective-permute-done.refs_0_
  4.6 0.0 collective-permute-done.1.refs_1_
  4.7 0.0 collective-permute-done.2.refs_2_
  4.7 0.0 collective-permute-done.3.refs_3_
  4.7 0.1 relay.2
  4.8 1.3 collective-permute-start.4
  6.1 0.7 collective-permute-start.5
  6.8 0.7 collective-permute-start.6
  7.5 13.4 %collective-permute-done.4.refs_2_ = bf16[32,1024]{1,0:T(8,128)(2,1)S(1)} collective-permute-done((bf16[32,1024]{1,0:T(8,128)(2,1)S(1)}, bf16[32,1024]{1,0:T(8,128)(2,1)S(1)}, u32[]{:S(2)}, u32[]{:S(2)}) %collective-permute-start.4) | collective-permute-done | bytes 65568 | tf_op jit(solution)/shard_map/ppermute | solution.py:277
  20.8 0.0 collective-permute-done.5.refs_3_
  20.8 0.0 collective-permute-done.6.refs_4_
  20.8 0.0 copy-done
  20.9 0.0 copy-done.3
  20.9 1.7 %project_queries.2 = (bf16[32,1024]{1,0:T(8,128)(2,1)S(1)}, bf16[16,32,1024]{2,1,0:T(8,128)(2,1)}) custom-call(f32[1,1024]{1,0:T(1,128)S(1)} %bitcast.8, bf16[1024,1024]{1,0:T(8,128)(2,1)S(1)} %copy-done, bf16[32,1024]{1,0:T(8,128)(2,1)S(1)} %get-tuple-element.42.refs_0_, bf16[32,1024]{1,0:T(8,128)(2,1)S(1)} %get-tuple-element.47.refs_1_, ...), custom_call_target="tpu_custom_call" | custom-call | flops 67108864 | bytes 4194304 | tf_op jit(solution)/shard_map/project_queries/pallas_call | solution.py:80
  22.5 8.4 %all-to-all-start = ((bf16[16,32,1024]{2,1,0:T(8,128)(2,1)}), bf16[16,32,1024]{2,1,0:T(8,128)(2,1)}, u32[]{:S(2)}, u32[]{:S(2)}) async-start(bf16[16,32,1024]{2,1,0:T(8,128)(2,1)} %get-tuple-element.51), calls=%async_computation | async-start | bytes 2097152 | tf_op jit(solution)/shard_map/all_to_all | solution.py:292
  30.9 0.7 collective-permute-start.7
  31.6 0.7 collective-permute-start.8
  32.3 0.7 collective-permute-start.9
  33.0 0.7 collective-permute-start.10
  33.7 0.0 collective-permute-done.7.refs_0_
  33.7 0.0 collective-permute-done.8.refs_1_
  33.7 0.0 collective-permute-done.9.refs_2_
  33.7 0.0 collective-permute-done.10.refs_3_
  33.7 0.1 relay.3
  33.9 1.3 collective-permute-start.11
  35.2 0.7 collective-permute-start.12
  35.8 0.0 copy-start.4
  35.8 0.7 collective-permute-start.13
  36.5 9.3 %project_kv.1 = (bf16[1024,1024]{1,0:T(8,128)(2,1)}, bf16[1024,1024]{1,0:T(8,128)(2,1)}) custom-call(bf16[1024,1024]{1,0:T(8,128)(2,1)} %tokens.2, f32[1,1024]{1,0:T(1,128)} %bitcast.7, bf16[1024,1024]{1,0:T(8,128)(2,1)} %w_key.1, bf16[1024,1024]{1,0:T(8,128)(2,1)} %w_value.1), custom_call_target="tpu_custom_call" | custom-call | flops 4294967296 | bytes 10485760 | tf_op jit(solution)/shard_map/project_kv/pallas_call | solution.py:46
  45.8 10.4 %collective-permute-done.11.refs_2_ = bf16[32,1024]{1,0:T(8,128)(2,1)S(1)} collective-permute-done((bf16[32,1024]{1,0:T(8,128)(2,1)S(1)}, bf16[32,1024]{1,0:T(8,128)(2,1)S(1)}, u32[]{:S(2)}, u32[]{:S(2)}) %collective-permute-start.11) | collective-permute-done | bytes 65568 | tf_op jit(solution)/shard_map/ppermute | solution.py:277
  56.2 0.0 collective-permute-done.12.refs_3_
  56.2 0.0 collective-permute-done.13.refs_4_
  56.2 0.0 copy-done.4
  56.2 1.6 %project_queries.3 = (bf16[32,1024]{1,0:T(8,128)(2,1)S(1)}, bf16[16,32,1024]{2,1,0:T(8,128)(2,1)}) custom-call(f32[1,1024]{1,0:T(1,128)S(1)} %bitcast.9, bf16[1024,1024]{1,0:T(8,128)(2,1)S(1)} %copy-done, bf16[32,1024]{1,0:T(8,128)(2,1)S(1)} %get-tuple-element.67.refs_0_, bf16[32,1024]{1,0:T(8,128)(2,1)S(1)} %get-tuple-element.68.refs_1_, ...), custom_call_target="tpu_custom_call" | custom-call | flops 67108864 | bytes 4194304 | tf_op jit(solution)/shard_map/project_queries/pallas_call | solution.py:80
  57.8 0.0 all-to-all-done
  57.8 12.0 %all-to-all-start.2 = ((bf16[16,32,1024]{2,1,0:T(8,128)(2,1)}), bf16[16,32,1024]{2,1,0:T(8,128)(2,1)S(1)}, u32[]{:S(2)}, u32[]{:S(2)}) async-start(bf16[16,32,1024]{2,1,0:T(8,128)(2,1)} %get-tuple-element.75), calls=%async_computation.2 | async-start | bytes 2097152 | tf_op jit(solution)/shard_map/all_to_all | solution.py:292
  69.8 27.6 %attend_0.1 = bf16[512,1152]{1,0:T(8,128)(2,1)} custom-call(s32[1]{0:T(128)} %bitcast.flag, bf16[512,1024]{1,0:T(8,128)(2,1)} %bitcast.2.queries, bf16[1024,1024]{1,0:T(8,128)(2,1)} %get-tuple-element.66.keys, bf16[1024,1024]{1,0:T(8,128)(2,1)} %get-tuple-element.74.values), custom_call_target="tpu_custom_call" | custom-call | flops 8589934592 | bytes 8388608 | tf_op jit(solution)/shard_map/attend_0/pallas_call | solution.py:161
  97.5 0.0 all-to-all-done.2
  97.5 0.0 copy-start.6
  97.5 7.2 %all-to-all-start.1 = ((bf16[16,32,1152]{2,1,0:T(8,128)(2,1)}), bf16[16,32,1152]{2,1,0:T(8,128)(2,1)S(1)}, u32[]{:S(2)}, u32[]{:S(2)}) async-start(bf16[16,32,1152]{2,1,0:T(8,128)(2,1)} %bitcast.11), calls=%async_computation.1 | async-start | bytes 2359296 | tf_op jit(solution)/shard_map/all_to_all | solution.py:292
  104.7 0.0 copy-done.6
  104.7 14.7 %attend_1.1 = bf16[512,1152]{1,0:T(8,128)(2,1)} custom-call(s32[1]{0:T(128)} %bitcast.flag, bf16[512,1024]{1,0:T(8,128)(2,1)} %bitcast.13, bf16[1024,1024]{1,0:T(8,128)(2,1)} %get-tuple-element.66.keys, bf16[1024,1024]{1,0:T(8,128)(2,1)} %get-tuple-element.74.values), custom_call_target="tpu_custom_call" | custom-call | flops 8589934592 | bytes 8388608 | tf_op jit(solution)/shard_map/attend_1/pallas_call | solution.py:161
  119.4 0.0 copy-start.2
  119.4 0.0 copy-start.5
  119.4 2.4 %all-to-all-done.1.refs_0_ = bf16[16,32,1152]{2,1,0:T(8,128)(2,1)S(1)} async-done(((bf16[16,32,1152]{2,1,0:T(8,128)(2,1)}), bf16[16,32,1152]{2,1,0:T(8,128)(2,1)S(1)}, u32[]{:S(2)}, u32[]{:S(2)}) %all-to-all-start.1) | async-done | bytes 1179680 | tf_op jit(solution)/shard_map/all_to_all | solution.py:292
  121.8 21.3 %all_to_all.20.refs_1_ = bf16[16,32,1152]{2,1,0:T(8,128)(2,1)S(1)} all-to-all(bf16[16,32,1152]{2,1,0:T(8,128)(2,1)} %bitcast.12), channel_id=1, replica_groups=mesh['ctx'=8,'seq'=16] {'seq'}, dimensions={0} | all-to-all | bytes 2359296 | tf_op jit(solution)/shard_map/all_to_all | solution.py:292
  143.1 0.0 copy-done.2
  143.1 0.0 copy-done.5
  143.1 2.1 %finish.1 = bf16[64,1024]{1,0:T(8,128)(2,1)} custom-call(bf16[16,32,1152]{2,1,0:T(8,128)(2,1)S(1)} %all-to-all-done.1.refs_0_, bf16[16,32,1152]{2,1,0:T(8,128)(2,1)S(1)} %all_to_all.20.refs_1_, bf16[32,1024]{1,0:T(8,128)(2,1)S(1)} %get-tuple-element.77.refs_2_, bf16[32,1024]{1,0:T(8,128)(2,1)S(1)} %get-tuple-element.78.refs_3_, f32[1,1024]{1,0:T(1,128)S(1)} %bitcast.10, ...), custom_call_target="tpu_custom_call" | custom-call | flops 268435456 | bytes 8388608 | tf_op jit(solution)/shard_map/finish/pallas_call | solution.py:213
Async XLA Ops:
  0.0 20.8 %copy-start = (bf16[1024,1024]{1,0:T(8,128)(2,1)S(1)}, bf16[1024,1024]{1,0:T(8,128)(2,1)}, u32[]{:S(2)}) copy-start(bf16[1024,1024]{1,0:T(8,128)(2,1)} %w_query.3) | copy-start | bytes 6291460
  0.0 1.7 %copy-start.1 = (bf16[1024,1024]{1,0:T(8,128)(2,1)S(1)}, bf16[1024,1024]{1,0:T(8,128)(2,1)}, u32[]{:S(2)}) copy-start(bf16[1024,1024]{1,0:T(8,128)(2,1)} %tokens.2) | copy-start | bytes 6291460
  1.7 19.1 %copy-start.3 = (f32[1024]{0:T(1024)S(1)}, f32[1024]{0:T(1024)}, u32[]{:S(2)}) copy-start(f32[1024]{0:T(1024)} %param.8) | copy-start | bytes 12292
  1.9 2.7 %collective-permute-start = (bf16[128,1024]{1,0:T(8,128)(2,1)S(1)}, bf16[128,1024]{1,0:T(8,128)(2,1)S(1)}, u32[]{:S(2)}, u32[]{:S(2)}) collective-permute-start(bf16[128,1024]{1,0:T(8,128)(2,1)S(1)} %get-tuple-element.43), channel_id=1, source_target_pairs={{15,3},{31,19},{47,35},{63,51},{79,67},{95,83},{111,99},{127,115}} | collective-permute-start | bytes 786440 | tf_op jit(solution)/shard_map/ppermute | solution.py:252
  2.6 2.1 %collective-permute-start.1 = (bf16[128,1024]{1,0:T(8,128)(2,1)S(1)}, bf16[128,1024]{1,0:T(8,128)(2,1)S(1)}, u32[]{:S(2)}, u32[]{:S(2)}) collective-permute-start(bf16[128,1024]{1,0:T(8,128)(2,1)S(1)} %get-tuple-element.44), channel_id=1, source_target_pairs={{15,11},{31,27},{47,43},{63,59},{79,75},{95,91},{111,107},{127,123}} | collective-permute-start | bytes 786440 | tf_op jit(solution)/shard_map/ppermute | solution.py:252
  3.3 1.4 collective-permute-start.2
  4.0 0.7 collective-permute-start.3
  4.8 16.0 %collective-permute-start.4 = (bf16[32,1024]{1,0:T(8,128)(2,1)S(1)}, bf16[32,1024]{1,0:T(8,128)(2,1)S(1)}, u32[]{:S(2)}, u32[]{:S(2)}) collective-permute-start(bf16[32,1024]{1,0:T(8,128)(2,1)S(1)} %get-tuple-element.48), channel_id=1, source_target_pairs={{3,0},{11,8},{12,13},{14,6},{19,16},{27,24},{28,29},{30,22},{35,32... | collective-permute-start | bytes 196616 | tf_op jit(solution)/shard_map/ppermute | solution.py:277
  6.1 14.7 %collective-permute-start.5 = (bf16[32,1024]{1,0:T(8,128)(2,1)S(1)}, bf16[32,1024]{1,0:T(8,128)(2,1)S(1)}, u32[]{:S(2)}, u32[]{:S(2)}) collective-permute-start(bf16[32,1024]{1,0:T(8,128)(2,1)S(1)} %get-tuple-element.49), channel_id=1, source_target_pairs={{3,2},{11,10},{12,4},{14,7},{19,18},{27,26},{28,20},{30,23},{35,34... | collective-permute-start | bytes 196616 | tf_op jit(solution)/shard_map/ppermute | solution.py:277
  6.8 14.1 %collective-permute-start.6 = (bf16[32,1024]{1,0:T(8,128)(2,1)S(1)}, bf16[32,1024]{1,0:T(8,128)(2,1)S(1)}, u32[]{:S(2)}, u32[]{:S(2)}) collective-permute-start(bf16[32,1024]{1,0:T(8,128)(2,1)S(1)} %get-tuple-element.50), channel_id=1, source_target_pairs={{3,1},{11,9},{12,5},{19,17},{27,25},{28,21},{35,33},{43,41},{44,37... | collective-permute-start | bytes 196616 | tf_op jit(solution)/shard_map/ppermute | solution.py:277
  22.5 35.3 %all-to-all-start = ((bf16[16,32,1024]{2,1,0:T(8,128)(2,1)}), bf16[16,32,1024]{2,1,0:T(8,128)(2,1)}, u32[]{:S(2)}, u32[]{:S(2)}) async-start(bf16[16,32,1024]{2,1,0:T(8,128)(2,1)} %get-tuple-element.51), calls=%async_computation | async-start | bytes 2097152 | tf_op jit(solution)/shard_map/all_to_all | solution.py:292
  30.9 2.7 %collective-permute-start.7 = (bf16[128,1024]{1,0:T(8,128)(2,1)S(1)}, bf16[128,1024]{1,0:T(8,128)(2,1)S(1)}, u32[]{:S(2)}, u32[]{:S(2)}) collective-permute-start(bf16[128,1024]{1,0:T(8,128)(2,1)S(1)} %get-tuple-element.53), channel_id=1, source_target_pairs={{15,3},{31,19},{47,35},{63,51},{79,67},{95,83},{111,99},{127,115}} | collective-permute-start | bytes 786440 | tf_op jit(solution)/shard_map/ppermute | solution.py:252
  31.6 2.1 %collective-permute-start.8 = (bf16[128,1024]{1,0:T(8,128)(2,1)S(1)}, bf16[128,1024]{1,0:T(8,128)(2,1)S(1)}, u32[]{:S(2)}, u32[]{:S(2)}) collective-permute-start(bf16[128,1024]{1,0:T(8,128)(2,1)S(1)} %get-tuple-element.54), channel_id=1, source_target_pairs={{15,11},{31,27},{47,43},{63,59},{79,75},{95,91},{111,107},{127,123}} | collective-permute-start | bytes 786440 | tf_op jit(solution)/shard_map/ppermute | solution.py:252
  32.3 1.4 collective-permute-start.9
  33.0 0.7 collective-permute-start.10
  33.9 22.3 %collective-permute-start.11 = (bf16[32,1024]{1,0:T(8,128)(2,1)S(1)}, bf16[32,1024]{1,0:T(8,128)(2,1)S(1)}, u32[]{:S(2)}, u32[]{:S(2)}) collective-permute-start(bf16[32,1024]{1,0:T(8,128)(2,1)S(1)} %get-tuple-element.62), channel_id=1, source_target_pairs={{3,0},{11,8},{12,13},{14,6},{19,16},{27,24},{28,29},{30,22},{35,32... | collective-permute-start | bytes 196616 | tf_op jit(solution)/shard_map/ppermute | solution.py:277
  35.2 21.0 %collective-permute-start.12 = (bf16[32,1024]{1,0:T(8,128)(2,1)S(1)}, bf16[32,1024]{1,0:T(8,128)(2,1)S(1)}, u32[]{:S(2)}, u32[]{:S(2)}) collective-permute-start(bf16[32,1024]{1,0:T(8,128)(2,1)S(1)} %get-tuple-element.63), channel_id=1, source_target_pairs={{3,2},{11,10},{12,4},{14,7},{19,18},{27,26},{28,20},{30,23},{35,34... | collective-permute-start | bytes 196616 | tf_op jit(solution)/shard_map/ppermute | solution.py:277
  35.8 20.3 %copy-start.4 = (f32[1024]{0:T(1024)S(1)}, f32[1024]{0:T(1024)}, u32[]{:S(2)}) copy-start(f32[1024]{0:T(1024)} %param.8) | copy-start | bytes 12292
  35.8 20.3 %collective-permute-start.13 = (bf16[32,1024]{1,0:T(8,128)(2,1)S(1)}, bf16[32,1024]{1,0:T(8,128)(2,1)S(1)}, u32[]{:S(2)}, u32[]{:S(2)}) collective-permute-start(bf16[32,1024]{1,0:T(8,128)(2,1)S(1)} %get-tuple-element.64), channel_id=1, source_target_pairs={{3,1},{11,9},{12,5},{19,17},{27,25},{28,21},{35,33},{43,41},{44,37... | collective-permute-start | bytes 196616 | tf_op jit(solution)/shard_map/ppermute | solution.py:277
  57.8 39.7 %all-to-all-start.2 = ((bf16[16,32,1024]{2,1,0:T(8,128)(2,1)}), bf16[16,32,1024]{2,1,0:T(8,128)(2,1)S(1)}, u32[]{:S(2)}, u32[]{:S(2)}) async-start(bf16[16,32,1024]{2,1,0:T(8,128)(2,1)} %get-tuple-element.75), calls=%async_computation.2 | async-start | bytes 2097152 | tf_op jit(solution)/shard_map/all_to_all | solution.py:292
  97.5 7.2 %copy-start.6 = (bf16[16,32,1024]{2,1,0:T(8,128)(2,1)}, bf16[16,32,1024]{2,1,0:T(8,128)(2,1)S(1)}, u32[]{:S(2)}) copy-start(bf16[16,32,1024]{2,1,0:T(8,128)(2,1)S(1)} %all-to-all-done.2) | copy-start | bytes 3145732
  97.5 24.3 %all-to-all-start.1 = ((bf16[16,32,1152]{2,1,0:T(8,128)(2,1)}), bf16[16,32,1152]{2,1,0:T(8,128)(2,1)S(1)}, u32[]{:S(2)}, u32[]{:S(2)}) async-start(bf16[16,32,1152]{2,1,0:T(8,128)(2,1)} %bitcast.11), calls=%async_computation.1 | async-start | bytes 2359296 | tf_op jit(solution)/shard_map/all_to_all | solution.py:292
  119.4 23.7 %copy-start.2 = (bf16[1024,1024]{1,0:T(8,128)(2,1)S(1)}, bf16[1024,1024]{1,0:T(8,128)(2,1)}, u32[]{:S(2)}) copy-start(bf16[1024,1024]{1,0:T(8,128)(2,1)} %refs_5_.1) | copy-start | bytes 6291460
  119.4 23.7 %copy-start.5 = (f32[1024]{0:T(1024)S(1)}, f32[1024]{0:T(1024)}, u32[]{:S(2)}) copy-start(f32[1024]{0:T(1024)} %param.9) | copy-start | bytes 12292

commit v6 on v4

--- a/solution.py
+++ b/solution.py
@@ -13,6 +13,7 @@
 PAIRS = HEADS // 2
 LATENTS = 1024
 PART = 32
+SPLIT = 4
 LOG2E = 1.4426950408889634
 EXP2_SCALE = LOG2E * HEAD_DIM ** (-0.5)
 MASKED = -1e30
@@ -34,7 +35,7 @@
         normed[...] = rms_rows(tokens[...], gain[...])
 
     rows = normed[...]
-    keys[...] = jnp.dot(rows, w_key[...], preferred_element_type=jnp.float32).astype(jnp.bfloat16)
+    keys[...] = jnp.dot(rows, w_key[...], preferred_element_type=jnp.float32).T.astype(jnp.bfloat16)
     values[...] = jnp.dot(rows, w_value[...], preferred_element_type=jnp.float32).astype(jnp.bfloat16)
 
 
@@ -46,14 +47,17 @@
     return pl.pallas_call(
         kv_kernel,
         grid=(D // cols,),
-        out_shape=(jax.ShapeDtypeStruct((rows, D), jnp.bfloat16),) * 2,
+        out_shape=(
+            jax.ShapeDtypeStruct((D, rows), jnp.bfloat16),
+            jax.ShapeDtypeStruct((rows, D), jnp.bfloat16),
+        ),
         in_specs=[
             pl.BlockSpec((rows, D), whole, pipeline_mode=pl.Buffered(1)),
             pl.BlockSpec((1, D), whole),
             pl.BlockSpec((D, cols), block),
             pl.BlockSpec((D, cols), block),
         ],
-        out_specs=(pl.BlockSpec((rows, cols), block),) * 2,
+        out_specs=(pl.BlockSpec((cols, rows), lambda c: (c, 0)), pl.BlockSpec((rows, cols), block)),
         scratch_shapes=[pltpu.VMEM((rows, D), jnp.bfloat16)],
         compiler_params=pltpu.CompilerParams(vmem_limit_bytes=56 * MIB),
         cost_estimate=pl.CostEstimate(flops=4 * rows * D * D, bytes_accessed=10 * rows * D, transcendentals=0),
@@ -91,13 +95,18 @@
     )(gain, w_query, *parts)
 
 
-def attend_kernel(chunk, owned, flag, queries, keys, values, out):
+def attend_kernel(chunk, owned, flag, queries, *refs):
+    keys, values, out = refs[:SPLIT], refs[SPLIT : 2 * SPLIT], refs[-1]
     rows = queries.shape[0]
-    count = keys.shape[0]
+    count = values[0].shape[0]
     step = pl.program_id(0)
     pairs = HEADS // 2
     part = PART
     low = lax.broadcasted_iota(jnp.int32, (1, 128), 1) < HEAD_DIM
+
+    def place(pair):
+        begin = pair * 128 % (D // SPLIT)
+        return pair * 128 // (D // SPLIT), slice(begin, begin + 128)
 
     def attention(causal, count):
         lane = lax.broadcasted_iota(jnp.int32, (rows, 128), 1)
@@ -115,9 +124,8 @@
             query = queries[:, at]
             none = jnp.zeros_like(query)
             both = jnp.concatenate([jnp.where(low, query, none), jnp.where(low, none, query)], axis=0)
-            scores = lax.dot_general(
-                both, keys[0:count, at], (((1,), (1,)), ((), ())), preferred_element_type=jnp.float32
-            )
+            block, features = place(pair)
+            scores = jnp.dot(both, keys[block][features, 0:count], preferred_element_type=jnp.float32)
             return jnp.where(allowed, scores, MASKED) if causal else scores
 
         ahead = scores_of(0)
@@ -126,11 +134,12 @@
             scores = ahead
             if pair + 1 < pairs:
                 ahead = scores_of(pair + 1)
+            block, features = place(pair)
             top = jnp.max(scores, axis=-1, keepdims=True)
             weights = jnp.exp2((scores - top) * EXP2_SCALE).astype(jnp.bfloat16)
             mixed = jnp.dot(
                 weights,
-                jnp.concatenate([values[0:count, at], ones], axis=1),
+                jnp.concatenate([values[block][0:count, features], ones], axis=1),
                 preferred_element_type=jnp.float32,
             )
             mix, total = mixed[:, 0:128], mixed[:, 128:256]
@@ -161,7 +170,8 @@
 def attend(chunk, owned, is_last, queries, keys, values):
     count = queries.shape[0]
     rows = 256
-    whole = lambda c: (0, 0)
+    key_block = lambda i, c: (i, 0)
+    value_block = lambda i, c: (0, i)
     block = lambda c: (c, 0)
     return pl.pallas_call(
         functools.partial(attend_kernel, chunk, owned),
@@ -170,16 +180,16 @@
         in_specs=[
             pl.BlockSpec(memory_space=pltpu.SMEM),
             pl.BlockSpec((rows, D), block),
-            pl.BlockSpec(keys.shape, whole),
-            pl.BlockSpec(values.shape, whole),
-        ],
+        ]
+        + [pl.BlockSpec((D // SPLIT, keys.shape[1]), functools.partial(key_block, i)) for i in range(SPLIT)]
+        + [pl.BlockSpec((values.shape[0], D // SPLIT), functools.partial(value_block, i)) for i in range(SPLIT)],
         out_specs=pl.BlockSpec((rows, WIDE), block),
         compiler_params=pltpu.CompilerParams(vmem_limit_bytes=56 * MIB),
         cost_estimate=pl.CostEstimate(
             flops=16 * count * D * D, bytes_accessed=8 * D * D, transcendentals=HEADS * count * D
         ),
         name="attend_%d" % chunk,
-    )(is_last, queries, keys, values)
+    )(is_last, queries, *([keys] * SPLIT), *([values] * SPLIT))
 
 
 def finish_kernel(number, *refs):

time: 127 us -> 127 us (level)
  no operation moved by 1% of the time
where the time goes in v6:
time: 127 us; the launch traced here: 128 us
  Pallas kernels  53.7 us (42%)
  blocking collectives  46.2 us (36%)
  starting transfers between devices  16.4 us (13%)
  waiting for transfers between devices  10.2 us (8%)
  local copies, waits for them, and re-layouts  1.61 us (1%)
    pallas_call x2, Pallas kernels, attend(): pl.pallas_call(functools.partial(attend_kernel, chunk, owned), grid=(coun...  40.2 us
    all_to_all x1, blocking collectives, local(): rows_a = lax.all_to_all(tiled_a, 'seq', 0, 0)  24.8 us
    all_to_all x1, blocking collectives, local(): lax.all_to_all(each.reshape(count, PART, WIDE), 'seq', 0, 0)  21.4 us
    ppermute x3, waiting for transfers between devices, scatter(): parts.append(lax.ppermute(passed[place - 1], 'seq', pairs))  10.2 us
    pallas_call x1, Pallas kernels, project_kv(): pl.pallas_call(kv_kernel, grid=(D // cols,), out_shape=(jax.ShapeDtypeStr...  9.27 us
    all_to_all x1, starting transfers between devices, local(): lax.all_to_all(each.reshape(count, PART, WIDE), 'seq', 0, 0)  7.16 us
    all_to_all x1, starting transfers between devices, local(): rows_b = lax.all_to_all(tiled_b, 'seq', 0, 0)  3.65 us
    ppermute x4, starting transfers between devices, scatter(): lax.ppermute(bundle, 'seq', [(source, members[0])])  2.78 us
  transfers between devices with their start and end apart: 9, of which 1 were waited for; matrix products, arithmetic and copies ran while one was open for 0% of the time, Pallas kernels for 39%

profile of v6, /device:TPU:0, one launch (start us, length us, event | category | flops | bytes accessed | tf_op | source)
XLA Modules:
  0.0 128.5 jit_solution(6093533650617618315)
XLA Ops:
  0.0 0.0 copy-start
  0.0 1.6 %copy-done = bf16[1024,1024]{1,0:T(8,128)(2,1)S(1)} copy-done((bf16[1024,1024]{1,0:T(8,128)(2,1)S(1)}, bf16[1024,1024]{1,0:T(8,128)(2,1)}, u32[]{:S(2)}) %copy-start) | copy-done | bytes 2097176
  1.6 0.1 pack.1
  1.7 0.7 collective-permute-start
  2.4 0.7 collective-permute-start.1
  3.1 0.7 collective-permute-start.2
  3.9 0.7 collective-permute-start.3
  4.6 9.3 %project_kv.1 = (bf16[1024,1024]{1,0:T(8,128)(2,1)}, bf16[1024,1024]{1,0:T(8,128)(2,1)}) custom-call(bf16[1024,1024]{1,0:T(8,128)(2,1)} %tokens.3, f32[1,1024]{1,0:T(1,128)} %bitcast.7, bf16[1024,1024]{1,0:T(8,128)(2,1)} %w_key.1, bf16[1024,1024]{1,0:T(8,128)(2,1)} %w_value.1), custom_call_target="tpu_custom_call" | custom-call | flops 4294967296 | bytes 10485760 | tf_op jit(solution)/shard_map/project_kv/pallas_call | solution.py:47
  13.8 0.0 copy-start.1
  13.8 0.0 copy-start.3
  13.8 0.0 collective-permute-done.refs_0_
  13.8 0.0 collective-permute-done.1.refs_1_
  13.9 0.0 collective-permute-done.2.refs_2_
  13.9 0.0 collective-permute-done.3.refs_3_
  13.9 0.3 relay.1
  14.1 1.4 %collective-permute-start.4 = (bf16[64,1024]{1,0:T(8,128)(2,1)S(1)}, bf16[64,1024]{1,0:T(8,128)(2,1)S(1)}, u32[]{:S(2)}, u32[]{:S(2)}) collective-permute-start(bf16[64,1024]{1,0:T(8,128)(2,1)S(1)} %get-tuple-element.37), channel_id=1, source_target_pairs={{3,0},{11,8},{12,13},{14,6},{19,16},{27,24},{28,29},{30,22},{35,32... | collective-permute-start | bytes 393224 | tf_op jit(solution)/shard_map/ppermute | solution.py:285
  15.6 0.7 collective-permute-start.5
  16.2 0.7 collective-permute-start.6
  16.9 10.2 %collective-permute-done.4.refs_2_ = bf16[64,1024]{1,0:T(8,128)(2,1)S(1)} collective-permute-done((bf16[64,1024]{1,0:T(8,128)(2,1)S(1)}, bf16[64,1024]{1,0:T(8,128)(2,1)S(1)}, u32[]{:S(2)}, u32[]{:S(2)}) %collective-permute-start.4) | collective-permute-done | bytes 131104 | tf_op jit(solution)/shard_map/ppermute | solution.py:285
  27.1 0.0 collective-permute-done.5.refs_3_
  27.1 0.0 collective-permute-done.6.refs_4_
  27.1 0.0 copy-done.1
  27.1 0.0 copy-done.3
  27.2 1.7 %project_queries.1 = (bf16[64,1024]{1,0:T(8,128)(2,1)S(1)}, bf16[16,32,1024]{2,1,0:T(8,128)(2,1)S(1)}, bf16[16,32,1024]{2,1,0:T(8,128)(2,1)}) custom-call(f32[1,1024]{1,0:T(1,128)S(1)} %bitcast.8, bf16[1024,1024]{1,0:T(8,128)(2,1)S(1)} %copy-done.1, bf16[64,1024]{1,0:T(8,128)(2,1)S(1)} %get-tuple-element.26.refs_0_, ...), custom_call_target="tpu_custom_call" | custom-call | flops 134217728 | bytes 4194304 | tf_op jit(solution)/shard_map/project_queries/pallas_call | solution.py:88
  28.9 24.8 %all_to_all.20 = bf16[16,32,1024]{2,1,0:T(8,128)(2,1)} all-to-all(bf16[16,32,1024]{2,1,0:T(8,128)(2,1)S(1)} %get-tuple-element.40), channel_id=1, replica_groups=mesh['ctx'=8,'seq'=16] {'seq'}, dimensions={0} | all-to-all | bytes 2097152 | tf_op jit(solution)/shard_map/all_to_all | solution.py:298
  53.7 3.7 %all-to-all-start.2 = ((bf16[16,32,1024]{2,1,0:T(8,128)(2,1)}), bf16[16,32,1024]{2,1,0:T(8,128)(2,1)S(1)}, u32[]{:S(2)}, u32[]{:S(2)}) async-start(bf16[16,32,1024]{2,1,0:T(8,128)(2,1)} %get-tuple-element.44), calls=%async_computation.2 | async-start | bytes 2097152 | tf_op jit(solution)/shard_map/all_to_all | solution.py:300
  57.3 14.4 %attend_0.1 = bf16[512,1152]{1,0:T(8,128)(2,1)} custom-call(s32[1]{0:T(128)} %bitcast.flag, bf16[512,1024]{1,0:T(8,128)(2,1)} %bitcast.13, bf16[1024,1024]{1,0:T(8,128)(2,1)} %get-tuple-element.31.refs_0_.refs_1_.refs_2_.refs_3_, bf16[1024,1024]{1,0:T(8,128)(2,1)} %get-tuple-element.31.refs_0_.refs_1_.refs_2_.refs_3_, ...), custom_call_target="tpu_custom_call" | custom-call | flops 8589934592 | bytes 8388608 | tf_op jit(solution)/shard_map/attend_0/pallas_call | solution.py:176
  71.7 0.0 all-to-all-done.2
  71.7 0.0 copy-start.5
  71.7 7.2 %all-to-all-start.1 = ((bf16[16,32,1152]{2,1,0:T(8,128)(2,1)}), bf16[16,32,1152]{2,1,0:T(8,128)(2,1)S(1)}, u32[]{:S(2)}, u32[]{:S(2)}) async-start(bf16[16,32,1152]{2,1,0:T(8,128)(2,1)} %bitcast.10), calls=%async_computation.1 | async-start | bytes 2359296 | tf_op jit(solution)/shard_map/all_to_all | solution.py:304
  78.9 0.0 copy-done.5
  78.9 25.9 %attend_1.1 = bf16[512,1152]{1,0:T(8,128)(2,1)} custom-call(s32[1]{0:T(128)} %bitcast.flag, bf16[512,1024]{1,0:T(8,128)(2,1)} %bitcast.12, bf16[1024,1024]{1,0:T(8,128)(2,1)} %get-tuple-element.31.refs_0_.refs_1_.refs_2_.refs_3_, bf16[1024,1024]{1,0:T(8,128)(2,1)} %get-tuple-element.31.refs_0_.refs_1_.refs_2_.refs_3_, ...), custom_call_target="tpu_custom_call" | custom-call | flops 8589934592 | bytes 8388608 | tf_op jit(solution)/shard_map/attend_1/pallas_call | solution.py:176
  104.7 0.0 copy-start.2
  104.7 0.0 copy-start.4
  104.7 0.0 all-to-all-done.1.refs_0_
  104.8 21.4 %all_to_all.21.refs_1_ = bf16[16,32,1152]{2,1,0:T(8,128)(2,1)S(1)} all-to-all(bf16[16,32,1152]{2,1,0:T(8,128)(2,1)} %bitcast.11), channel_id=1, replica_groups=mesh['ctx'=8,'seq'=16] {'seq'}, dimensions={0} | all-to-all | bytes 2359296 | tf_op jit(solution)/shard_map/all_to_all | solution.py:304
  126.2 0.0 copy-done.2
  126.2 0.0 copy-done.4
  126.2 2.1 %finish.1 = bf16[64,1024]{1,0:T(8,128)(2,1)} custom-call(bf16[16,32,1152]{2,1,0:T(8,128)(2,1)S(1)} %all-to-all-done.1.refs_0_, bf16[16,32,1152]{2,1,0:T(8,128)(2,1)S(1)} %all_to_all.21.refs_1_, bf16[64,1024]{1,0:T(8,128)(2,1)S(1)} %get-tuple-element.46.refs_2_, f32[1,1024]{1,0:T(1,128)S(1)} %bitcast.9, bf16[1024,1024]{1,0:T(8,128)(2,1)S(1)} %copy-done.2), custom_call_target="tpu_custom_call" | custom-call | flops 268435456 | bytes 8388608 | tf_op jit(solution)/shard_map/finish/pallas_call | solution.py:226
Async XLA Ops:
  0.0 1.6 %copy-start = (bf16[1024,1024]{1,0:T(8,128)(2,1)S(1)}, bf16[1024,1024]{1,0:T(8,128)(2,1)}, u32[]{:S(2)}) copy-start(bf16[1024,1024]{1,0:T(8,128)(2,1)} %tokens.3) | copy-start | bytes 6291460
  1.7 12.1 %collective-permute-start = (bf16[256,1024]{1,0:T(8,128)(2,1)S(1)}, bf16[256,1024]{1,0:T(8,128)(2,1)S(1)}, u32[]{:S(2)}, u32[]{:S(2)}) collective-permute-start(bf16[256,1024]{1,0:T(8,128)(2,1)S(1)} %get-tuple-element.27), channel_id=1, source_target_pairs={{15,3},{31,19},{47,35},{63,51},{79,67},{95,83},{111,99},{127,115}} | collective-permute-start | bytes 1572872 | tf_op jit(solution)/shard_map/ppermute | solution.py:272
  2.4 11.4 %collective-permute-start.1 = (bf16[256,1024]{1,0:T(8,128)(2,1)S(1)}, bf16[256,1024]{1,0:T(8,128)(2,1)S(1)}, u32[]{:S(2)}, u32[]{:S(2)}) collective-permute-start(bf16[256,1024]{1,0:T(8,128)(2,1)S(1)} %get-tuple-element.28), channel_id=1, source_target_pairs={{15,11},{31,27},{47,43},{63,59},{79,75},{95,91},{111,107},{127,123}} | collective-permute-start | bytes 1572872 | tf_op jit(solution)/shard_map/ppermute | solution.py:272
  3.1 10.7 %collective-permute-start.2 = (bf16[256,1024]{1,0:T(8,128)(2,1)S(1)}, bf16[256,1024]{1,0:T(8,128)(2,1)S(1)}, u32[]{:S(2)}, u32[]{:S(2)}) collective-permute-start(bf16[256,1024]{1,0:T(8,128)(2,1)S(1)} %get-tuple-element.29), channel_id=1, source_target_pairs={{15,12},{31,28},{47,44},{63,60},{79,76},{95,92},{111,108},{127,124}} | collective-permute-start | bytes 1572872 | tf_op jit(solution)/shard_map/ppermute | solution.py:272
  3.9 10.0 %collective-permute-start.3 = (bf16[256,1024]{1,0:T(8,128)(2,1)S(1)}, bf16[256,1024]{1,0:T(8,128)(2,1)S(1)}, u32[]{:S(2)}, u32[]{:S(2)}) collective-permute-start(bf16[256,1024]{1,0:T(8,128)(2,1)S(1)} %get-tuple-element.30), channel_id=1, source_target_pairs={{15,14},{31,30},{47,46},{63,62},{79,78},{95,94},{111,110},{127,126}} | collective-permute-start | bytes 1572872 | tf_op jit(solution)/shard_map/ppermute | solution.py:272
  13.8 13.3 %copy-start.1 = (bf16[1024,1024]{1,0:T(8,128)(2,1)S(1)}, bf16[1024,1024]{1,0:T(8,128)(2,1)}, u32[]{:S(2)}) copy-start(bf16[1024,1024]{1,0:T(8,128)(2,1)} %w_query.1) | copy-start | bytes 6291460
  13.8 13.3 %copy-start.3 = (f32[1024]{0:T(1024)S(1)}, f32[1024]{0:T(1024)}, u32[]{:S(2)}) copy-start(f32[1024]{0:T(1024)} %param.8) | copy-start | bytes 12292
  14.1 13.0 %collective-permute-start.4 = (bf16[64,1024]{1,0:T(8,128)(2,1)S(1)}, bf16[64,1024]{1,0:T(8,128)(2,1)S(1)}, u32[]{:S(2)}, u32[]{:S(2)}) collective-permute-start(bf16[64,1024]{1,0:T(8,128)(2,1)S(1)} %get-tuple-element.37), channel_id=1, source_target_pairs={{3,0},{11,8},{12,13},{14,6},{19,16},{27,24},{28,29},{30,22},{35,32... | collective-permute-start | bytes 393224 | tf_op jit(solution)/shard_map/ppermute | solution.py:285
  15.6 11.6 %collective-permute-start.5 = (bf16[64,1024]{1,0:T(8,128)(2,1)S(1)}, bf16[64,1024]{1,0:T(8,128)(2,1)S(1)}, u32[]{:S(2)}, u32[]{:S(2)}) collective-permute-start(bf16[64,1024]{1,0:T(8,128)(2,1)S(1)} %get-tuple-element.38), channel_id=1, source_target_pairs={{3,2},{11,10},{12,4},{14,7},{19,18},{27,26},{28,20},{30,23},{35,34... | collective-permute-start | bytes 393224 | tf_op jit(solution)/shard_map/ppermute | solution.py:285
  16.2 10.9 %collective-permute-start.6 = (bf16[64,1024]{1,0:T(8,128)(2,1)S(1)}, bf16[64,1024]{1,0:T(8,128)(2,1)S(1)}, u32[]{:S(2)}, u32[]{:S(2)}) collective-permute-start(bf16[64,1024]{1,0:T(8,128)(2,1)S(1)} %get-tuple-element.39), channel_id=1, source_target_pairs={{3,1},{11,9},{12,5},{19,17},{27,25},{28,21},{35,33},{43,41},{44,37... | collective-permute-start | bytes 393224 | tf_op jit(solution)/shard_map/ppermute | solution.py:285
  53.7 18.0 %all-to-all-start.2 = ((bf16[16,32,1024]{2,1,0:T(8,128)(2,1)}), bf16[16,32,1024]{2,1,0:T(8,128)(2,1)S(1)}, u32[]{:S(2)}, u32[]{:S(2)}) async-start(bf16[16,32,1024]{2,1,0:T(8,128)(2,1)} %get-tuple-element.44), calls=%async_computation.2 | async-start | bytes 2097152 | tf_op jit(solution)/shard_map/all_to_all | solution.py:300
  71.7 7.2 %copy-start.5 = (bf16[16,32,1024]{2,1,0:T(8,128)(2,1)}, bf16[16,32,1024]{2,1,0:T(8,128)(2,1)S(1)}, u32[]{:S(2)}) copy-start(bf16[16,32,1024]{2,1,0:T(8,128)(2,1)S(1)} %all-to-all-done.2) | copy-start | bytes 3145732
  71.7 33.1 %all-to-all-start.1 = ((bf16[16,32,1152]{2,1,0:T(8,128)(2,1)}), bf16[16,32,1152]{2,1,0:T(8,128)(2,1)S(1)}, u32[]{:S(2)}, u32[]{:S(2)}) async-start(bf16[16,32,1152]{2,1,0:T(8,128)(2,1)} %bitcast.10), calls=%async_computation.1 | async-start | bytes 2359296 | tf_op jit(solution)/shard_map/all_to_all | solution.py:304
  104.7 21.5 %copy-start.2 = (bf16[1024,1024]{1,0:T(8,128)(2,1)S(1)}, bf16[1024,1024]{1,0:T(8,128)(2,1)}, u32[]{:S(2)}) copy-start(bf16[1024,1024]{1,0:T(8,128)(2,1)} %refs_4_.1) | copy-start | bytes 6291460
  104.7 21.5 %copy-start.4 = (f32[1024]{0:T(1024)S(1)}, f32[1024]{0:T(1024)}, u32[]{:S(2)}) copy-start(f32[1024]{0:T(1024)} %param.9) | copy-start | bytes 12292

commit v7 on v6

--- a/solution.py
+++ b/solution.py
@@ -35,8 +35,8 @@
         normed[...] = rms_rows(tokens[...], gain[...])
 
     rows = normed[...]
-    keys[...] = jnp.dot(rows, w_key[...], preferred_element_type=jnp.float32).T.astype(jnp.bfloat16)
-    values[...] = jnp.dot(rows, w_value[...], preferred_element_type=jnp.float32).astype(jnp.bfloat16)
+    keys[...] = jnp.dot(rows, w_key[...], preferred_element_type=jnp.float32).astype(jnp.bfloat16)
+    values[...] = jnp.dot(rows, w_value[...], preferred_element_type=jnp.float32).T.astype(jnp.bfloat16)
 
 
 def project_kv(tokens, gain, w_key, w_value):
@@ -48,8 +48,8 @@
         kv_kernel,
         grid=(D // cols,),
         out_shape=(
+            jax.ShapeDtypeStruct((rows, D), jnp.bfloat16),
             jax.ShapeDtypeStruct((D, rows), jnp.bfloat16),
-            jax.ShapeDtypeStruct((rows, D), jnp.bfloat16),
         ),
         in_specs=[
             pl.BlockSpec((rows, D), whole, pipeline_mode=pl.Buffered(1)),
@@ -57,7 +57,7 @@
             pl.BlockSpec((D, cols), block),
             pl.BlockSpec((D, cols), block),
         ],
-        out_specs=(pl.BlockSpec((cols, rows), lambda c: (c, 0)), pl.BlockSpec((rows, cols), block)),
+        out_specs=(pl.BlockSpec((rows, cols), block), pl.BlockSpec((cols, rows), lambda c: (c, 0))),
         scratch_shapes=[pltpu.VMEM((rows, D), jnp.bfloat16)],
         compiler_params=pltpu.CompilerParams(vmem_limit_bytes=56 * MIB),
         cost_estimate=pl.CostEstimate(flops=4 * rows * D * D, bytes_accessed=10 * rows * D, transcendentals=0),
@@ -98,56 +98,55 @@
 def attend_kernel(chunk, owned, flag, queries, *refs):
     keys, values, out = refs[:SPLIT], refs[SPLIT : 2 * SPLIT], refs[-1]
     rows = queries.shape[0]
-    count = values[0].shape[0]
+    count = keys[0].shape[0]
     step = pl.program_id(0)
     pairs = HEADS // 2
     part = PART
     low = lax.broadcasted_iota(jnp.int32, (1, 128), 1) < HEAD_DIM
 
-    def place(pair):
-        begin = pair * 128 % (D // SPLIT)
-        return pair * 128 // (D // SPLIT), slice(begin, begin + 128)
-
     def attention(causal, count):
-        lane = lax.broadcasted_iota(jnp.int32, (rows, 128), 1)
-        lse = jnp.zeros((rows, 128), jnp.float32)
-        ones = jnp.ones((count, 128), jnp.bfloat16)
+        ones = jnp.ones((16, count), jnp.bfloat16)
         if causal:
-            key_pos = lax.broadcasted_iota(jnp.int32, (rows, count), 1)
-            row = step * rows + lax.broadcasted_iota(jnp.int32, (rows, count), 0)
+            key_pos = lax.broadcasted_iota(jnp.int32, (count, rows), 0)
+            row = step * rows + lax.broadcasted_iota(jnp.int32, (count, rows), 1)
             query_pos = (row // part) * owned + chunk * part + row % part
             allowed = key_pos <= query_pos
-            allowed = jnp.concatenate([allowed, allowed], axis=0)
+            allowed = jnp.concatenate([allowed, allowed], axis=1)
 
         def scores_of(pair):
-            at = slice(pair * 128, (pair + 1) * 128)
-            query = queries[:, at]
+            query = queries[:, pair * 128 : (pair + 1) * 128]
             none = jnp.zeros_like(query)
             both = jnp.concatenate([jnp.where(low, query, none), jnp.where(low, none, query)], axis=0)
-            block, features = place(pair)
-            scores = jnp.dot(both, keys[block][features, 0:count], preferred_element_type=jnp.float32)
+            begin = pair * 128 % (D // SPLIT)
+            key = keys[pair * 128 // (D // SPLIT)][0:count, begin : begin + 128]
+            scores = lax.dot_general(key, both, (((1,), (1,)), ((), ())), preferred_element_type=jnp.float32)
             return jnp.where(allowed, scores, MASKED) if causal else scores
 
+        levels = []
         ahead = scores_of(0)
         for pair in range(pairs):
-            at = slice(pair * 128, (pair + 1) * 128)
             scores = ahead
             if pair + 1 < pairs:
                 ahead = scores_of(pair + 1)
-            block, features = place(pair)
-            top = jnp.max(scores, axis=-1, keepdims=True)
+            top = jnp.max(scores, axis=0, keepdims=True)
             weights = jnp.exp2((scores - top) * EXP2_SCALE).astype(jnp.bfloat16)
-            mixed = jnp.dot(
-                weights,
-                jnp.concatenate([values[block][0:count, features], ones], axis=1),
-                preferred_element_type=jnp.float32,
-            )
-            mix, total = mixed[:, 0:128], mixed[:, 128:256]
-            both = jnp.where(low, mix[:rows], mix[rows:]) / jnp.where(low, total[:rows], total[rows:])
-            out[:, at] = both.astype(jnp.bfloat16)
-            level = top * EXP2_SCALE + jnp.log2(total)
-            lse = jnp.where(lane == 2 * pair, level[:rows], lse)
-            lse = jnp.where(lane == 2 * pair + 1, level[rows:], lse)
+            halves = []
+            for half in range(2):
+                begin = (pair * 128 + half * HEAD_DIM) % (D // SPLIT)
+                value = values[pair * 128 // (D // SPLIT)][begin : begin + HEAD_DIM, 0:count]
+                across = slice(half * rows, (half + 1) * rows)
+                mixed = jnp.dot(
+                    jnp.concatenate([value, ones], axis=0),
+                    weights[:, across],
+                    preferred_element_type=jnp.float32,
+                )
+                total = mixed[HEAD_DIM : HEAD_DIM + 1]
+                halves.append(mixed[:HEAD_DIM] / total)
+                levels.append(top[:, across] * EXP2_SCALE + jnp.log2(total))
+            mix = jnp.concatenate(halves, axis=0).T
+            out[:, pair * 128 : (pair + 1) * 128] = mix.astype(jnp.bfloat16)
+        levels.append(jnp.zeros((128 - HEADS, rows), jnp.float32))
+        lse = jnp.concatenate(levels, axis=0).T
         first = lse.astype(jnp.bfloat16).astype(jnp.float32)
         second = (lse - first).astype(jnp.bfloat16).astype(jnp.float32)
         third = lse - first - second
@@ -170,8 +169,8 @@
 def attend(chunk, owned, is_last, queries, keys, values):
     count = queries.shape[0]
     rows = 256
-    key_block = lambda i, c: (i, 0)
-    value_block = lambda i, c: (0, i)
+    key_block = lambda i, c: (0, i)
+    value_block = lambda i, c: (i, 0)
     block = lambda c: (c, 0)
     return pl.pallas_call(
         functools.partial(attend_kernel, chunk, owned),
@@ -181,8 +180,8 @@
             pl.BlockSpec(memory_space=pltpu.SMEM),
             pl.BlockSpec((rows, D), block),
         ]
-        + [pl.BlockSpec((D // SPLIT, keys.shape[1]), functools.partial(key_block, i)) for i in range(SPLIT)]
-        + [pl.BlockSpec((values.shape[0], D // SPLIT), functools.partial(value_block, i)) for i in range(SPLIT)],
+        + [pl.BlockSpec((keys.shape[0], D // SPLIT), functools.partial(key_block, i)) for i in range(SPLIT)]
+        + [pl.BlockSpec((D // SPLIT, values.shape[1]), functools.partial(value_block, i)) for i in range(SPLIT)],
         out_specs=pl.BlockSpec((rows, WIDE), block),
         compiler_params=pltpu.CompilerParams(vmem_limit_bytes=56 * MIB),
         cost_estimate=pl.CostEstimate(

time: 127 us -> 120 us (0.945); the launches traced: 128 us -> 119 us
  Pallas kernels: 53.7 us -> 44.6 us
    pallas_call x2, Pallas kernels: 40.2 us -> 31.1 us  [attend(): pl.pallas_call(functools.partial(attend_kernel, chunk, owned), grid=(coun...]
  transfers between devices with their start and end apart: 9 -> 9, of which waited for: 1 -> 1; matrix products, arithmetic and copies ran while one was open for 0% -> 0% of each run, Pallas kernels for 39% -> 34%
where the time goes in v7:
time: 120 us; the launch traced here: 119 us
  blocking collectives  46.2 us (38%)
  Pallas kernels  44.6 us (37%)
  starting transfers between devices  16.3 us (14%)
  waiting for transfers between devices  10.2 us (8%)
  local copies, waits for them, and re-layouts  1.61 us (1%)
    pallas_call x2, Pallas kernels, attend(): pl.pallas_call(functools.partial(attend_kernel, chunk, owned), grid=(coun...  31.1 us
    all_to_all x1, blocking collectives, local(): rows_a = lax.all_to_all(tiled_a, 'seq', 0, 0)  24.8 us
    all_to_all x1, blocking collectives, local(): lax.all_to_all(each.reshape(count, PART, WIDE), 'seq', 0, 0)  21.5 us
    ppermute x3, waiting for transfers between devices, scatter(): parts.append(lax.ppermute(passed[place - 1], 'seq', pairs))  10.2 us
    pallas_call x1, Pallas kernels, project_kv(): pl.pallas_call(kv_kernel, grid=(D // cols,), out_shape=(jax.ShapeDtypeStr...  9.28 us
    all_to_all x1, starting transfers between devices, local(): lax.all_to_all(each.reshape(count, PART, WIDE), 'seq', 0, 0)  7.15 us
    all_to_all x1, starting transfers between devices, local(): rows_b = lax.all_to_all(tiled_b, 'seq', 0, 0)  3.65 us
    ppermute x4, starting transfers between devices, scatter(): lax.ppermute(bundle, 'seq', [(source, members[0])])  2.78 us
  transfers between devices with their start and end apart: 9, of which 1 were waited for; matrix products, arithmetic and copies ran while one was open for 0% of the time, Pallas kernels for 34%

profile of v7, /device:TPU:0, one launch (start us, length us, event | category | flops | bytes accessed | tf_op | source)
XLA Modules:
  0.0 119.2 jit_solution(3119009656047961303)
XLA Ops:
  0.0 0.0 copy-start
  0.0 1.6 %copy-done = bf16[1024,1024]{1,0:T(8,128)(2,1)S(1)} copy-done((bf16[1024,1024]{1,0:T(8,128)(2,1)S(1)}, bf16[1024,1024]{1,0:T(8,128)(2,1)}, u32[]{:S(2)}) %copy-start) | copy-done | bytes 2097176
  1.6 0.1 pack.1
  1.7 0.7 collective-permute-start
  2.4 0.7 collective-permute-start.1
  3.1 0.7 collective-permute-start.2
  3.9 0.7 collective-permute-start.3
  4.6 9.3 %project_kv.1 = (bf16[1024,1024]{1,0:T(8,128)(2,1)}, bf16[1024,1024]{1,0:T(8,128)(2,1)}) custom-call(bf16[1024,1024]{1,0:T(8,128)(2,1)} %tokens.3, f32[1,1024]{1,0:T(1,128)} %bitcast.7, bf16[1024,1024]{1,0:T(8,128)(2,1)} %w_key.1, bf16[1024,1024]{1,0:T(8,128)(2,1)} %w_value.1), custom_call_target="tpu_custom_call" | custom-call | flops 4294967296 | bytes 10485760 | tf_op jit(solution)/shard_map/project_kv/pallas_call | solution.py:47
  13.8 0.0 copy-start.1
  13.8 0.0 copy-start.3
  13.8 0.0 collective-permute-done.refs_0_
  13.8 0.0 collective-permute-done.1.refs_1_
  13.9 0.0 collective-permute-done.2.refs_2_
  13.9 0.0 collective-permute-done.3.refs_3_
  13.9 0.3 relay.1
  14.1 1.4 %collective-permute-start.4 = (bf16[64,1024]{1,0:T(8,128)(2,1)S(1)}, bf16[64,1024]{1,0:T(8,128)(2,1)S(1)}, u32[]{:S(2)}, u32[]{:S(2)}) collective-permute-start(bf16[64,1024]{1,0:T(8,128)(2,1)S(1)} %get-tuple-element.37), channel_id=1, source_target_pairs={{3,0},{11,8},{12,13},{14,6},{19,16},{27,24},{28,29},{30,22},{35,32... | collective-permute-start | bytes 393224 | tf_op jit(solution)/shard_map/ppermute | solution.py:284
  15.6 0.7 collective-permute-start.5
  16.3 0.7 collective-permute-start.6
  16.9 10.2 %collective-permute-done.4.refs_2_ = bf16[64,1024]{1,0:T(8,128)(2,1)S(1)} collective-permute-done((bf16[64,1024]{1,0:T(8,128)(2,1)S(1)}, bf16[64,1024]{1,0:T(8,128)(2,1)S(1)}, u32[]{:S(2)}, u32[]{:S(2)}) %collective-permute-start.4) | collective-permute-done | bytes 131104 | tf_op jit(solution)/shard_map/ppermute | solution.py:284
  27.1 0.0 collective-permute-done.5.refs_3_
  27.1 0.0 collective-permute-done.6.refs_4_
  27.1 0.0 copy-done.1
  27.1 0.0 copy-done.3
  27.2 1.7 %project_queries.1 = (bf16[64,1024]{1,0:T(8,128)(2,1)S(1)}, bf16[16,32,1024]{2,1,0:T(8,128)(2,1)S(1)}, bf16[16,32,1024]{2,1,0:T(8,128)(2,1)}) custom-call(f32[1,1024]{1,0:T(1,128)S(1)} %bitcast.8, bf16[1024,1024]{1,0:T(8,128)(2,1)S(1)} %copy-done.1, bf16[64,1024]{1,0:T(8,128)(2,1)S(1)} %get-tuple-element.26.refs_0_, ...), custom_call_target="tpu_custom_call" | custom-call | flops 134217728 | bytes 4194304 | tf_op jit(solution)/shard_map/project_queries/pallas_call | solution.py:88
  28.9 24.8 %all_to_all.20 = bf16[16,32,1024]{2,1,0:T(8,128)(2,1)} all-to-all(bf16[16,32,1024]{2,1,0:T(8,128)(2,1)S(1)} %get-tuple-element.40), channel_id=1, replica_groups=mesh['ctx'=8,'seq'=16] {'seq'}, dimensions={0} | all-to-all | bytes 2097152 | tf_op jit(solution)/shard_map/all_to_all | solution.py:297
  53.7 3.7 %all-to-all-start.2 = ((bf16[16,32,1024]{2,1,0:T(8,128)(2,1)}), bf16[16,32,1024]{2,1,0:T(8,128)(2,1)S(1)}, u32[]{:S(2)}, u32[]{:S(2)}) async-start(bf16[16,32,1024]{2,1,0:T(8,128)(2,1)} %get-tuple-element.44), calls=%async_computation.2 | async-start | bytes 2097152 | tf_op jit(solution)/shard_map/all_to_all | solution.py:299
  57.3 15.5 %attend_0.1 = bf16[512,1152]{1,0:T(8,128)(2,1)} custom-call(s32[1]{0:T(128)} %bitcast.flag, bf16[512,1024]{1,0:T(8,128)(2,1)} %bitcast.13, bf16[1024,1024]{1,0:T(8,128)(2,1)} %get-tuple-element.31.refs_0_.refs_1_.refs_2_.refs_3_, bf16[1024,1024]{1,0:T(8,128)(2,1)} %get-tuple-element.31.refs_0_.refs_1_.refs_2_.refs_3_, ...), custom_call_target="tpu_custom_call" | custom-call | flops 8589934592 | bytes 8388608 | tf_op jit(solution)/shard_map/attend_0/pallas_call | solution.py:175
  72.9 0.0 all-to-all-done.2
  72.9 0.0 copy-start.5
  72.9 7.2 %all-to-all-start.1 = ((bf16[16,32,1152]{2,1,0:T(8,128)(2,1)}), bf16[16,32,1152]{2,1,0:T(8,128)(2,1)S(1)}, u32[]{:S(2)}, u32[]{:S(2)}) async-start(bf16[16,32,1152]{2,1,0:T(8,128)(2,1)} %bitcast.10), calls=%async_computation.1 | async-start | bytes 2359296 | tf_op jit(solution)/shard_map/all_to_all | solution.py:303
  80.0 0.0 copy-done.5
  80.0 15.6 %attend_1.1 = bf16[512,1152]{1,0:T(8,128)(2,1)} custom-call(s32[1]{0:T(128)} %bitcast.flag, bf16[512,1024]{1,0:T(8,128)(2,1)} %bitcast.12, bf16[1024,1024]{1,0:T(8,128)(2,1)} %get-tuple-element.31.refs_0_.refs_1_.refs_2_.refs_3_, bf16[1024,1024]{1,0:T(8,128)(2,1)} %get-tuple-element.31.refs_0_.refs_1_.refs_2_.refs_3_, ...), custom_call_target="tpu_custom_call" | custom-call | flops 8589934592 | bytes 8388608 | tf_op jit(solution)/shard_map/attend_1/pallas_call | solution.py:175
  95.6 0.0 copy-start.2
  95.6 0.0 copy-start.4
  95.6 0.0 all-to-all-done.1.refs_0_
  95.6 21.5 %all_to_all.21.refs_1_ = bf16[16,32,1152]{2,1,0:T(8,128)(2,1)S(1)} all-to-all(bf16[16,32,1152]{2,1,0:T(8,128)(2,1)} %bitcast.11), channel_id=1, replica_groups=mesh['ctx'=8,'seq'=16] {'seq'}, dimensions={0} | all-to-all | bytes 2359296 | tf_op jit(solution)/shard_map/all_to_all | solution.py:303
  117.1 0.0 copy-done.2
  117.1 0.0 copy-done.4
  117.1 2.1 %finish.1 = bf16[64,1024]{1,0:T(8,128)(2,1)} custom-call(bf16[16,32,1152]{2,1,0:T(8,128)(2,1)S(1)} %all-to-all-done.1.refs_0_, bf16[16,32,1152]{2,1,0:T(8,128)(2,1)S(1)} %all_to_all.21.refs_1_, bf16[64,1024]{1,0:T(8,128)(2,1)S(1)} %get-tuple-element.46.refs_2_, f32[1,1024]{1,0:T(1,128)S(1)} %bitcast.9, bf16[1024,1024]{1,0:T(8,128)(2,1)S(1)} %copy-done.2), custom_call_target="tpu_custom_call" | custom-call | flops 268435456 | bytes 8388608 | tf_op jit(solution)/shard_map/finish/pallas_call | solution.py:225
Async XLA Ops:
  0.0 1.6 %copy-start = (bf16[1024,1024]{1,0:T(8,128)(2,1)S(1)}, bf16[1024,1024]{1,0:T(8,128)(2,1)}, u32[]{:S(2)}) copy-start(bf16[1024,1024]{1,0:T(8,128)(2,1)} %tokens.3) | copy-start | bytes 6291460
  1.7 12.1 %collective-permute-start = (bf16[256,1024]{1,0:T(8,128)(2,1)S(1)}, bf16[256,1024]{1,0:T(8,128)(2,1)S(1)}, u32[]{:S(2)}, u32[]{:S(2)}) collective-permute-start(bf16[256,1024]{1,0:T(8,128)(2,1)S(1)} %get-tuple-element.27), channel_id=1, source_target_pairs={{15,3},{31,19},{47,35},{63,51},{79,67},{95,83},{111,99},{127,115}} | collective-permute-start | bytes 1572872 | tf_op jit(solution)/shard_map/ppermute | solution.py:271
  2.4 11.4 %collective-permute-start.1 = (bf16[256,1024]{1,0:T(8,128)(2,1)S(1)}, bf16[256,1024]{1,0:T(8,128)(2,1)S(1)}, u32[]{:S(2)}, u32[]{:S(2)}) collective-permute-start(bf16[256,1024]{1,0:T(8,128)(2,1)S(1)} %get-tuple-element.28), channel_id=1, source_target_pairs={{15,11},{31,27},{47,43},{63,59},{79,75},{95,91},{111,107},{127,123}} | collective-permute-start | bytes 1572872 | tf_op jit(solution)/shard_map/ppermute | solution.py:271
  3.1 10.7 %collective-permute-start.2 = (bf16[256,1024]{1,0:T(8,128)(2,1)S(1)}, bf16[256,1024]{1,0:T(8,128)(2,1)S(1)}, u32[]{:S(2)}, u32[]{:S(2)}) collective-permute-start(bf16[256,1024]{1,0:T(8,128)(2,1)S(1)} %get-tuple-element.29), channel_id=1, source_target_pairs={{15,12},{31,28},{47,44},{63,60},{79,76},{95,92},{111,108},{127,124}} | collective-permute-start | bytes 1572872 | tf_op jit(solution)/shard_map/ppermute | solution.py:271
  3.9 10.0 %collective-permute-start.3 = (bf16[256,1024]{1,0:T(8,128)(2,1)S(1)}, bf16[256,1024]{1,0:T(8,128)(2,1)S(1)}, u32[]{:S(2)}, u32[]{:S(2)}) collective-permute-start(bf16[256,1024]{1,0:T(8,128)(2,1)S(1)} %get-tuple-element.30), channel_id=1, source_target_pairs={{15,14},{31,30},{47,46},{63,62},{79,78},{95,94},{111,110},{127,126}} | collective-permute-start | bytes 1572872 | tf_op jit(solution)/shard_map/ppermute | solution.py:271
  13.8 13.3 %copy-start.1 = (bf16[1024,1024]{1,0:T(8,128)(2,1)S(1)}, bf16[1024,1024]{1,0:T(8,128)(2,1)}, u32[]{:S(2)}) copy-start(bf16[1024,1024]{1,0:T(8,128)(2,1)} %w_query.1) | copy-start | bytes 6291460
  13.8 13.3 %copy-start.3 = (f32[1024]{0:T(1024)S(1)}, f32[1024]{0:T(1024)}, u32[]{:S(2)}) copy-start(f32[1024]{0:T(1024)} %param.8) | copy-start | bytes 12292
  14.1 13.0 %collective-permute-start.4 = (bf16[64,1024]{1,0:T(8,128)(2,1)S(1)}, bf16[64,1024]{1,0:T(8,128)(2,1)S(1)}, u32[]{:S(2)}, u32[]{:S(2)}) collective-permute-start(bf16[64,1024]{1,0:T(8,128)(2,1)S(1)} %get-tuple-element.37), channel_id=1, source_target_pairs={{3,0},{11,8},{12,13},{14,6},{19,16},{27,24},{28,29},{30,22},{35,32... | collective-permute-start | bytes 393224 | tf_op jit(solution)/shard_map/ppermute | solution.py:284
  15.6 11.6 %collective-permute-start.5 = (bf16[64,1024]{1,0:T(8,128)(2,1)S(1)}, bf16[64,1024]{1,0:T(8,128)(2,1)S(1)}, u32[]{:S(2)}, u32[]{:S(2)}) collective-permute-start(bf16[64,1024]{1,0:T(8,128)(2,1)S(1)} %get-tuple-element.38), channel_id=1, source_target_pairs={{3,2},{11,10},{12,4},{14,7},{19,18},{27,26},{28,20},{30,23},{35,34... | collective-permute-start | bytes 393224 | tf_op jit(solution)/shard_map/ppermute | solution.py:284
  16.3 10.9 %collective-permute-start.6 = (bf16[64,1024]{1,0:T(8,128)(2,1)S(1)}, bf16[64,1024]{1,0:T(8,128)(2,1)S(1)}, u32[]{:S(2)}, u32[]{:S(2)}) collective-permute-start(bf16[64,1024]{1,0:T(8,128)(2,1)S(1)} %get-tuple-element.39), channel_id=1, source_target_pairs={{3,1},{11,9},{12,5},{19,17},{27,25},{28,21},{35,33},{43,41},{44,37... | collective-permute-start | bytes 393224 | tf_op jit(solution)/shard_map/ppermute | solution.py:284
  53.7 19.2 %all-to-all-start.2 = ((bf16[16,32,1024]{2,1,0:T(8,128)(2,1)}), bf16[16,32,1024]{2,1,0:T(8,128)(2,1)S(1)}, u32[]{:S(2)}, u32[]{:S(2)}) async-start(bf16[16,32,1024]{2,1,0:T(8,128)(2,1)} %get-tuple-element.44), calls=%async_computation.2 | async-start | bytes 2097152 | tf_op jit(solution)/shard_map/all_to_all | solution.py:299
  72.9 7.2 %copy-start.5 = (bf16[16,32,1024]{2,1,0:T(8,128)(2,1)}, bf16[16,32,1024]{2,1,0:T(8,128)(2,1)S(1)}, u32[]{:S(2)}) copy-start(bf16[16,32,1024]{2,1,0:T(8,128)(2,1)S(1)} %all-to-all-done.2) | copy-start | bytes 3145732
  72.9 22.8 %all-to-all-start.1 = ((bf16[16,32,1152]{2,1,0:T(8,128)(2,1)}), bf16[16,32,1152]{2,1,0:T(8,128)(2,1)S(1)}, u32[]{:S(2)}, u32[]{:S(2)}) async-start(bf16[16,32,1152]{2,1,0:T(8,128)(2,1)} %bitcast.10), calls=%async_computation.1 | async-start | bytes 2359296 | tf_op jit(solution)/shard_map/all_to_all | solution.py:303
  95.6 21.5 %copy-start.2 = (bf16[1024,1024]{1,0:T(8,128)(2,1)S(1)}, bf16[1024,1024]{1,0:T(8,128)(2,1)}, u32[]{:S(2)}) copy-start(bf16[1024,1024]{1,0:T(8,128)(2,1)} %refs_4_.1) | copy-start | bytes 6291460
  95.6 21.5 %copy-start.4 = (f32[1024]{0:T(1024)S(1)}, f32[1024]{0:T(1024)}, u32[]{:S(2)}) copy-start(f32[1024]{0:T(1024)} %param.9) | copy-start | bytes 12292

commit v8 on v6

--- a/solution.py
+++ b/solution.py
@@ -20,7 +20,7 @@
 WIDE = D + 128
 MIB = 2**20
 
-BUNDLES = ((3, 0, 2, 1), (11, 8, 10, 9), (12, 13, 4, 5), (14, 6, 7))
+BUNDLES = ((12, 0, 8, 13), (14, 2, 10), (3, 1, 5, 7), (11, 9, 4, 6))
 
 
 def rms_rows(rows, gain):
@@ -239,9 +239,8 @@
     mine = block(source)
     own[...] = jnp.where(flag[0] != 0, mine, jnp.zeros_like(mine))
     for members, bundle in zip(BUNDLES, bundles):
-        for place in range(4):
-            at = slice(place * owned, (place + 1) * owned)
-            bundle[at, :] = block(members[min(place, len(members) - 1)])
+        for place, member in enumerate(members):
+            bundle[place * owned : (place + 1) * owned, :] = block(member)
 
 
 def relay_kernel(*refs):
@@ -249,10 +248,8 @@
     rows = outs[0].shape[0]
     for place, out in enumerate(outs):
         at = slice(place * rows, (place + 1) * rows)
-        total = bundles[0][at, :].astype(jnp.float32)
-        for bundle in bundles[1:]:
-            total = total + bundle[at, :].astype(jnp.float32)
-        out[...] = total.astype(jnp.bfloat16)
+        held = [bundle[at, :].astype(jnp.float32) for bundle in bundles if place * rows < bundle.shape[0]]
+        out[...] = sum(held[1:], held[0]).astype(jnp.bfloat16)
 
 
 def scatter(tokens, owned, source, flag, beside):
@@ -262,7 +259,7 @@
     vmem = pl.BlockSpec(memory_space=pltpu.VMEM)
     own, *bundles = pl.pallas_call(
         functools.partial(pack_kernel, owned, source),
-        out_shape=(block,) + (jax.ShapeDtypeStruct((4 * owned, D), jnp.bfloat16),) * 4,
+        out_shape=(block,) + tuple(jax.ShapeDtypeStruct((len(members) * owned, D), jnp.bfloat16) for members in BUNDLES),
         in_specs=[smem, vmem],
         compiler_params=limit,
         cost_estimate=pl.CostEstimate(flops=0, bytes_accessed=8 * D * D, transcendentals=0),

time: 127 us -> 127 us (level)
  transfers between devices with their start and end apart: 9 -> 9, of which waited for: 1 -> 2; matrix products, arithmetic and copies ran while one was open for 0% -> 0% of each run, Pallas kernels for 39% -> 39%
where the time goes in v8:
time: 127 us; the launch traced here: 129 us
  Pallas kernels  53.8 us (42%)
  blocking collectives  47.1 us (37%)
  starting transfers between devices  16.1 us (13%)
  waiting for transfers between devices  9.52 us (7%)
  local copies, waits for them, and re-layouts  1.61 us (1%)
    pallas_call x2, Pallas kernels, attend(): pl.pallas_call(functools.partial(attend_kernel, chunk, owned), grid=(coun...  40.2 us
    all_to_all x1, blocking collectives, local(): rows_a = lax.all_to_all(tiled_a, 'seq', 0, 0)  25.2 us
    all_to_all x1, blocking collectives, local(): lax.all_to_all(each.reshape(count, PART, WIDE), 'seq', 0, 0)  22 us
    ppermute x3, waiting for transfers between devices, scatter(): parts.append(lax.ppermute(passed[place - 1], 'seq', pairs))  9.41 us
    pallas_call x1, Pallas kernels, project_kv(): pl.pallas_call(kv_kernel, grid=(D // cols,), out_shape=(jax.ShapeDtypeStr...  9.38 us
    all_to_all x1, starting transfers between devices, local(): lax.all_to_all(each.reshape(count, PART, WIDE), 'seq', 0, 0)  7.06 us
    all_to_all x1, starting transfers between devices, local(): rows_b = lax.all_to_all(tiled_b, 'seq', 0, 0)  3.65 us
    ppermute x4, starting transfers between devices, scatter(): lax.ppermute(bundle, 'seq', [(source, members[0])])  2.77 us
  transfers between devices with their start and end apart: 9, of which 2 were waited for; matrix products, arithmetic and copies ran while one was open for 0% of the time, Pallas kernels for 39%

profile of v8, /device:TPU:0, one launch (start us, length us, event | category | flops | bytes accessed | tf_op | source)
XLA Modules:
  0.0 128.5 jit_solution(8993081413491210182)
XLA Ops:
  0.0 0.0 copy-start
  0.0 1.6 %copy-done = bf16[1024,1024]{1,0:T(8,128)(2,1)S(1)} copy-done((bf16[1024,1024]{1,0:T(8,128)(2,1)S(1)}, bf16[1024,1024]{1,0:T(8,128)(2,1)}, u32[]{:S(2)}) %copy-start) | copy-done | bytes 2097176
  1.6 0.1 pack.1
  1.7 0.7 collective-permute-start
  2.4 0.7 collective-permute-start.2
  3.1 0.7 collective-permute-start.3
  3.8 0.7 collective-permute-start.1
  4.5 0.0 copy-start.1
  4.5 0.0 copy-start.3
  4.6 9.4 %project_kv.1 = (bf16[1024,1024]{1,0:T(8,128)(2,1)}, bf16[1024,1024]{1,0:T(8,128)(2,1)}) custom-call(bf16[1024,1024]{1,0:T(8,128)(2,1)} %tokens.3, f32[1,1024]{1,0:T(1,128)} %bitcast.7, bf16[1024,1024]{1,0:T(8,128)(2,1)} %w_key.1, bf16[1024,1024]{1,0:T(8,128)(2,1)} %w_value.1), custom_call_target="tpu_custom_call" | custom-call | flops 4294967296 | bytes 10485760 | tf_op jit(solution)/shard_map/project_kv/pallas_call | solution.py:47
  13.9 0.0 collective-permute-done.1.refs_1_
  13.9 0.0 collective-permute-done.refs_0_
  14.0 0.0 collective-permute-done.2.refs_2_
  14.0 0.0 collective-permute-done.3.refs_3_
  14.0 0.2 relay.1
  14.2 1.3 %collective-permute-start.4 = (bf16[64,1024]{1,0:T(8,128)(2,1)S(1)}, bf16[64,1024]{1,0:T(8,128)(2,1)S(1)}, u32[]{:S(2)}, u32[]{:S(2)}) collective-permute-start(bf16[64,1024]{1,0:T(8,128)(2,1)S(1)} %get-tuple-element.37), channel_id=1, source_target_pairs={{12,0},{14,2},{3,1},{11,9},{28,16},{30,18},{19,17},{27,25},{44,32}... | collective-permute-start | bytes 393224 | tf_op jit(solution)/shard_map/ppermute | solution.py:282
  15.5 0.7 collective-permute-start.5
  16.2 0.7 collective-permute-start.6
  16.9 9.4 %collective-permute-done.4.refs_2_ = bf16[64,1024]{1,0:T(8,128)(2,1)S(1)} collective-permute-done((bf16[64,1024]{1,0:T(8,128)(2,1)S(1)}, bf16[64,1024]{1,0:T(8,128)(2,1)S(1)}, u32[]{:S(2)}, u32[]{:S(2)}) %collective-permute-start.4) | collective-permute-done | bytes 131104 | tf_op jit(solution)/shard_map/ppermute | solution.py:282
  26.3 0.0 collective-permute-done.5.refs_3_
  26.3 0.0 collective-permute-done.6.refs_4_
  26.3 0.0 copy-done.1
  26.3 0.0 copy-done.3
  26.3 1.7 %project_queries.1 = (bf16[64,1024]{1,0:T(8,128)(2,1)S(1)}, bf16[16,32,1024]{2,1,0:T(8,128)(2,1)S(1)}, bf16[16,32,1024]{2,1,0:T(8,128)(2,1)}) custom-call(f32[1,1024]{1,0:T(1,128)S(1)} %bitcast.8, bf16[1024,1024]{1,0:T(8,128)(2,1)S(1)} %copy-done.1, bf16[64,1024]{1,0:T(8,128)(2,1)S(1)} %get-tuple-element.26.refs_0_, ...), custom_call_target="tpu_custom_call" | custom-call | flops 134217728 | bytes 4194304 | tf_op jit(solution)/shard_map/project_queries/pallas_call | solution.py:88
  28.0 25.2 %all_to_all.20 = bf16[16,32,1024]{2,1,0:T(8,128)(2,1)} all-to-all(bf16[16,32,1024]{2,1,0:T(8,128)(2,1)S(1)} %get-tuple-element.40), channel_id=1, replica_groups=mesh['ctx'=8,'seq'=16] {'seq'}, dimensions={0} | all-to-all | bytes 2097152 | tf_op jit(solution)/shard_map/all_to_all | solution.py:295
  53.2 3.7 %all-to-all-start.2 = ((bf16[16,32,1024]{2,1,0:T(8,128)(2,1)}), bf16[16,32,1024]{2,1,0:T(8,128)(2,1)S(1)}, u32[]{:S(2)}, u32[]{:S(2)}) async-start(bf16[16,32,1024]{2,1,0:T(8,128)(2,1)} %get-tuple-element.44), calls=%async_computation.2 | async-start | bytes 2097152 | tf_op jit(solution)/shard_map/all_to_all | solution.py:297
  56.8 14.4 %attend_0.1 = bf16[512,1152]{1,0:T(8,128)(2,1)} custom-call(s32[1]{0:T(128)} %bitcast.flag, bf16[512,1024]{1,0:T(8,128)(2,1)} %bitcast.13, bf16[1024,1024]{1,0:T(8,128)(2,1)} %get-tuple-element.31.refs_0_.refs_1_.refs_2_.refs_3_, bf16[1024,1024]{1,0:T(8,128)(2,1)} %get-tuple-element.31.refs_0_.refs_1_.refs_2_.refs_3_, ...), custom_call_target="tpu_custom_call" | custom-call | flops 8589934592 | bytes 8388608 | tf_op jit(solution)/shard_map/attend_0/pallas_call | solution.py:176
  71.2 0.1 all-to-all-done.2
  71.3 0.0 copy-start.5
  71.3 7.1 %all-to-all-start.1 = ((bf16[16,32,1152]{2,1,0:T(8,128)(2,1)}), bf16[16,32,1152]{2,1,0:T(8,128)(2,1)S(1)}, u32[]{:S(2)}, u32[]{:S(2)}) async-start(bf16[16,32,1152]{2,1,0:T(8,128)(2,1)} %bitcast.10), calls=%async_computation.1 | async-start | bytes 2359296 | tf_op jit(solution)/shard_map/all_to_all | solution.py:301
  78.4 0.0 copy-done.5
  78.4 25.9 %attend_1.1 = bf16[512,1152]{1,0:T(8,128)(2,1)} custom-call(s32[1]{0:T(128)} %bitcast.flag, bf16[512,1024]{1,0:T(8,128)(2,1)} %bitcast.12, bf16[1024,1024]{1,0:T(8,128)(2,1)} %get-tuple-element.31.refs_0_.refs_1_.refs_2_.refs_3_, bf16[1024,1024]{1,0:T(8,128)(2,1)} %get-tuple-element.31.refs_0_.refs_1_.refs_2_.refs_3_, ...), custom_call_target="tpu_custom_call" | custom-call | flops 8589934592 | bytes 8388608 | tf_op jit(solution)/shard_map/attend_1/pallas_call | solution.py:176
  104.3 0.0 copy-start.2
  104.3 0.0 copy-start.4
  104.3 0.0 all-to-all-done.1.refs_0_
  104.3 22.0 %all_to_all.21.refs_1_ = bf16[16,32,1152]{2,1,0:T(8,128)(2,1)S(1)} all-to-all(bf16[16,32,1152]{2,1,0:T(8,128)(2,1)} %bitcast.11), channel_id=1, replica_groups=mesh['ctx'=8,'seq'=16] {'seq'}, dimensions={0} | all-to-all | bytes 2359296 | tf_op jit(solution)/shard_map/all_to_all | solution.py:301
  126.3 0.0 copy-done.2
  126.3 0.0 copy-done.4
  126.3 2.1 %finish.1 = bf16[64,1024]{1,0:T(8,128)(2,1)} custom-call(bf16[16,32,1152]{2,1,0:T(8,128)(2,1)S(1)} %all-to-all-done.1.refs_0_, bf16[16,32,1152]{2,1,0:T(8,128)(2,1)S(1)} %all_to_all.21.refs_1_, bf16[64,1024]{1,0:T(8,128)(2,1)S(1)} %get-tuple-element.46.refs_2_, f32[1,1024]{1,0:T(1,128)S(1)} %bitcast.9, bf16[1024,1024]{1,0:T(8,128)(2,1)S(1)} %copy-done.2), custom_call_target="tpu_custom_call" | custom-call | flops 268435456 | bytes 8388608 | tf_op jit(solution)/shard_map/finish/pallas_call | solution.py:226
Async XLA Ops:
  0.0 1.6 %copy-start = (bf16[1024,1024]{1,0:T(8,128)(2,1)S(1)}, bf16[1024,1024]{1,0:T(8,128)(2,1)}, u32[]{:S(2)}) copy-start(bf16[1024,1024]{1,0:T(8,128)(2,1)} %tokens.3) | copy-start | bytes 6291460
  1.7 12.2 %collective-permute-start = (bf16[256,1024]{1,0:T(8,128)(2,1)S(1)}, bf16[256,1024]{1,0:T(8,128)(2,1)S(1)}, u32[]{:S(2)}, u32[]{:S(2)}) collective-permute-start(bf16[256,1024]{1,0:T(8,128)(2,1)S(1)} %get-tuple-element.27), channel_id=1, source_target_pairs={{15,12},{31,28},{47,44},{63,60},{79,76},{95,92},{111,108},{127,124}} | collective-permute-start | bytes 1572872 | tf_op jit(solution)/shard_map/ppermute | solution.py:269
  2.4 11.5 %collective-permute-start.2 = (bf16[256,1024]{1,0:T(8,128)(2,1)S(1)}, bf16[256,1024]{1,0:T(8,128)(2,1)S(1)}, u32[]{:S(2)}, u32[]{:S(2)}) collective-permute-start(bf16[256,1024]{1,0:T(8,128)(2,1)S(1)} %get-tuple-element.29), channel_id=1, source_target_pairs={{15,3},{31,19},{47,35},{63,51},{79,67},{95,83},{111,99},{127,115}} | collective-permute-start | bytes 1572872 | tf_op jit(solution)/shard_map/ppermute | solution.py:269
  3.1 10.8 %collective-permute-start.3 = (bf16[256,1024]{1,0:T(8,128)(2,1)S(1)}, bf16[256,1024]{1,0:T(8,128)(2,1)S(1)}, u32[]{:S(2)}, u32[]{:S(2)}) collective-permute-start(bf16[256,1024]{1,0:T(8,128)(2,1)S(1)} %get-tuple-element.30), channel_id=1, source_target_pairs={{15,11},{31,27},{47,43},{63,59},{79,75},{95,91},{111,107},{127,123}} | collective-permute-start | bytes 1572872 | tf_op jit(solution)/shard_map/ppermute | solution.py:269
  3.8 10.1 %collective-permute-start.1 = (bf16[192,1024]{1,0:T(8,128)(2,1)S(1)}, bf16[192,1024]{1,0:T(8,128)(2,1)S(1)}, u32[]{:S(2)}, u32[]{:S(2)}) collective-permute-start(bf16[192,1024]{1,0:T(8,128)(2,1)S(1)} %get-tuple-element.28), channel_id=1, source_target_pairs={{15,14},{31,30},{47,46},{63,62},{79,78},{95,94},{111,110},{127,126}} | collective-permute-start | bytes 1179656 | tf_op jit(solution)/shard_map/ppermute | solution.py:269
  4.5 21.8 %copy-start.1 = (bf16[1024,1024]{1,0:T(8,128)(2,1)S(1)}, bf16[1024,1024]{1,0:T(8,128)(2,1)}, u32[]{:S(2)}) copy-start(bf16[1024,1024]{1,0:T(8,128)(2,1)} %w_query.1) | copy-start | bytes 6291460
  4.5 21.8 %copy-start.3 = (f32[1024]{0:T(1024)S(1)}, f32[1024]{0:T(1024)}, u32[]{:S(2)}) copy-start(f32[1024]{0:T(1024)} %param.8) | copy-start | bytes 12292
  14.2 12.1 %collective-permute-start.4 = (bf16[64,1024]{1,0:T(8,128)(2,1)S(1)}, bf16[64,1024]{1,0:T(8,128)(2,1)S(1)}, u32[]{:S(2)}, u32[]{:S(2)}) collective-permute-start(bf16[64,1024]{1,0:T(8,128)(2,1)S(1)} %get-tuple-element.37), channel_id=1, source_target_pairs={{12,0},{14,2},{3,1},{11,9},{28,16},{30,18},{19,17},{27,25},{44,32}... | collective-permute-start | bytes 393224 | tf_op jit(solution)/shard_map/ppermute | solution.py:282
  15.5 10.8 %collective-permute-start.5 = (bf16[64,1024]{1,0:T(8,128)(2,1)S(1)}, bf16[64,1024]{1,0:T(8,128)(2,1)S(1)}, u32[]{:S(2)}, u32[]{:S(2)}) collective-permute-start(bf16[64,1024]{1,0:T(8,128)(2,1)S(1)} %get-tuple-element.38), channel_id=1, source_target_pairs={{12,8},{14,10},{3,5},{11,4},{28,24},{30,26},{19,21},{27,20},{44,40... | collective-permute-start | bytes 393224 | tf_op jit(solution)/shard_map/ppermute | solution.py:282
  16.2 10.1 %collective-permute-start.6 = (bf16[64,1024]{1,0:T(8,128)(2,1)S(1)}, bf16[64,1024]{1,0:T(8,128)(2,1)S(1)}, u32[]{:S(2)}, u32[]{:S(2)}) collective-permute-start(bf16[64,1024]{1,0:T(8,128)(2,1)S(1)} %get-tuple-element.39), channel_id=1, source_target_pairs={{12,13},{3,7},{11,6},{28,29},{19,23},{27,22},{44,45},{35,39},{43,3... | collective-permute-start | bytes 393224 | tf_op jit(solution)/shard_map/ppermute | solution.py:282
  53.2 18.1 %all-to-all-start.2 = ((bf16[16,32,1024]{2,1,0:T(8,128)(2,1)}), bf16[16,32,1024]{2,1,0:T(8,128)(2,1)S(1)}, u32[]{:S(2)}, u32[]{:S(2)}) async-start(bf16[16,32,1024]{2,1,0:T(8,128)(2,1)} %get-tuple-element.44), calls=%async_computation.2 | async-start | bytes 2097152 | tf_op jit(solution)/shard_map/all_to_all | solution.py:297
  71.3 7.1 %copy-start.5 = (bf16[16,32,1024]{2,1,0:T(8,128)(2,1)}, bf16[16,32,1024]{2,1,0:T(8,128)(2,1)S(1)}, u32[]{:S(2)}) copy-start(bf16[16,32,1024]{2,1,0:T(8,128)(2,1)S(1)} %all-to-all-done.2) | copy-start | bytes 3145732
  71.3 33.0 %all-to-all-start.1 = ((bf16[16,32,1152]{2,1,0:T(8,128)(2,1)}), bf16[16,32,1152]{2,1,0:T(8,128)(2,1)S(1)}, u32[]{:S(2)}, u32[]{:S(2)}) async-start(bf16[16,32,1152]{2,1,0:T(8,128)(2,1)} %bitcast.10), calls=%async_computation.1 | async-start | bytes 2359296 | tf_op jit(solution)/shard_map/all_to_all | solution.py:301
  104.3 22.0 %copy-start.2 = (bf16[1024,1024]{1,0:T(8,128)(2,1)S(1)}, bf16[1024,1024]{1,0:T(8,128)(2,1)}, u32[]{:S(2)}) copy-start(bf16[1024,1024]{1,0:T(8,128)(2,1)} %refs_4_.1) | copy-start | bytes 6291460
  104.3 22.0 %copy-start.4 = (f32[1024]{0:T(1024)S(1)}, f32[1024]{0:T(1024)}, u32[]{:S(2)}) copy-start(f32[1024]{0:T(1024)} %param.9) | copy-start | bytes 12292
